TPU v7x, 32 devices: a whole 2x2x4 slice. The times are simulated.
32 devices in a mesh: src: 4 (over z), gx: 2 (over y), gy: 4 (over x, core).
Axes of the slice: x: 2, y: 2, z: 4, core: 2. Of those that a mesh axis runs over, the one named last changes fastest.
Arguments:
- adjoint_now: float32 [4, 2, 8, 128, 512], P('src', None, 'gx', 'gy'), may hold values from -6 to 6
- adjoint_before: float32 [4, 2, 8, 128, 512], P('src', None, 'gx', 'gy'), may hold values from -6 to 6
- forward_field: bfloat16 [3, 4, 2, 8, 128, 512], P(None, 'src', None, 'gx', 'gy'), may hold values from -6 to 6
- velocity: float32 [8, 128, 512], P('gx', 'gy'), may hold values from 0.2 to 0.4
- thomsen_eps: float32 [8, 128, 512], P('gx', 'gy'), may hold values from 0.05 to 0.35
- thomsen_delta: float32 [8, 128, 512], P('gx', 'gy'), may hold values from 0 to 0.25
- tilt_level: int32 [8, 128, 512], P('gx', 'gy'), may hold values from 0 to 31
- azimuth_level: int32 [8, 128, 512], P('gx', 'gy'), may hold values from 0 to 31
- channel_cell: int32 [4, 1536], P('src'), may hold values from 0 to 1023
- channel_count: int32 [4], P('src'), may hold values from 512 to 1536, as said below
- residual_trace: float32 [4, 3, 1536], P('src'), may hold values from -6 to 6
Outputs:
- adjoint_next: float32 [4, 2, 8, 128, 512], P('src', None, 'gx', 'gy')
- grad_velocity: float32 [8, 128, 512], P('gx', 'gy', 'src')
- grad_epsilon: float32 [8, 128, 512], P('gx', 'gy', 'src')
- grad_delta: float32 [8, 128, 512], P('gx', 'gy', 'src')
Inputs may be any that keep to these rules, and one draw needn't show every extreme that they name: `channel_count`: some virtual source has 1536 live channels and some other has 512.
All inputs are finite; a program needn't handle non-finite values.
Results may differ from a plain program's by a relative error of at most 0.0003.
Values sent between devices are 32-bit elements; how exact they have to be, the bound alone decides.
No kernel may reach another device: no remote copies, remote signals or barrier semaphores. Data moves between devices by JAX's collectives and lax.ppermute only.
A program may use at most 64 MiB of HBM per device.

v0:
```python
import math

import jax
import jax.numpy as jnp
from jax import lax
from jax.sharding import PartitionSpec as P

LEVELS = 32


def extended_2(block, sides, width):
    for axis, dim in sides:
        count = lax.axis_size(axis)
        forward = [(i, i + 1) for i in range(count - 1)]
        backward = [(target, source) for source, target in forward]
        low = lax.ppermute(
            lax.slice_in_dim(block, block.shape[dim] - width, None, axis=dim), axis, forward
        )
        high = lax.ppermute(lax.slice_in_dim(block, 0, width, axis=dim), axis, backward)
        block = jnp.concatenate([low, block, high], axis=dim)
    return block


def derivatives(padded):
    center = padded[..., 1:-1, 1:-1, 1:-1]
    second_x = padded[..., 2:, 1:-1, 1:-1] + padded[..., :-2, 1:-1, 1:-1] - 2.0 * center
    second_y = padded[..., 1:-1, 2:, 1:-1] + padded[..., 1:-1, :-2, 1:-1] - 2.0 * center
    second_z = padded[..., 1:-1, 1:-1, 2:] + padded[..., 1:-1, 1:-1, :-2] - 2.0 * center
    mixed_xy = 0.25 * (
        padded[..., 2:, 2:, 1:-1]
        - padded[..., 2:, :-2, 1:-1]
        - padded[..., :-2, 2:, 1:-1]
        + padded[..., :-2, :-2, 1:-1]
    )
    mixed_yz = 0.25 * (
        padded[..., 1:-1, 2:, 2:]
        - padded[..., 1:-1, 2:, :-2]
        - padded[..., 1:-1, :-2, 2:]
        + padded[..., 1:-1, :-2, :-2]
    )
    mixed_xz = 0.25 * (
        padded[..., 2:, 1:-1, 2:]
        - padded[..., 2:, 1:-1, :-2]
        - padded[..., :-2, 1:-1, 2:]
        + padded[..., :-2, 1:-1, :-2]
    )
    return (second_x, second_y, second_z, mixed_xy, mixed_yz, mixed_xz)


def tilt_weights(tilt_level, azimuth_level):
    theta = tilt_level.astype(jnp.float32) * (0.5 * math.pi / LEVELS)
    azimuth = azimuth_level.astype(jnp.float32) * (2.0 * math.pi / LEVELS)
    sin_t = jnp.sin(theta)
    cos_t = jnp.cos(theta)
    sin_p = jnp.sin(azimuth)
    cos_p = jnp.cos(azimuth)
    return (
        sin_t * sin_t * cos_p * cos_p,
        sin_t * sin_t * sin_p * sin_p,
        cos_t * cos_t,
        2.0 * sin_t * sin_t * sin_p * cos_p,
        2.0 * sin_t * cos_t * sin_p,
        2.0 * sin_t * cos_t * cos_p,
    )


def split_operators(padded, weights):
    parts = derivatives(padded)
    axial = weights[0] * parts[0]
    for index in range(1, 6):
        axial = axial + weights[index] * parts[index]
    laplace = parts[0] + parts[1] + parts[2]
    return (laplace[..., 0, :, :, :] - axial[..., 0, :, :, :], axial[..., 1, :, :, :])


def exchange_rims(current):
    return extended_2(current, (("gx", 2), ("gy", 3)), 1)


def on_device(
    adjoint_now,
    adjoint_before,
    forward_field,
    velocity,
    thomsen_eps,
    thomsen_delta,
    tilt_level,
    azimuth_level,
    channel_cell,
    channel_count,
    residual_trace,
):
    tile_x, tile_y, depth = velocity.shape
    sources_here = adjoint_now.shape[0]
    step_count = forward_field.shape[0]
    width_y = tile_y * lax.axis_size("gy")
    start_x = lax.axis_index("gx") * tile_x
    start_y = lax.axis_index("gy") * tile_y
    local_x = channel_cell // width_y - start_x
    local_y = channel_cell % width_y - start_y
    slots = lax.broadcasted_iota(jnp.int32, channel_cell.shape, 1)
    inside = (
        (local_x >= 0)
        & (local_x < tile_x)
        & (local_y >= 0)
        & (local_y < tile_y)
        & (slots < channel_count[:, None])
    )
    target = jnp.where(inside, local_x * tile_y + local_y, -1)
    cells = jnp.arange(tile_x * tile_y, dtype=jnp.int32)
    onehot = (target[:, :, None] == cells[None, None, :]).astype(jnp.float32)
    surface = jnp.einsum("stc,scm->stm", residual_trace, onehot, precision=lax.Precision.HIGHEST)
    surface = surface.reshape(sources_here, step_count, tile_x, tile_y)
    weights = tilt_weights(tilt_level, azimuth_level)
    speed_sq = velocity * velocity
    stretch = 1.0 + 2.0 * thomsen_eps
    root = jnp.sqrt(1.0 + 2.0 * thomsen_delta)
    share_velocity = None
    total_velocity = jnp.zeros_like(velocity)
    total_epsilon = jnp.zeros_like(velocity)
    total_delta = jnp.zeros_like(velocity)
    current = adjoint_now
    previous = adjoint_before
    for time_step in range(step_count):
        extended = exchange_rims(current)
        padded = jnp.pad(extended, ((0, 0), (0, 0), (0, 0), (0, 0), (1, 1)))
        horiz_p, axial_q = split_operators(padded, weights)
        update_p = stretch * horiz_p + root * axial_q
        update_q = root * horiz_p + axial_q
        following = 2.0 * current - previous + speed_sq * jnp.stack([update_p, update_q], axis=1)
        following = following.at[:, 0, :, :, 0].add(surface[:, time_step])
        forward_p = forward_field[time_step, :, 0].astype(jnp.float32)
        forward_q = forward_field[time_step, :, 1].astype(jnp.float32)
        term_velocity = jnp.sum(
            2.0 * velocity * (forward_p * update_p + forward_q * update_q), axis=0
        )
        term_epsilon = jnp.sum(2.0 * speed_sq * forward_p * horiz_p, axis=0)
        term_delta = jnp.sum(speed_sq / root * (forward_p * axial_q + forward_q * horiz_p), axis=0)
        total_velocity = total_velocity + term_velocity
        total_epsilon = total_epsilon + term_epsilon
        total_delta = total_delta + term_delta
        previous = current
        current = following
    share_velocity, share_epsilon, share_delta = (
        lax.psum_scatter(total_velocity, "src", scatter_dimension=2, tiled=True),
        lax.psum_scatter(total_epsilon, "src", scatter_dimension=2, tiled=True),
        lax.psum_scatter(total_delta, "src", scatter_dimension=2, tiled=True),
    )
    return (current, share_velocity, share_epsilon, share_delta)


def solution(mesh):
    placed = (
        P("src", None, "gx", "gy", None),
        P("src", None, "gx", "gy", None),
        P(None, "src", None, "gx", "gy", None),
        P("gx", "gy", None),
        P("gx", "gy", None),
        P("gx", "gy", None),
        P("gx", "gy", None),
        P("gx", "gy", None),
        P("src", None),
        P("src"),
        P("src", None, None),
    )
    return jax.shard_map(
        on_device,
        mesh=mesh,
        in_specs=placed,
        out_specs=(
            P("src", None, "gx", "gy", None),
            P("gx", "gy", "src"),
            P("gx", "gy", "src"),
            P("gx", "gy", "src"),
        ),
        check_vma=False,
    )
```

profile of v0, /device:TPU:0, one launch (start us, length us, event | category | flops | bytes accessed | tf_op | source)
XLA Modules:
  0.0 217.6 jit_solution(5912625835324830934)
XLA Ops:
  7.2 1.0 fusion.95
  8.2 4.9 %collective-permute-start.1 = (f32[1,2,1,32,512]{4,3,2,1,0:T(8,128)S(1)}, f32[1,2,1,32,512]{4,3,2,1,0:T(8,128)S(1)}, u32[]{:S(2)}, u32[]{:S(2)}) collective-permute-start(f32[1,2,1,32,512]{4,3,2,1,0:T(8,128)S(1)} %get-tuple-element.104), channel_id=1, source_target_pairs={{0,4},{1,5},{2,6},{3,7},{8,12},{9,13},{10,14},{11,15},{16,20},{17,... | collective-permute-start | bytes 393224 | tf_op jit(solution)/shard_map/ppermute | solution.py:16
  13.1 1.3 collective-permute-start
  15.1 3.4 %multiply_multiply_fusion.1 = (f32[4,32,512]{2,1,0:T(8,128)S(1)}, f32[4,32,512]{2,1,0:T(8,128)S(1)}, f32[4,32,512]{2,1,0:T(8,128)S(1)}, f32[4,32,512]{2,1,0:T(8,...) fusion(s32[4,32,512]{2,1,0:T(8,128)} %param.24, s32[4,32,512]{2,1,0:T(8,128)} %param.23), kind=kLoop, calls=%fused_computation.120 | loop fusion | flops 1310720 | bytes 2097152 | tf_op jit(solution)/shard_map/mul | solution.py:58
  19.3 0.7 collective-permute-done
  20.1 0.7 copy.264
  20.8 1.3 collective-permute-start.2
  22.1 0.6 copy.265
  22.7 3.6 %collective-permute-start.3 = (f32[1,2,6,1,512]{4,1,3,2,0:T(2,128)}, f32[1,2,6,1,512]{4,1,3,2,0:T(2,128)}, u32[]{:S(2)}, u32[]{:S(2)}) collective-permute-start(f32[1,2,6,1,512]{4,1,3,2,0:T(2,128)} %copy.265), channel_id=1, source_target_pairs={{0,1},{1,2},{2,3},{4,5},{5,6},{6,7},{8,9},{9,10},{10,11},{12,13},{... | collective-permute-start | bytes 73736 | tf_op jit(solution)/shard_map/ppermute | solution.py:16
  26.3 0.6 slice_bitcast_fusion.3
  27.0 1.4 copy.242
  28.4 0.8 copy.237
  29.2 0.8 copy.239
  30.0 0.6 select_maximum_fusion.8
  30.6 3.8 %fusion.10 = (f32[1,2,4,32,512]{4,3,2,1,0:T(8,128)S(1)}, f32[1,2,4,32,512]{4,3,2,1,0:T(8,128)S(1)}, f32[1,2,4,32,512]{4,3,2,1,0:T(8,128)S(1)}, f32[1,2,4,32,512]{4,3,2,1,0:T(8,128)S(1)}) fusion(f32[1,2,6,32,512]{4,3,2,1,0:T(8,128)} %copy-done.23, f32[1,2,6,1,512]{4,3,2,1,0:T(1,128)S(1)} %copy.239, f32[1,2,6,1,512]{4,3,2,1,0:T(1,128)S(1)} %copy.237, ...), kind=kLoop, calls=%fused_computation.35 | loop fusion | flops 4587520 | bytes 10534912 | tf_op jit(solution)/shard_map/add | solution.py:71
  34.8 0.7 copy-done.36
  35.9 1.3 collective-permute-start.4
  37.2 4.6 %collective-permute-start.5 = (f32[1,2,1,32,512]{4,3,2,1,0:T(8,128)S(1)}, f32[1,2,1,32,512]{4,3,2,1,0:T(8,128)S(1)}, u32[]{:S(2)}, u32[]{:S(2)}) collective-permute-start(f32[1,2,1,32,512]{4,3,2,1,0:T(8,128)S(1)} %get-tuple-element.96), channel_id=1, source_target_pairs={{0,4},{1,5},{2,6},{3,7},{8,12},{9,13},{10,14},{11,15},{16,20},{17,... | collective-permute-start | bytes 393224 | tf_op jit(solution)/shard_map/ppermute | solution.py:16
  41.7 2.0 collective-permute-done.4
  43.7 1.2 collective-permute-done.5
  44.9 1.3 collective-permute-start.6
  46.2 3.0 %collective-permute-start.7 = (f32[1,2,6,1,512]{4,1,3,2,0:T(2,128)S(1)}, f32[1,2,6,1,512]{4,1,3,2,0:T(2,128)S(1)}, u32[]{:S(2)}, u32[]{:S(2)}) collective-permute-start(f32[1,2,6,1,512]{4,1,3,2,0:T(2,128)S(1)} %copy.245), channel_id=1, source_target_pairs={{0,1},{1,2},{2,3},{4,5},{5,6},{6,7},{8,9},{9,10},{10,11},{12,13},{... | collective-permute-start | bytes 73736 | tf_op jit(solution)/shard_map/ppermute | solution.py:16
  49.4 0.7 collective-permute-done.7
  50.4 0.5 select_maximum_fusion.4
  51.6 1.1 fusion.27
  53.9 1.3 collective-permute-start.8
  55.2 4.6 %collective-permute-start.9 = (f32[1,2,1,32,512]{4,3,2,1,0:T(8,128)S(1)}, f32[1,2,1,32,512]{4,3,2,1,0:T(8,128)S(1)}, u32[]{:S(2)}, u32[]{:S(2)}) collective-permute-start(f32[1,2,1,32,512]{4,3,2,1,0:T(8,128)S(1)} %get-tuple-element.94), channel_id=1, source_target_pairs={{0,4},{1,5},{2,6},{3,7},{8,12},{9,13},{10,14},{11,15},{16,20},{17,... | collective-permute-start | bytes 393224 | tf_op jit(solution)/shard_map/ppermute | solution.py:16
  59.8 2.3 %collective-permute-done.8 = f32[1,2,1,32,512]{4,3,2,1,0:T(8,128)S(1)} collective-permute-done((f32[1,2,1,32,512]{4,3,2,1,0:T(8,128)S(1)}, f32[1,2,1,32,512]{4,3,2,1,0:T(8,128)S(1)}, u32[]{:S(2)}, u32[]{:S(2)}) %collective-permute-start.8) | collective-permute-done | bytes 131104 | tf_op jit(solution)/shard_map/ppermute | solution.py:19
  62.1 1.2 collective-permute-done.9
  63.3 1.3 collective-permute-start.10
  64.7 3.2 %collective-permute-start.11 = (f32[1,2,6,1,512]{4,1,3,2,0:T(2,128)S(1)}, f32[1,2,6,1,512]{4,1,3,2,0:T(2,128)S(1)}, u32[]{:S(2)}, u32[]{:S(2)}) collective-permute-start(f32[1,2,6,1,512]{4,1,3,2,0:T(2,128)S(1)} %copy.252), channel_id=1, source_target_pairs={{0,1},{1,2},{2,3},{4,5},{5,6},{6,7},{8,9},{9,10},{10,11},{12,13},{... | collective-permute-start | bytes 73736 | tf_op jit(solution)/shard_map/ppermute | solution.py:16
  67.9 0.6 collective-permute-done.11
  68.9 0.5 select_maximum_fusion
  70.2 1.1 fusion.17
  71.5 1.1 fusion.52
  72.6 0.9 fusion.62
  73.8 1.2 fusion.48
  74.9 2.4 %copy.258 = f32[4,32,512]{1,0,2:T(4,128)} copy(f32[4,32,512]{2,1,0:T(8,128)} %fusion.62) | data formatting | bytes 524288 | tf_op jit(solution)/shard_map/add | solution.py:140
  77.3 1.3 copy.257
  78.7 1.3 copy.259
  80.2 0.5 copy-done.40
  80.7 0.6 dynamic-slice.21
  82.3 124.2 %all-reduce.9.cloned.1.call-done = (f32[4,32,512]{1,0,2:T(4,128)}, f32[4,32,512]{1,0,2:T(4,128)}, f32[4,32,512]{1,0,2:T(4,128)}) async-done(((f32[4,32,512]{1,0,2:T(4,128)}, f32[4,32,512]{1,0,2:T(4,128)}, f32[4,32,512]{1,0,2:T(4,128)}), (f32[4,32,512]{1,0,2:T(4,128)}, f32[4,32,512]{1,0,2:T(4,128)}, f32[4,32,512]{1,0,2:T(4,128)})) %all-reduce.9.cloned.1.call-update) | async-done | bytes 786448
  206.5 1.1 constant_dynamic-slice_fusion
  207.6 0.7 copy.261
  208.3 0.7 copy.262
  209.1 1.0 constant_dynamic-slice_fusion.2
  210.0 0.7 copy.260
  (124 shorter events, 6.0 us)
Async XLA Ops:
  7.2 11.4 %copy-start.38 = (s32[1,1536]{1,0:T(1,128)S(1)}, s32[1,1536]{1,0:T(1,128)}, u32[]{:S(2)}) copy-start(s32[1,1536]{1,0:T(1,128)} %param.25) | copy-start | bytes 18436
  7.2 11.5 %copy-start.39 = (f32[1,3,1536]{2,0,1:T(1,128)S(1)}, f32[1,3,1536]{2,0,1:T(1,128)}, u32[]{:S(2)}) copy-start(f32[1,3,1536]{2,0,1:T(1,128)} %param.27) | copy-start | bytes 55300
  7.2 199.3 %all-reduce.9.cloned.1.call-start = ((), (), s32[]{:S(2)}) async-start(), calls=%async_computation | async-start | bytes 6291456
  8.2 11.0 %collective-permute-start.1 = (f32[1,2,1,32,512]{4,3,2,1,0:T(8,128)S(1)}, f32[1,2,1,32,512]{4,3,2,1,0:T(8,128)S(1)}, u32[]{:S(2)}, u32[]{:S(2)}) collective-permute-start(f32[1,2,1,32,512]{4,3,2,1,0:T(8,128)S(1)} %get-tuple-element.104), channel_id=1, source_target_pairs={{0,4},{1,5},{2,6},{3,7},{8,12},{9,13},{10,14},{11,15},{16,20},{17,... | collective-permute-start | bytes 393224 | tf_op jit(solution)/shard_map/ppermute | solution.py:16
  13.1 6.9 %collective-permute-start = (f32[1,2,1,32,512]{4,3,2,1,0:T(8,128)S(1)}, f32[1,2,1,32,512]{4,3,2,1,0:T(8,128)S(1)}, u32[]{:S(2)}, u32[]{:S(2)}) collective-permute-start(f32[1,2,1,32,512]{4,3,2,1,0:T(8,128)S(1)} %get-tuple-element.103), channel_id=1, source_target_pairs={{4,0},{5,1},{6,2},{7,3},{12,8},{13,9},{14,10},{15,11},{20,16},{21,... | collective-permute-start | bytes 393224 | tf_op jit(solution)/shard_map/ppermute | solution.py:19
  15.1 4.2 %copy-start = (f32[1,2,4,32,512]{4,3,2,1,0:T(8,128)S(1)}, f32[1,2,4,32,512]{4,3,2,1,0:T(8,128)}, u32[]{:S(2)}) copy-start(f32[1,2,4,32,512]{4,3,2,1,0:T(8,128)} %param.17) | copy-start | bytes 1572868
  18.5 12.1 %copy-start.8 = (f32[4,32,512]{2,1,0:T(8,128)}, f32[4,32,512]{2,1,0:T(8,128)S(1)}, u32[]{:S(2)}) copy-start(f32[4,32,512]{2,1,0:T(8,128)S(1)} %get-tuple-element.99) | copy-start | bytes 786436
  18.5 12.1 %copy-start.11 = (f32[4,32,512]{2,1,0:T(8,128)}, f32[4,32,512]{2,1,0:T(8,128)S(1)}, u32[]{:S(2)}) copy-start(f32[4,32,512]{2,1,0:T(8,128)S(1)} %get-tuple-element.100) | copy-start | bytes 786436
  18.5 12.1 %copy-start.14 = (f32[4,32,512]{2,1,0:T(8,128)}, f32[4,32,512]{2,1,0:T(8,128)S(1)}, u32[]{:S(2)}) copy-start(f32[4,32,512]{2,1,0:T(8,128)S(1)} %get-tuple-element.101) | copy-start | bytes 786436
  18.5 12.1 %copy-start.17 = (f32[4,32,512]{2,1,0:T(8,128)}, f32[4,32,512]{2,1,0:T(8,128)S(1)}, u32[]{:S(2)}) copy-start(f32[4,32,512]{2,1,0:T(8,128)S(1)} %get-tuple-element.102) | copy-start | bytes 786436
  18.5 12.1 %copy-start.20 = (f32[4,32,512]{2,1,0:T(8,128)}, f32[4,32,512]{2,1,0:T(8,128)S(1)}, u32[]{:S(2)}) copy-start(f32[4,32,512]{2,1,0:T(8,128)S(1)} %get-tuple-element.105) | copy-start | bytes 786436
  18.5 32.5 %copy-start.6 = (f32[4,32,512]{2,1,0:T(8,128)}, f32[4,32,512]{2,1,0:T(8,128)S(1)}, u32[]{:S(2)}) copy-start(f32[4,32,512]{2,1,0:T(8,128)S(1)} %get-tuple-element.98) | copy-start | bytes 786436
  18.5 8.4 %copy-start.2 = (f32[4,32,512]{2,1,0:T(8,128)S(1)}, f32[4,32,512]{2,1,0:T(8,128)}, u32[]{:S(2)}) copy-start(f32[4,32,512]{2,1,0:T(8,128)} %param.20) | copy-start | bytes 786436
  20.0 6.4 %copy-start.34 = (f32[1,2,1,32,512]{4,3,2,1,0:T(8,128)}, f32[1,2,1,32,512]{4,3,2,1,0:T(8,128)S(1)}, u32[]{:S(2)}) copy-start(f32[1,2,1,32,512]{4,3,2,1,0:T(8,128)S(1)} %collective-permute-done) | copy-start | bytes 393220
  20.0 10.5 %copy-start.23 = (f32[1,2,6,32,512]{4,3,2,1,0:T(8,128)}, f32[1,2,6,32,512]{4,3,2,1,0:T(8,128)S(1)}, u32[]{:S(2)}) copy-start(f32[1,2,6,32,512]{4,3,2,1,0:T(8,128)S(1)} %constant_dynamic-update-slice_fusion) | copy-start | bytes 2359300
  20.8 7.6 %collective-permute-start.2 = (f32[1,2,6,1,512]{4,1,3,2,0:T(2,128)}, f32[1,2,6,1,512]{4,1,3,2,0:T(2,128)}, u32[]{:S(2)}, u32[]{:S(2)}) collective-permute-start(f32[1,2,6,1,512]{4,1,3,2,0:T(2,128)} %copy.264), channel_id=1, source_target_pairs={{1,0},{2,1},{3,2},{5,4},{6,5},{7,6},{9,8},{10,9},{11,10},{13,12},{... | collective-permute-start | bytes 73736 | tf_op jit(solution)/shard_map/ppermute | solution.py:19
  22.7 6.5 %collective-permute-start.3 = (f32[1,2,6,1,512]{4,1,3,2,0:T(2,128)}, f32[1,2,6,1,512]{4,1,3,2,0:T(2,128)}, u32[]{:S(2)}, u32[]{:S(2)}) collective-permute-start(f32[1,2,6,1,512]{4,1,3,2,0:T(2,128)} %copy.265), channel_id=1, source_target_pairs={{0,1},{1,2},{2,3},{4,5},{5,6},{6,7},{8,9},{9,10},{10,11},{12,13},{... | collective-permute-start | bytes 73736 | tf_op jit(solution)/shard_map/ppermute | solution.py:16
  28.4 2.2 %copy-start.35 = (f32[1,2,1,32,512]{4,3,2,1,0:T(8,128)S(1)}, f32[1,2,1,32,512]{4,3,2,1,0:T(8,128)}, u32[]{:S(2)}) copy-start(f32[1,2,1,32,512]{4,3,2,1,0:T(8,128)} %copy-done.34) | copy-start | bytes 393220
  30.6 3.8 %copy-start.1 = (f32[4,32,512]{2,1,0:T(8,128)S(1)}, f32[4,32,512]{2,1,0:T(8,128)}, u32[]{:S(2)}) copy-start(f32[4,32,512]{2,1,0:T(8,128)} %param.22) | copy-start | bytes 786436
  30.6 3.8 %copy-start.24 = (f32[4,32,512]{2,1,0:T(8,128)S(1)}, f32[4,32,512]{2,1,0:T(8,128)}, u32[]{:S(2)}) copy-start(f32[4,32,512]{2,1,0:T(8,128)} %param.21) | copy-start | bytes 786436
  34.4 1.0 copy-start.36
  34.6 1.0 copy-start.27
  35.9 7.8 %collective-permute-start.4 = (f32[1,2,1,32,512]{4,3,2,1,0:T(8,128)S(1)}, f32[1,2,1,32,512]{4,3,2,1,0:T(8,128)S(1)}, u32[]{:S(2)}, u32[]{:S(2)}) collective-permute-start(f32[1,2,1,32,512]{4,3,2,1,0:T(8,128)S(1)} %get-tuple-element.97), channel_id=1, source_target_pairs={{4,0},{5,1},{6,2},{7,3},{12,8},{13,9},{14,10},{15,11},{20,16},{21,... | collective-permute-start | bytes 393224 | tf_op jit(solution)/shard_map/ppermute | solution.py:19
  37.2 7.7 %collective-permute-start.5 = (f32[1,2,1,32,512]{4,3,2,1,0:T(8,128)S(1)}, f32[1,2,1,32,512]{4,3,2,1,0:T(8,128)S(1)}, u32[]{:S(2)}, u32[]{:S(2)}) collective-permute-start(f32[1,2,1,32,512]{4,3,2,1,0:T(8,128)S(1)} %get-tuple-element.96), channel_id=1, source_target_pairs={{0,4},{1,5},{2,6},{3,7},{8,12},{9,13},{10,14},{11,15},{16,20},{17,... | collective-permute-start | bytes 393224 | tf_op jit(solution)/shard_map/ppermute | solution.py:16
  44.9 4.5 %collective-permute-start.6 = (f32[1,2,6,1,512]{4,1,3,2,0:T(2,128)S(1)}, f32[1,2,6,1,512]{4,1,3,2,0:T(2,128)S(1)}, u32[]{:S(2)}, u32[]{:S(2)}) collective-permute-start(f32[1,2,6,1,512]{4,1,3,2,0:T(2,128)S(1)} %copy.243), channel_id=1, source_target_pairs={{1,0},{2,1},{3,2},{5,4},{6,5},{7,6},{9,8},{10,9},{11,10},{13,12},{... | collective-permute-start | bytes 73736 | tf_op jit(solution)/shard_map/ppermute | solution.py:19
  46.2 3.9 %collective-permute-start.7 = (f32[1,2,6,1,512]{4,1,3,2,0:T(2,128)S(1)}, f32[1,2,6,1,512]{4,1,3,2,0:T(2,128)S(1)}, u32[]{:S(2)}, u32[]{:S(2)}) collective-permute-start(f32[1,2,6,1,512]{4,1,3,2,0:T(2,128)S(1)} %copy.245), channel_id=1, source_target_pairs={{0,1},{1,2},{2,3},{4,5},{5,6},{6,7},{8,9},{9,10},{10,11},{12,13},{... | collective-permute-start | bytes 73736 | tf_op jit(solution)/shard_map/ppermute | solution.py:16
  50.4 1.0 copy-start.9
  50.4 1.0 copy-start.12
  50.4 1.1 copy-start.15
  50.4 1.2 copy-start.18
  50.4 1.2 copy-start.21
  51.6 1.1 copy-start.25
  53.9 8.2 %collective-permute-start.8 = (f32[1,2,1,32,512]{4,3,2,1,0:T(8,128)S(1)}, f32[1,2,1,32,512]{4,3,2,1,0:T(8,128)S(1)}, u32[]{:S(2)}, u32[]{:S(2)}) collective-permute-start(f32[1,2,1,32,512]{4,3,2,1,0:T(8,128)S(1)} %get-tuple-element.95), channel_id=1, source_target_pairs={{4,0},{5,1},{6,2},{7,3},{12,8},{13,9},{14,10},{15,11},{20,16},{21,... | collective-permute-start | bytes 393224 | tf_op jit(solution)/shard_map/ppermute | solution.py:19
  55.2 8.1 %collective-permute-start.9 = (f32[1,2,1,32,512]{4,3,2,1,0:T(8,128)S(1)}, f32[1,2,1,32,512]{4,3,2,1,0:T(8,128)S(1)}, u32[]{:S(2)}, u32[]{:S(2)}) collective-permute-start(f32[1,2,1,32,512]{4,3,2,1,0:T(8,128)S(1)} %get-tuple-element.94), channel_id=1, source_target_pairs={{0,4},{1,5},{2,6},{3,7},{8,12},{9,13},{10,14},{11,15},{16,20},{17,... | collective-permute-start | bytes 393224 | tf_op jit(solution)/shard_map/ppermute | solution.py:16
  63.3 4.5 %collective-permute-start.10 = (f32[1,2,6,1,512]{4,1,3,2,0:T(2,128)S(1)}, f32[1,2,6,1,512]{4,1,3,2,0:T(2,128)S(1)}, u32[]{:S(2)}, u32[]{:S(2)}) collective-permute-start(f32[1,2,6,1,512]{4,1,3,2,0:T(2,128)S(1)} %copy.250), channel_id=1, source_target_pairs={{1,0},{2,1},{3,2},{5,4},{6,5},{7,6},{9,8},{10,9},{11,10},{13,12},{... | collective-permute-start | bytes 73736 | tf_op jit(solution)/shard_map/ppermute | solution.py:19
  64.7 3.9 %collective-permute-start.11 = (f32[1,2,6,1,512]{4,1,3,2,0:T(2,128)S(1)}, f32[1,2,6,1,512]{4,1,3,2,0:T(2,128)S(1)}, u32[]{:S(2)}, u32[]{:S(2)}) collective-permute-start(f32[1,2,6,1,512]{4,1,3,2,0:T(2,128)S(1)} %copy.252), channel_id=1, source_target_pairs={{0,1},{1,2},{2,3},{4,5},{5,6},{6,7},{8,9},{9,10},{10,11},{12,13},{... | collective-permute-start | bytes 73736 | tf_op jit(solution)/shard_map/ppermute | solution.py:16
  68.8 1.0 copy-start.10
  68.8 1.1 copy-start.13
  68.8 1.2 copy-start.16
  68.8 1.2 copy-start.19
  68.8 1.3 copy-start.22
  70.2 1.1 copy-start.4
  70.2 1.3 copy-start.5
  72.6 1.0 copy-start.28
  72.6 1.2 copy-start.30
  74.9 2.4 %copy-start.32 = (f32[4,32,512]{2,1,0:T(8,128)S(1)}, f32[4,32,512]{2,1,0:T(8,128)}, u32[]{:S(2)}) copy-start(f32[4,32,512]{2,1,0:T(8,128)} %get-tuple-element.65) | copy-start | bytes 786436
  74.9 3.7 %copy-start.31 = (f32[4,32,512]{2,1,0:T(8,128)S(1)}, f32[4,32,512]{2,1,0:T(8,128)}, u32[]{:S(2)}) copy-start(f32[4,32,512]{2,1,0:T(8,128)} %get-tuple-element.63) | copy-start | bytes 786436
  82.3 128.5 %copy-start.33 = (f32[1,2,4,32,512]{4,3,2,1,0:T(8,128)}, f32[1,2,4,32,512]{4,3,2,1,0:T(8,128)S(1)}, u32[]{:S(2)}) copy-start(f32[1,2,4,32,512]{4,3,2,1,0:T(8,128)S(1)} %scatter-add.14) | copy-start | bytes 1572868
  (6 other events, 5.0 us)
Sparse Core Ops, SparseCore 0:
  80.2 126.2 all-reduce.8
where the time goes:
time: 218 us
  waiting for transfers between devices  133 us (61%)
  starting transfers between devices  31.6 us (14%)
  local copies, waits for them, and re-layouts  20.6 us (9%)
  between operations  16.1 us (7%)
  other arithmetic  16 us (7%)
    unnamed x2, waiting for transfers between devices  124 us
    ppermute x6, starting transfers between devices, extended_2(): lax.ppermute(lax.slice_in_dim(block, block.shape[dim] - width, None, axis...  23.9 us
    unnamed x92, local copies, waits for them, and re-layouts  10 us
    ppermute x6, starting transfers between devices, extended_2(): lax.ppermute(lax.slice_in_dim(block, 0, width, axis=dim), axis, backward)  7.74 us
    add x3, other arithmetic, split_operators(): axial = axial + weights[index] * parts[index]  5.88 us
    ppermute x6, waiting for transfers between devices, extended_2(): lax.ppermute(lax.slice_in_dim(block, 0, width, axis=dim), axis, backward)  4.96 us
  transfers between devices with their start and end apart: 13, of which 8 were waited for; matrix products, arithmetic and copies ran while one was open for 4% of the time, Pallas kernels for 0%

commit v1 on v0

v1 whole, which is shorter than its diff:
```python
import math

import jax
import jax.numpy as jnp
from jax import lax
from jax.experimental import pallas as pl
from jax.experimental.pallas import tpu as pltpu
from jax.sharding import PartitionSpec as P

LEVELS = 32
LANES = 128
HALO = 4
VMEM_LIMIT = 16 * 1024 * 1024
F32 = jnp.float32


def run_kernel(body, ins, outs, scratch=None, smem=(), name=None, flops=0):
    scratch = scratch or {}
    names = list(ins) + list(outs) + list(scratch)

    def kernel(*refs):
        body(dict(zip(names, refs)))

    results = pl.pallas_call(
        kernel,
        name=name,
        out_shape=[jax.ShapeDtypeStruct(shape, F32) for shape in outs.values()],
        in_specs=[
            pl.BlockSpec(memory_space=pltpu.SMEM if key in smem else pltpu.VMEM) for key in ins
        ],
        out_specs=[pl.BlockSpec(memory_space=pltpu.VMEM)] * len(outs),
        scratch_shapes=[pltpu.VMEM(shape, F32) for shape in scratch.values()],
        compiler_params=pltpu.CompilerParams(vmem_limit_bytes=VMEM_LIMIT),
        cost_estimate=pl.CostEstimate(flops=flops, bytes_accessed=flops // 8, transcendentals=0),
    )(*ins.values())
    return dict(zip(outs, results))


def pair_swaps(count, first):
    pairs = []
    for low in range(first, count - 1, 2):
        pairs += [(low, low + 1), (low + 1, low)]
    return pairs


def swap(block, axis, count, first):
    return lax.ppermute(block, axis, pair_swaps(count, first))


def lanes_of(j):
    return pl.ds(j * LANES, LANES)


def is_odd(axis):
    return lax.rem(lax.axis_index(axis), 2)


class Tile:
    def __init__(self, mesh, velocity, steps):
        self.nx, self.ny, self.nz = velocity.shape
        self.steps = steps
        self.nj = self.nz // LANES
        self.rows = self.ny + 2 * HALO
        self.gx, self.gy, self.src = mesh.shape["gx"], mesh.shape["gy"], mesh.shape["src"]
        self.far = self.gx > 2

    def place(self, m):
        return m + is_odd("gx") * (self.nx - 1 - 2 * m)

    def phase(self, t, m):
        if m == self.nx or m == -1:
            return t + 2 if (m == self.nx or self.far) else 0
        if t < 0:
            return 0
        return max(self.phase(t - 1, k) for k in (m - 1, m, m + 1))


def rolled(value, by, axis):
    return pltpu.roll(value, by % value.shape[axis], axis)


def pack_edges(tile, raw):
    shape = (9, tile.nx // 2, 2 * HALO, tile.nz)

    def body(r):
        odd = is_odd("gy") == 1
        low_half = lax.broadcasted_iota(jnp.int32, (8, tile.nz), 0) < HALO

        def rows(item, m, start):
            here = tile.place(m)
            if item < 4:
                ref = r["now"] if item < 2 else r["before"]
                return ref[0, item % 2, here, pl.ds(start, 8), :]
            ref = r[("velocity", "eps", "delta", "tilt", "azimuth")[item - 4]]
            return ref[here, pl.ds(start, 8), :].astype(F32)

        for item in range(9):
            for pair in range(tile.nx // 2):
                a, b = 2 * pair, 2 * pair + 1
                top = jnp.where(
                    low_half,
                    rolled(rows(item, a, tile.ny - 8), HALO, 0),
                    rows(item, b, tile.ny - 8),
                )
                bottom = jnp.where(low_half, rows(item, a, 0), rolled(rows(item, b, 0), HALO, 0))
                r["even"][item, pair] = jnp.where(odd, bottom, top)
                r["odd"][item, pair] = jnp.where(odd, top, bottom)

    out = run_kernel(body, raw, {"even": shape, "odd": shape}, name="pack_edges", flops=10**6)
    return out["even"], out["odd"]


def halo_rows(tile, r, item, m):
    odd = is_odd("gy") == 1
    low_half = lax.broadcasted_iota(jnp.int32, (8, tile.nz), 0) < HALO
    even_got, odd_got = r["got_even"][item, m // 2], r["got_odd"][item, m // 2]
    upper = jnp.where(odd, odd_got, even_got)
    lower = jnp.where(odd, even_got, odd_got)
    if m % 2 == 0:
        return jnp.where(low_half, upper, rolled(lower, HALO, 0))
    return jnp.where(low_half, rolled(upper, HALO, 0), lower)


def edge_planes(tile, now, got_even, got_odd):
    outs = {"near": (2, tile.rows, tile.nz)}
    if tile.far:
        outs["far"] = (2, tile.rows, tile.nz)

    def body(r):
        for key in outs:
            m = tile.nx - 1 if key == "near" else 0
            for c in range(2):
                r[key][c, : tile.ny] = r["now"][0, c, tile.place(m)]
                r[key][c, tile.ny :] = halo_rows(tile, r, c, m)

    ins = {"now": now, "got_even": got_even, "got_odd": got_odd}
    return run_kernel(body, ins, outs, name="edge_planes", flops=10**5)


def angle_tables(rows):
    level = lax.broadcasted_iota(jnp.int32, (rows, LANES), 1).astype(F32)
    theta = level * (0.5 * math.pi / LEVELS)
    azimuth = level * (2.0 * math.pi / LEVELS)
    sin_t, cos_t, sin_p, cos_p = jnp.sin(theta), jnp.cos(theta), jnp.sin(azimuth), jnp.cos(azimuth)
    return (
        sin_t * sin_t,
        0.5 * sin_t * cos_t,
        cos_t * cos_t,
        cos_p * cos_p,
        sin_p * sin_p,
        0.5 * sin_p * cos_p,
        sin_p,
        cos_p,
    )


def store_weights(out, m, rows, j, tables, sign, velocity, eps, delta, tilt, azimuth):
    def look(table, level):
        return jnp.take_along_axis(table, level, axis=1)

    sin2_t, sincos_t, cos2_t = (look(tables[k], tilt) for k in range(3))
    cos2_p, sin2_p, sincos_p, sin_p, cos_p = (look(tables[k], azimuth) for k in range(3, 8))
    speed_sq = velocity * velocity
    root = jnp.sqrt(1.0 + 2.0 * delta)
    values = (
        sin2_t * cos2_p,
        sin2_t * sin2_p,
        cos2_t,
        sign * (sin2_t * sincos_p),
        sincos_t * sin_p,
        sign * (sincos_t * cos_p),
        speed_sq * (1.0 + 2.0 * eps),
        speed_sq * root,
        speed_sq,
    )
    for k, value in enumerate(values):
        out[k, m, rows, lanes_of(j)] = value


def x_sign():
    return 1.0 - 2.0 * is_odd("gx").astype(F32)


def own_weights(tile, raw):
    coefs = ("velocity", "eps", "delta", "tilt", "azimuth")

    def body(r):
        tables = angle_tables(8)
        sign = x_sign()

        def plane(m, _):
            here = tile.place(m)
            for j in range(tile.nj):
                for start in range(0, tile.ny, 8):
                    rows = pl.ds(start, 8)
                    store_weights(
                        r["w"], m, rows, j, tables, sign,
                        *(r[key][here, rows, lanes_of(j)] for key in coefs),
                    )
            return 0

        lax.fori_loop(0, tile.nx, plane, 0)

    ins = {key: raw[key] for key in coefs}
    out = run_kernel(
        body, ins, {"w": (9, tile.nx, tile.ny, tile.nz)}, name="own_weights", flops=3 * 10**6
    )
    return out["w"]


def surface_load(tile, cell, count, trace):
    channels = cell.shape[1]
    width = tile.ny * tile.gy

    def body(r):
        start_x = lax.axis_index("gx") * tile.nx
        start_y = lax.axis_index("gy") * tile.ny
        cell_here = r["cell"][...]
        slots = lax.broadcasted_iota(jnp.int32, (1, channels), 1)
        live = slots < r["count"][0]
        if width & (width - 1) == 0:
            row_of = cell_here & (width - 1)
        else:
            row_of = lax.rem(cell_here, jnp.full_like(cell_here, width))
        place = lax.broadcasted_iota(jnp.int32, (tile.rows, 1), 0)
        place = jnp.where(place >= tile.ny + HALO, place - tile.rows, place) + start_y
        onehot = jnp.where(row_of == place, 1.0, 0.0)
        first = lax.broadcasted_iota(jnp.int32, (tile.rows, LANES), 1) == 0
        pad = jnp.zeros((LANES - tile.steps, channels), F32)
        trace_here = r["trace"][0]
        for m in range(tile.nx):
            low = (start_x + tile.place(m)) * width
            inside = live & (cell_here >= low) & (cell_here < low + width)
            load = jnp.concatenate([jnp.where(inside, trace_here, 0.0), pad], axis=0)
            columns = lax.dot_general(
                onehot, load, (((1,), (1,)), ((), ())),
                precision=lax.Precision.HIGHEST, preferred_element_type=F32,
            )
            for t in range(tile.steps):
                column = columns if t == 0 else rolled(columns, -t, 1)
                r["surface"][t, m] = jnp.where(first, column, 0.0)

    out = run_kernel(
        body,
        {"cell": cell, "count": count, "trace": trace},
        {"surface": (tile.steps, tile.nx, tile.rows, LANES)},
        smem=("count",),
        name="surface_load",
        flops=2 * 10**6,
    )
    return out["surface"]


def halo_state(tile, got_even, got_odd):
    def body(r):
        tables = angle_tables(8)
        sign = x_sign()
        for m in range(tile.nx):
            for item in range(4):
                r["uh"][item, m] = halo_rows(tile, r, item, m)
            coefs = [halo_rows(tile, r, item, m) for item in range(4, 9)]
            for j in range(tile.nj):
                part = [value[:, j * LANES : (j + 1) * LANES] for value in coefs]
                store_weights(
                    r["wh"], m, pl.ds(0, 8), j, tables, sign, *part[:3],
                    part[3].astype(jnp.int32), part[4].astype(jnp.int32),
                )

    outs = {"uh": (4, tile.nx, 8, tile.nz), "wh": (9, tile.nx, 8, tile.nz)}
    out = run_kernel(
        body, {"got_even": got_even, "got_odd": got_odd}, outs, name="halo_state", flops=10**6
    )
    return out["uh"], out["wh"]


class Stage:
    def __init__(self, tile, state, ops, pieces, name):
        self.tile, self.state, self.ops, self.pieces, self.name = tile, state, ops, pieces, name
        self.ins, self.outs, self.scratch = {}, {}, {}

    def need(self, key):
        if key not in self.outs and key not in self.scratch:
            self.ins[key] = self.state[key]

    def run(self):
        tile = self.tile
        for t, m in self.ops:
            last = t == tile.steps - 1
            for key in ("w", "forward"):
                self.need(key)
            for k in (m - 1, m, m + 1):
                if k == -1 and not tile.far:
                    continue
                if k in (-1, tile.nx):
                    self.need(("xf", t) if k == -1 else ("xn", t))
                elif t == 0:
                    for key in ("now", "uh"):
                        self.need(key)
                else:
                    self.need(("u", t, k))
            if t <= 1:
                for key in ("before" if t == 0 else "now", "uh"):
                    self.need(key)
            else:
                self.need(("u", t - 1, m))
            if not last:
                self.need("wh")
            self.need("surface")
            if t > 0:
                self.need(("g", t - 1, m))
            rows = tile.ny if last else tile.rows
            self.outs[("u", t + 1, m)] = (2, rows, tile.nz)
            total = (tile.nj, 3, tile.ny, LANES)
            if last and any(m in planes for planes in self.pieces):
                self.scratch[("g", t, m)] = total
            else:
                self.outs[("g", t, m)] = total
        for planes in self.pieces:
            for m in planes:
                self.need(("g", tile.steps - 1, m))
            for k in range(tile.src):
                self.outs[("s", planes, k)] = (len(planes), 3, tile.ny, tile.nz // tile.src)
        flops = len(self.ops) * 2 * 10**6 + 10**5
        out = run_kernel(self.body, self.ins, self.outs, self.scratch, name=self.name, flops=flops)
        self.state.update(out)

    def body(self, r):
        tile = self.tile
        for t, m in self.ops:
            self.update(r, t, m)
        me = lax.axis_index("src")
        per = tile.nj // tile.src
        for planes in self.pieces:
            for i, m in enumerate(planes):
                for k in range(tile.src):
                    owner = jnp.bitwise_xor(me, k)
                    for part in range(per):
                        r[("s", planes, k)][i, :, :, lanes_of(part)] = r[("g", tile.steps - 1, m)][
                            owner * per + part
                        ]

    def field(self, r, t, m, c, j):
        tile, lanes = self.tile, lanes_of(j)
        if m == -1:
            return r[("xf", t)][c, :, lanes] if tile.far else None
        if m == tile.nx:
            return r[("xn", t)][c, :, lanes]
        if t > 0:
            return r[("u", t, m)][c, :, lanes]
        ref, item = (r["now"], c) if t == 0 else (r["before"], 2 + c)
        return jnp.concatenate(
            [ref[0, c, tile.place(m), :, lanes], r["uh"][item, m, :, lanes]], axis=0
        )

    def update(self, r, t, m):
        tile = self.tile
        last = t == tile.steps - 1
        rows = tile.ny if last else tile.rows
        lane = lax.broadcasted_iota(jnp.int32, (tile.rows, LANES), 1)
        at_first, at_last = lane == 0, lane == LANES - 1

        def weight(k, j):
            own = r["w"][k, m, :, lanes_of(j)]
            return own if last else jnp.concatenate([own, r["wh"][k, m, :, lanes_of(j)]], axis=0)

        centers, halves = [], []
        for c in range(2):
            center = [self.field(r, t, m, c, j) for j in range(tile.nj)]
            total_x, diff_x = [], []
            for j in range(tile.nj):
                above, below = self.field(r, t, m + 1, c, j), self.field(r, t, m - 1, c, j)
                total_x.append(above if below is None else above + below)
                diff_x.append(above if below is None else above - below)
            centers.append(center)
            halves.append((total_x, diff_x))

        def deeper(blocks):
            moved = [rolled(block, -1, 1) for block in blocks] + [0.0]
            return [jnp.where(at_last, moved[j + 1], moved[j]) for j in range(tile.nj)]

        def shallower(blocks):
            moved = [rolled(block, 1, 1) for block in blocks] + [0.0]
            return [jnp.where(at_first, moved[j - 1], moved[j]) for j in range(tile.nj)]

        shifted = []
        for c in range(2):
            diff_x = halves[c][1]
            shifted.append(
                (deeper(centers[c]), shallower(centers[c]), deeper(diff_x), shallower(diff_x))
            )

        def both(block):
            return rolled(block, -1, 0)[:rows], rolled(block, 1, 0)[:rows]

        for j in range(tile.nj):
            weights = [weight(k, j) for k in range(6)]
            results = []
            for c in range(2):
                center = centers[c][j]
                total_x, diff_x = halves[c][0][j], halves[c][1][j]
                below, above, diff_below, diff_above = (part[j] for part in shifted[c])
                total_z, slope_z = (below + above)[:rows], below - above
                mixed_xz = (diff_below - diff_above)[:rows]
                up, down = both(center)
                total_y = up + down
                up, down = both(diff_x)
                mixed_xy = up - down
                up, down = both(slope_z)
                mixed_yz = up - down
                total_x, center = total_x[:rows], center[:rows]
                axial = (
                    weights[0] * total_x + weights[1] * total_y + weights[2] * total_z
                    + weights[3] * mixed_xy + weights[4] * mixed_yz + weights[5] * mixed_xz
                )
                if c == 0:
                    results.append(total_x + total_y + total_z - 4.0 * center - axial)
                else:
                    results.append(axial - 2.0 * center)
            horiz, axial = results
            stretched, rooted, speed_sq = (weight(k, j) for k in range(6, 9))
            before = [self.field(r, t - 1, m, c, j)[:rows] for c in range(2)]
            new_p = (
                2.0 * centers[0][j][:rows] - before[0] + stretched * horiz + rooted * axial
            )
            new_q = 2.0 * centers[1][j][:rows] - before[1] + rooted * horiz + speed_sq * axial
            if j == 0:
                new_p = new_p + r["surface"][t, m][:rows]
            r[("u", t + 1, m)][0, :, lanes_of(j)] = new_p
            r[("u", t + 1, m)][1, :, lanes_of(j)] = new_q
            here = tile.place(m)
            forward_p = r["forward"][t, 0, 0, here, :, lanes_of(j)].astype(F32)
            forward_q = r["forward"][t, 0, 1, here, :, lanes_of(j)].astype(F32)
            horiz, axial = horiz[: tile.ny], axial[: tile.ny]
            terms = (
                forward_p * horiz,
                forward_p * axial + forward_q * horiz,
                forward_q * axial,
            )
            for k, term in enumerate(terms):
                if t > 0:
                    term = term + r[("g", t - 1, m)][j, k]
                r[("g", t, m)][j, k] = term


def combine(tile, state, pieces, raw):
    depth = tile.nz // tile.src
    ins = {key: raw[key] for key in ("velocity", "eps", "delta")}
    for planes in pieces:
        ins[("s", planes, 0)] = state[("s", planes, 0)]
        for k in range(1, tile.src):
            ins[("r", planes, k)] = state[("r", planes, k)]
    shape = (tile.nx, tile.ny, depth)

    def body(r):
        lanes = pl.ds(pl.multiple_of(lax.axis_index("src") * depth, LANES), depth)
        for planes in pieces:
            for i, m in enumerate(planes):
                here = tile.place(m)
                sums = []
                for item in range(3):
                    total = r[("s", planes, 0)][i, item]
                    for k in range(1, tile.src):
                        total = total + r[("r", planes, k)][i, item]
                    sums.append(total)
                velocity = r["velocity"][here, :, lanes]
                root = jnp.sqrt(1.0 + 2.0 * r["delta"][here, :, lanes])
                stretch = 1.0 + 2.0 * r["eps"][here, :, lanes]
                speed_sq = velocity * velocity
                r["gv"][here] = 2.0 * velocity * (stretch * sums[0] + root * sums[1] + sums[2])
                r["ge"][here] = 2.0 * speed_sq * sums[0]
                r["gd"][here] = speed_sq / root * sums[1]

    out = run_kernel(body, ins, {"gv": shape, "ge": shape, "gd": shape}, name="combine", flops=10**6)
    return out["gv"], out["ge"], out["gd"]


def final_fields(tile, state):
    keys = [("u", tile.steps, m) for m in range(tile.nx)]

    def body(r):
        for m, key in enumerate(keys):
            for c in range(2):
                r["out"][0, c, tile.place(m)] = r[key][c]

    outs = {"out": (1, 2, tile.nx, tile.ny, tile.nz)}
    return run_kernel(body, {key: state[key] for key in keys}, outs, name="final_fields", flops=10**6)["out"]


def on_device(
    mesh,
    adjoint_now,
    adjoint_before,
    forward_field,
    velocity,
    thomsen_eps,
    thomsen_delta,
    tilt_level,
    azimuth_level,
    channel_cell,
    channel_count,
    residual_trace,
):
    tile = Tile(mesh, velocity, forward_field.shape[0])
    raw = {
        "now": adjoint_now,
        "before": adjoint_before,
        "velocity": velocity,
        "eps": thomsen_eps,
        "delta": thomsen_delta,
        "tilt": tilt_level,
        "azimuth": azimuth_level,
    }
    send_even, send_odd = pack_edges(tile, raw)
    got_even = swap(send_even, "gy", tile.gy, 0)
    got_odd = swap(send_odd, "gy", tile.gy, 1)
    state = {"now": adjoint_now, "before": adjoint_before, "forward": forward_field}
    state["w"] = own_weights(tile, raw)
    state["surface"] = surface_load(tile, channel_cell, channel_count, residual_trace)

    def exchange(t, near, far):
        state[("xn", t)] = swap(near, "gx", tile.gx, 0)
        if tile.far:
            state[("xf", t)] = swap(far, "gx", tile.gx, 1)

    edges = edge_planes(tile, adjoint_now, got_even, got_odd)
    exchange(0, edges["near"], edges.get("far"))
    state["uh"], state["wh"] = halo_state(tile, got_even, got_odd)

    ops = [(t, m) for t in range(tile.steps) for m in range(tile.nx)]
    last = tile.steps - 1
    ready = {m: tile.phase(last, m) for m in range(tile.nx)}
    issue = {}
    for m in range(tile.nx):
        issue.setdefault(max(ready[m], 1), []).append(m)
    pieces = []
    edge = {tile.nx - 1} | ({0} if tile.far else set())
    for phase in range(tile.steps + 1):
        mine = [op for op in ops if tile.phase(*op) == phase]
        front = [op for op in mine if phase > 0 and op[0] == phase - 1 and op[1] in edge]
        bulk = [op for op in mine if op not in front]
        done = [tuple(issue[phase])] if phase in issue else []
        pieces += done
        if phase == tile.steps:
            front, bulk = mine, []
        if front:
            Stage(tile, state, front, [] if bulk else done, f"front_{phase}").run()
            if phase < tile.steps:
                exchange(phase, state[("u", phase, tile.nx - 1)], state.get(("u", phase, 0)))
        if bulk:
            Stage(tile, state, bulk, done, f"bulk_{phase}").run()
        for planes in done:
            for k in range(1, tile.src):
                state[("r", planes, k)] = lax.ppermute(
                    state[("s", planes, k)], "src", [(i, i ^ k) for i in range(tile.src)]
                )
    following = final_fields(tile, state)
    return (following, *combine(tile, state, pieces, raw))


def solution(mesh):
    placed = (
        P("src", None, "gx", "gy", None),
        P("src", None, "gx", "gy", None),
        P(None, "src", None, "gx", "gy", None),
        P("gx", "gy", None),
        P("gx", "gy", None),
        P("gx", "gy", None),
        P("gx", "gy", None),
        P("gx", "gy", None),
        P("src", None),
        P("src"),
        P("src", None, None),
    )

    def program(*args):
        return on_device(mesh, *args)

    return jax.shard_map(
        program,
        mesh=mesh,
        in_specs=placed,
        out_specs=(
            P("src", None, "gx", "gy", None),
            P("gx", "gy", "src"),
            P("gx", "gy", "src"),
            P("gx", "gy", "src"),
        ),
        check_vma=False,
    )
```

time: 218 us -> 52.8 us (0.24)
  the two profiles are of different devices: /device:TPU:0 before, /device:TPU:1 now
where the time goes in v1:
time: 52.8 us; the launch traced here: 52.4 us
  starting transfers between devices  24.9 us (47%)
  waiting for transfers between devices  10.3 us (20%)
  Pallas kernels  8.89 us (17%)
  local copies, waits for them, and re-layouts  6.87 us (13%)
  between operations  1.5 us (3%)
    ppermute x9, starting transfers between devices, on_device(): lax.ppermute(state['s', planes, k], 'src', [(i, i ^ k) for i in range(til...  15.3 us
    ppermute x5, starting transfers between devices, swap(): return lax.ppermute(block, axis, pair_swaps(count, first))  9.55 us
    pallas_call x13, Pallas kernels, run_kernel(): pl.pallas_call(kernel, name=name, out_shape=[jax.ShapeDtypeStruct(shape,...  8.89 us
    unnamed x33, local copies, waits for them, and re-layouts  6.87 us
    ppermute x5, waiting for transfers between devices, swap(): return lax.ppermute(block, axis, pair_swaps(count, first))  6.6 us
    ppermute x9, waiting for transfers between devices, on_device(): lax.ppermute(state['s', planes, k], 'src', [(i, i ^ k) for i in range(til...  3.71 us
  transfers between devices with their start and end apart: 14, of which 5 were waited for; matrix products, arithmetic and copies ran while one was open for 0% of the time, Pallas kernels for 14%

profile of v1, /device:TPU:1, one launch (start us, length us, event | category | flops | bytes accessed | tf_op | source)
XLA Modules:
  0.0 52.4 jit_solution(7554133764242491159)
XLA Ops:
  0.6 0.0 copy-start.1
  0.6 1.0 %copy-done.1 = f32[1,2,4,32,512]{4,3,2,1,0:T(8,128)S(1)} copy-done((f32[1,2,4,32,512]{4,3,2,1,0:T(8,128)S(1)}, f32[1,2,4,32,512]{4,3,2,1,0:T(8,128)}, u32[]{:S(2)}) %copy-start.1) | copy-done | bytes 524312
  1.7 1.0 %copy-done.3 = f32[1,2,4,32,512]{4,3,2,1,0:T(8,128)S(1)} copy-done((f32[1,2,4,32,512]{4,3,2,1,0:T(8,128)S(1)}, f32[1,2,4,32,512]{4,3,2,1,0:T(8,128)}, u32[]{:S(2)}) %copy-start.3) | copy-done | bytes 524312
  2.7 0.9 %copy-done.5 = f32[4,32,512]{2,1,0:T(8,128)S(1)} copy-done((f32[4,32,512]{2,1,0:T(8,128)S(1)}, f32[4,32,512]{2,1,0:T(8,128)}, u32[]{:S(2)}) %copy-start.5) | copy-done | bytes 262168
  3.7 0.9 %copy-done.7 = f32[4,32,512]{2,1,0:T(8,128)S(1)} copy-done((f32[4,32,512]{2,1,0:T(8,128)S(1)}, f32[4,32,512]{2,1,0:T(8,128)}, u32[]{:S(2)}) %copy-start.7) | copy-done | bytes 262168
  4.6 0.9 %copy-done.9 = f32[4,32,512]{2,1,0:T(8,128)S(1)} copy-done((f32[4,32,512]{2,1,0:T(8,128)S(1)}, f32[4,32,512]{2,1,0:T(8,128)}, u32[]{:S(2)}) %copy-start.9) | copy-done | bytes 262168
  5.6 0.9 %copy-done.11 = s32[4,32,512]{2,1,0:T(8,128)S(1)} copy-done((s32[4,32,512]{2,1,0:T(8,128)S(1)}, s32[4,32,512]{2,1,0:T(8,128)}, u32[]{:S(2)}) %copy-start.11) | copy-done | bytes 262168
  6.5 0.9 %copy-done.12 = s32[4,32,512]{2,1,0:T(8,128)S(1)} copy-done((s32[4,32,512]{2,1,0:T(8,128)S(1)}, s32[4,32,512]{2,1,0:T(8,128)}, u32[]{:S(2)}) %copy-start.12) | copy-done | bytes 262168
  7.5 0.1 pack_edges.1
  7.6 0.1 collective-permute-start
  7.7 4.6 %collective-permute-start.1 = (f32[9,2,8,512]{3,2,1,0:T(8,128)S(1)}, f32[9,2,8,512]{3,2,1,0:T(8,128)S(1)}, u32[]{:S(2)}, u32[]{:S(2)}) collective-permute-start(f32[9,2,8,512]{3,2,1,0:T(8,128)S(1)} %get-tuple-element.41), channel_id=1, source_target_pairs={{1,2},{2,1},{5,6},{6,5},{9,10},{10,9},{13,14},{14,13},{17,18},{18,... | collective-permute-start | bytes 884744 | tf_op jit(solution)/shard_map/ppermute | solution.py:47
  12.3 0.0 collective-permute-done.refs_0_.refs_1_
  12.3 4.4 %collective-permute-done.1.refs_1_.refs_2_ = f32[9,2,8,512]{3,2,1,0:T(8,128)S(1)} collective-permute-done((f32[9,2,8,512]{3,2,1,0:T(8,128)S(1)}, f32[9,2,8,512]{3,2,1,0:T(8,128)S(1)}, u32[]{:S(2)}, u32[]{:S(2)}) %collective-permute-start.1) | collective-permute-done | bytes 294944 | tf_op jit(solution)/shard_map/ppermute | solution.py:47
  16.7 0.0 copy-start
  16.7 0.0 copy-start.2
  16.8 0.0 copy-start.4
  16.8 1.8 %collective-permute-start.2 = (f32[2,40,512]{2,1,0:T(8,128)S(1)}, f32[2,40,512]{2,1,0:T(8,128)S(1)}, u32[]{:S(2)}, u32[]{:S(2)}) collective-permute-start(f32[2,40,512]{2,1,0:T(8,128)S(1)} %edge_planes.1), channel_id=1, source_target_pairs={{0,4},{4,0},{1,5},{5,1},{2,6},{6,2},{3,7},{7,3},{8,12},{12,8},{9,1... | collective-permute-start | bytes 491528 | tf_op jit(solution)/shard_map/ppermute | solution.py:47
  19.2 1.0 %surface_load.1.refs_6_.refs_7_.refs_8_ = f32[3,4,40,128]{3,2,1,0:T(8,128)S(1)} custom-call(s32[1,1536]{1,0:T(1,128)S(1)} %copy-done.14, s32[1]{0:T(128)S(6)} %copy.16.refs_1_, f32[1,3,1536]{2,1,0:T(4,128)S(1)} %copy.15.refs_2_), custom_call_target="tpu_custom_call" | custom-call | flops 2000000 | bytes 250000 | tf_op jit(solution)/shard_map/surface_load/pallas_call | solution.py:24
  20.3 1.4 %own_weights.1.refs_0_ = f32[9,4,32,512]{3,2,1,0:T(8,128)S(1)} custom-call(f32[4,32,512]{2,1,0:T(8,128)S(1)} %copy-done.6, f32[4,32,512]{2,1,0:T(8,128)S(1)} %copy-done.7, f32[4,32,512]{2,1,0:T(8,128)S(1)} %copy-done.10, s32[4,32,512]{2,1,0:T(8,128)S(1)} %copy-done.11, s32[4,32,512]{2,1,0:T(8,128)S(1)} %copy-done.13), custom_call_target="tpu_custom_call" | custom-call | flops 3000000 | bytes 375000 | tf_op jit(solution)/shard_map/own_weights/pallas_call | solution.py:24
  21.7 0.4 halo_state.1
  22.1 0.7 %collective-permute-done.2.refs_4_ = f32[2,40,512]{2,1,0:T(8,128)S(1)} collective-permute-done((f32[2,40,512]{2,1,0:T(8,128)S(1)}, f32[2,40,512]{2,1,0:T(8,128)S(1)}, u32[]{:S(2)}, u32[]{:S(2)}) %collective-permute-start.2) | collective-permute-done | bytes 163872 | tf_op jit(solution)/shard_map/ppermute | solution.py:47
  22.8 0.3 front_1.1
  23.1 1.6 %collective-permute-start.3 = (f32[2,40,512]{2,1,0:T(8,128)S(1)}, f32[2,40,512]{2,1,0:T(8,128)S(1)}, u32[]{:S(2)}, u32[]{:S(2)}) collective-permute-start(f32[2,40,512]{2,1,0:T(8,128)S(1)} %get-tuple-element.47.refs_4_.refs_3_.refs_5_), channel_id=1, source_target_pairs={{0,4},{4,0},{1,5},{5,1},{2,6},{6,2},{3,7},{7,3},{8,12},{12,8},{9,1... | collective-permute-start | bytes 491528 | tf_op jit(solution)/shard_map/ppermute | solution.py:47
  24.7 2.5 %bulk_0.1 = (f32[2,40,512]{2,1,0:T(8,128)}, f32[4,3,32,128]{3,2,1,0:T(8,128)}, f32[2,40,512]{2,1,0:T(8,128)S(1)}, f32[4,3,32,128]{3,2,1,0:T(8,128)}, f32[2,40,51...) custom-call(f32[9,4,32,512]{3,2,1,0:T(8,128)S(1)} %own_weights.1.ref, ...), custom_call_target="tpu_custom_call" | custom-call | flops 12100000 | bytes 1512500 | tf_op jit(solution)/shard_map/bulk_0/pallas_call | solution.py:24
  27.3 1.5 %collective-permute-done.3.refs_4_ = f32[2,40,512]{2,1,0:T(8,128)S(1)} collective-permute-done((f32[2,40,512]{2,1,0:T(8,128)S(1)}, f32[2,40,512]{2,1,0:T(8,128)S(1)}, u32[]{:S(2)}, u32[]{:S(2)}) %collective-permute-start.3) | collective-permute-done | bytes 163872 | tf_op jit(solution)/shard_map/ppermute | solution.py:47
  28.8 0.3 front_2.1
  29.1 1.4 %collective-permute-start.4 = (f32[2,40,512]{2,1,0:T(8,128)S(1)}, f32[2,40,512]{2,1,0:T(8,128)S(1)}, u32[]{:S(2)}, u32[]{:S(2)}) collective-permute-start(f32[2,40,512]{2,1,0:T(8,128)S(1)} %get-tuple-element.56.refs_4_.refs_3_), channel_id=1, source_target_pairs={{0,4},{4,0},{1,5},{5,1},{2,6},{6,2},{3,7},{7,3},{8,12},{12,8},{9,1... | collective-permute-start | bytes 491528 | tf_op jit(solution)/shard_map/ppermute | solution.py:47
  30.5 0.6 %bulk_1.1 = (f32[2,40,512]{2,1,0:T(8,128)S(1)}, f32[4,3,32,128]{3,2,1,0:T(8,128)S(1)}, f32[2,32,512]{2,1,0:T(8,128)S(1)}, f32[2,3,32,128]{3,2,1,0:T(8,128)S(1)},...) custom-call(f32[9,4,32,512]{3,2,1,0:T(8,128)S(1)} %own_weights.1.refs_0_, ...), custom_call_target="tpu_custom_call" | custom-call | flops 4100000 | bytes 512500 | tf_op jit(solution)/shard_map/bulk_1/pallas_call | solution.py:24
  31.2 1.4 %collective-permute-start.5 = (f32[2,3,32,128]{3,2,1,0:T(8,128)S(1)}, f32[2,3,32,128]{3,2,1,0:T(8,128)S(1)}, u32[]{:S(2)}, u32[]{:S(2)}) collective-permute-start(f32[2,3,32,128]{3,2,1,0:T(8,128)S(1)} %get-tuple-element.62), channel_id=1, source_target_pairs={{0,8},{8,0},{16,24},{24,16},{1,9},{9,1},{17,25},{25,17},{2,10},{10... | collective-permute-start | bytes 294920 | tf_op jit(solution)/shard_map/ppermute | solution.py:553
  32.5 2.3 %collective-permute-start.6 = (f32[2,3,32,128]{3,2,1,0:T(8,128)S(1)}, f32[2,3,32,128]{3,2,1,0:T(8,128)S(1)}, u32[]{:S(2)}, u32[]{:S(2)}) collective-permute-start(f32[2,3,32,128]{3,2,1,0:T(8,128)S(1)} %get-tuple-element.63), channel_id=1, source_target_pairs={{0,16},{8,24},{16,0},{24,8},{1,17},{9,25},{17,1},{25,9},{2,18},{10... | collective-permute-start | bytes 294920 | tf_op jit(solution)/shard_map/ppermute | solution.py:553
  34.8 0.0 collective-permute-start.7
  34.8 0.3 bulk_2.1
  35.2 0.4 collective-permute-start.8
  35.6 0.0 collective-permute-done.4.refs_4_
  35.6 3.2 %collective-permute-start.9 = (f32[1,3,32,128]{3,2,1,0:T(8,128)S(1)}, f32[1,3,32,128]{3,2,1,0:T(8,128)S(1)}, u32[]{:S(2)}, u32[]{:S(2)}) collective-permute-start(f32[1,3,32,128]{3,2,1,0:T(8,128)S(1)} %get-tuple-element.67), channel_id=1, source_target_pairs={{0,16},{8,24},{16,0},{24,8},{1,17},{9,25},{17,1},{25,9},{2,18},{10... | collective-permute-start | bytes 147464 | tf_op jit(solution)/shard_map/ppermute | solution.py:553
  38.8 0.3 front_3.1
  39.1 0.0 collective-permute-done.5.refs_4_
  39.1 0.5 collective-permute-start.10
  39.6 1.1 %collective-permute-start.11 = (f32[1,3,32,128]{3,2,1,0:T(8,128)S(1)}, f32[1,3,32,128]{3,2,1,0:T(8,128)S(1)}, u32[]{:S(2)}, u32[]{:S(2)}) collective-permute-start(f32[1,3,32,128]{3,2,1,0:T(8,128)S(1)} %get-tuple-element.70), channel_id=1, source_target_pairs={{0,8},{8,0},{16,24},{24,16},{1,9},{9,1},{17,25},{25,17},{2,10},{10... | collective-permute-start | bytes 147464 | tf_op jit(solution)/shard_map/ppermute | solution.py:553
  40.7 0.0 collective-permute-done.7.refs_6_
  40.7 6.2 %collective-permute-start.12 = (f32[1,3,32,128]{3,2,1,0:T(8,128)S(1)}, f32[1,3,32,128]{3,2,1,0:T(8,128)S(1)}, u32[]{:S(2)}, u32[]{:S(2)}) collective-permute-start(f32[1,3,32,128]{3,2,1,0:T(8,128)S(1)} %get-tuple-element.71), channel_id=1, source_target_pairs={{0,16},{8,24},{16,0},{24,8},{1,17},{9,25},{17,1},{25,9},{2,18},{10... | collective-permute-start | bytes 147464 | tf_op jit(solution)/shard_map/ppermute | solution.py:553
  46.9 0.0 collective-permute-done.8.refs_8_
  46.9 0.2 collective-permute-start.13
  47.1 0.8 %final_fields.1 = f32[1,2,4,32,512]{4,3,2,1,0:T(8,128)} custom-call(f32[2,32,512]{2,1,0:T(8,128)S(1)} %get-tuple-element.44.refs_0_, f32[2,32,512]{2,1,0:T(8,128)S(1)} %get-tuple-element.53.refs_1_, f32[2,32,512]{2,1,0:T(8,128)S(1)} %get-tuple-element.58.refs_2_, f32[2,32,512]{2,1,0:T(8,128)S(1)} %get-tuple-element.60.refs_3_), custom_call_target="tpu_custom_call" | custom-call | flops 1000000 | bytes 125000 | tf_op jit(solution)/shard_map/final_fields/pallas_call | solution.py:24
  48.0 0.0 collective-permute-done.9.refs_9_
  48.0 1.0 %collective-permute-done.12.refs_13_ = f32[1,3,32,128]{3,2,1,0:T(8,128)S(1)} collective-permute-done((f32[1,3,32,128]{3,2,1,0:T(8,128)S(1)}, f32[1,3,32,128]{3,2,1,0:T(8,128)S(1)}, u32[]{:S(2)}, u32[]{:S(2)}) %collective-permute-start.12) | collective-permute-done | bytes 49184 | tf_op jit(solution)/shard_map/ppermute | solution.py:553
  48.9 2.7 %collective-permute-done.13.refs_14_ = f32[1,3,32,128]{3,2,1,0:T(8,128)S(1)} collective-permute-done((f32[1,3,32,128]{3,2,1,0:T(8,128)S(1)}, f32[1,3,32,128]{3,2,1,0:T(8,128)S(1)}, u32[]{:S(2)}, u32[]{:S(2)}) %collective-permute-start.13) | collective-permute-done | bytes 49184 | tf_op jit(solution)/shard_map/ppermute | solution.py:553
  51.7 0.7 %combine.1 = (f32[4,32,128]{2,1,0:T(8,128)}, f32[4,32,128]{2,1,0:T(8,128)}, f32[4,32,128]{2,1,0:T(8,128)}) custom-call(f32[4,32,512]{2,1,0:T(8,128)S(1)} %copy-done.6, f32[4,32,512]{2,1,0:T(8,128)S(1)} %copy-done.8, f32[4,32,512]{2,1,0:T(8,128)S(1)} %copy-done.10, f32[2,3,32,128]{3,2,1,0:T(8,128)S(1)} %get-tuple-element.61.refs_3_, ...), custom_call_target="tpu_custom_call" | custom-call | flops 1000000 | bytes 125000 | tf_op jit(solution)/shard_map/combine/pallas_call | solution.py:24
  (26 shorter events, 0.1 us)
Async XLA Ops:
  0.6 1.0 %copy-start.1 = (f32[1,2,4,32,512]{4,3,2,1,0:T(8,128)S(1)}, f32[1,2,4,32,512]{4,3,2,1,0:T(8,128)}, u32[]{:S(2)}) copy-start(f32[1,2,4,32,512]{4,3,2,1,0:T(8,128)} %refs_5_.7) | copy-start | bytes 1572868
  1.7 1.0 %copy-start.3 = (f32[1,2,4,32,512]{4,3,2,1,0:T(8,128)S(1)}, f32[1,2,4,32,512]{4,3,2,1,0:T(8,128)}, u32[]{:S(2)}) copy-start(f32[1,2,4,32,512]{4,3,2,1,0:T(8,128)} %refs_5_.5) | copy-start | bytes 1572868
  2.7 0.9 %copy-start.5 = (f32[4,32,512]{2,1,0:T(8,128)S(1)}, f32[4,32,512]{2,1,0:T(8,128)}, u32[]{:S(2)}) copy-start(f32[4,32,512]{2,1,0:T(8,128)} %refs_0_.9) | copy-start | bytes 786436
  3.7 0.9 %copy-start.7 = (f32[4,32,512]{2,1,0:T(8,128)S(1)}, f32[4,32,512]{2,1,0:T(8,128)}, u32[]{:S(2)}) copy-start(f32[4,32,512]{2,1,0:T(8,128)} %refs_1_.18) | copy-start | bytes 786436
  4.6 0.9 %copy-start.9 = (f32[4,32,512]{2,1,0:T(8,128)S(1)}, f32[4,32,512]{2,1,0:T(8,128)}, u32[]{:S(2)}) copy-start(f32[4,32,512]{2,1,0:T(8,128)} %refs_2_.10) | copy-start | bytes 786436
  5.6 0.9 %copy-start.11 = (s32[4,32,512]{2,1,0:T(8,128)S(1)}, s32[4,32,512]{2,1,0:T(8,128)}, u32[]{:S(2)}) copy-start(s32[4,32,512]{2,1,0:T(8,128)} %refs_5_.4) | copy-start | bytes 786436
  6.5 0.9 %copy-start.12 = (s32[4,32,512]{2,1,0:T(8,128)S(1)}, s32[4,32,512]{2,1,0:T(8,128)}, u32[]{:S(2)}) copy-start(s32[4,32,512]{2,1,0:T(8,128)} %refs_6_.1) | copy-start | bytes 786436
  7.5 11.7 %copy-start.15 = (f32[1,3,1536]{2,0,1:T(1,128)S(1)}, f32[1,3,1536]{2,0,1:T(1,128)}, u32[]{:S(2)}) copy-start(f32[1,3,1536]{2,0,1:T(1,128)} %param.21) | copy-start | bytes 55300
  7.5 11.8 %copy-start.14 = (s32[1,1536]{1,0:T(1,128)S(1)}, s32[1,1536]{1,0:T(1,128)}, u32[]{:S(2)}) copy-start(s32[1,1536]{1,0:T(1,128)} %refs_0_.7) | copy-start | bytes 18436
  7.5 12.8 %copy-start.6 = (f32[4,32,512]{2,1,0:T(8,128)S(1)}, f32[4,32,512]{2,1,0:T(8,128)}, u32[]{:S(2)}) copy-start(f32[4,32,512]{2,1,0:T(8,128)} %refs_0_.9) | copy-start | bytes 786436
  7.5 12.8 %copy-start.10 = (f32[4,32,512]{2,1,0:T(8,128)S(1)}, f32[4,32,512]{2,1,0:T(8,128)}, u32[]{:S(2)}) copy-start(f32[4,32,512]{2,1,0:T(8,128)} %refs_2_.10) | copy-start | bytes 786436
  7.5 12.8 %copy-start.13 = (s32[4,32,512]{2,1,0:T(8,128)S(1)}, s32[4,32,512]{2,1,0:T(8,128)}, u32[]{:S(2)}) copy-start(s32[4,32,512]{2,1,0:T(8,128)} %refs_6_.1) | copy-start | bytes 786436
  7.6 4.7 %collective-permute-start = (f32[9,2,8,512]{3,2,1,0:T(8,128)S(1)}, f32[9,2,8,512]{3,2,1,0:T(8,128)S(1)}, u32[]{:S(2)}, u32[]{:S(2)}) collective-permute-start(f32[9,2,8,512]{3,2,1,0:T(8,128)S(1)} %get-tuple-element.40), channel_id=1, source_target_pairs={{0,1},{1,0},{2,3},{3,2},{4,5},{5,4},{6,7},{7,6},{8,9},{9,8},{10,11... | collective-permute-start | bytes 884744 | tf_op jit(solution)/shard_map/ppermute | solution.py:47
  7.7 9.0 %collective-permute-start.1 = (f32[9,2,8,512]{3,2,1,0:T(8,128)S(1)}, f32[9,2,8,512]{3,2,1,0:T(8,128)S(1)}, u32[]{:S(2)}, u32[]{:S(2)}) collective-permute-start(f32[9,2,8,512]{3,2,1,0:T(8,128)S(1)} %get-tuple-element.41), channel_id=1, source_target_pairs={{1,2},{2,1},{5,6},{6,5},{9,10},{10,9},{13,14},{14,13},{17,18},{18,... | collective-permute-start | bytes 884744 | tf_op jit(solution)/shard_map/ppermute | solution.py:47
  16.7 6.0 %copy-start = (bf16[3,1,2,4,32,512]{5,4,3,2,1,0:T(8,128)(2,1)S(1)}, bf16[3,1,2,4,32,512]{5,4,3,2,1,0:T(8,128)(2,1)}, u32[]{:S(2)}) copy-start(bf16[3,1,2,4,32,512]{5,4,3,2,1,0:T(8,128)(2,1)} %refs_1_.17) | copy-start | bytes 2359300
  16.7 6.0 %copy-start.2 = (f32[1,2,4,32,512]{4,3,2,1,0:T(8,128)S(1)}, f32[1,2,4,32,512]{4,3,2,1,0:T(8,128)}, u32[]{:S(2)}) copy-start(f32[1,2,4,32,512]{4,3,2,1,0:T(8,128)} %refs_5_.7) | copy-start | bytes 1572868
  16.8 6.0 %copy-start.4 = (f32[1,2,4,32,512]{4,3,2,1,0:T(8,128)S(1)}, f32[1,2,4,32,512]{4,3,2,1,0:T(8,128)}, u32[]{:S(2)}) copy-start(f32[1,2,4,32,512]{4,3,2,1,0:T(8,128)} %refs_5_.5) | copy-start | bytes 1572868
  16.8 6.0 %collective-permute-start.2 = (f32[2,40,512]{2,1,0:T(8,128)S(1)}, f32[2,40,512]{2,1,0:T(8,128)S(1)}, u32[]{:S(2)}, u32[]{:S(2)}) collective-permute-start(f32[2,40,512]{2,1,0:T(8,128)S(1)} %edge_planes.1), channel_id=1, source_target_pairs={{0,4},{4,0},{1,5},{5,1},{2,6},{6,2},{3,7},{7,3},{8,12},{12,8},{9,1... | collective-permute-start | bytes 491528 | tf_op jit(solution)/shard_map/ppermute | solution.py:47
  23.1 5.7 %collective-permute-start.3 = (f32[2,40,512]{2,1,0:T(8,128)S(1)}, f32[2,40,512]{2,1,0:T(8,128)S(1)}, u32[]{:S(2)}, u32[]{:S(2)}) collective-permute-start(f32[2,40,512]{2,1,0:T(8,128)S(1)} %get-tuple-element.47.refs_4_.refs_3_.refs_5_), channel_id=1, source_target_pairs={{0,4},{4,0},{1,5},{5,1},{2,6},{6,2},{3,7},{7,3},{8,12},{12,8},{9,1... | collective-permute-start | bytes 491528 | tf_op jit(solution)/shard_map/ppermute | solution.py:47
  29.1 6.4 %collective-permute-start.4 = (f32[2,40,512]{2,1,0:T(8,128)S(1)}, f32[2,40,512]{2,1,0:T(8,128)S(1)}, u32[]{:S(2)}, u32[]{:S(2)}) collective-permute-start(f32[2,40,512]{2,1,0:T(8,128)S(1)} %get-tuple-element.56.refs_4_.refs_3_), channel_id=1, source_target_pairs={{0,4},{4,0},{1,5},{5,1},{2,6},{6,2},{3,7},{7,3},{8,12},{12,8},{9,1... | collective-permute-start | bytes 491528 | tf_op jit(solution)/shard_map/ppermute | solution.py:47
  31.2 7.9 %collective-permute-start.5 = (f32[2,3,32,128]{3,2,1,0:T(8,128)S(1)}, f32[2,3,32,128]{3,2,1,0:T(8,128)S(1)}, u32[]{:S(2)}, u32[]{:S(2)}) collective-permute-start(f32[2,3,32,128]{3,2,1,0:T(8,128)S(1)} %get-tuple-element.62), channel_id=1, source_target_pairs={{0,8},{8,0},{16,24},{24,16},{1,9},{9,1},{17,25},{25,17},{2,10},{10... | collective-permute-start | bytes 294920 | tf_op jit(solution)/shard_map/ppermute | solution.py:553
  32.5 7.1 %collective-permute-start.6 = (f32[2,3,32,128]{3,2,1,0:T(8,128)S(1)}, f32[2,3,32,128]{3,2,1,0:T(8,128)S(1)}, u32[]{:S(2)}, u32[]{:S(2)}) collective-permute-start(f32[2,3,32,128]{3,2,1,0:T(8,128)S(1)} %get-tuple-element.63), channel_id=1, source_target_pairs={{0,16},{8,24},{16,0},{24,8},{1,17},{9,25},{17,1},{25,9},{2,18},{10... | collective-permute-start | bytes 294920 | tf_op jit(solution)/shard_map/ppermute | solution.py:553
  34.8 5.8 %collective-permute-start.7 = (f32[2,3,32,128]{3,2,1,0:T(8,128)S(1)}, f32[2,3,32,128]{3,2,1,0:T(8,128)S(1)}, u32[]{:S(2)}, u32[]{:S(2)}) collective-permute-start(f32[2,3,32,128]{3,2,1,0:T(8,128)S(1)} %get-tuple-element.64), channel_id=1, source_target_pairs={{0,24},{8,16},{16,8},{24,0},{1,25},{9,17},{17,9},{25,1},{2,26},{10... | collective-permute-start | bytes 294920 | tf_op jit(solution)/shard_map/ppermute | solution.py:553
  35.2 11.8 %collective-permute-start.8 = (f32[1,3,32,128]{3,2,1,0:T(8,128)S(1)}, f32[1,3,32,128]{3,2,1,0:T(8,128)S(1)}, u32[]{:S(2)}, u32[]{:S(2)}) collective-permute-start(f32[1,3,32,128]{3,2,1,0:T(8,128)S(1)} %get-tuple-element.66), channel_id=1, source_target_pairs={{0,8},{8,0},{16,24},{24,16},{1,9},{9,1},{17,25},{25,17},{2,10},{10... | collective-permute-start | bytes 147464 | tf_op jit(solution)/shard_map/ppermute | solution.py:553
  35.6 12.4 %collective-permute-start.9 = (f32[1,3,32,128]{3,2,1,0:T(8,128)S(1)}, f32[1,3,32,128]{3,2,1,0:T(8,128)S(1)}, u32[]{:S(2)}, u32[]{:S(2)}) collective-permute-start(f32[1,3,32,128]{3,2,1,0:T(8,128)S(1)} %get-tuple-element.67), channel_id=1, source_target_pairs={{0,16},{8,24},{16,0},{24,8},{1,17},{9,25},{17,1},{25,9},{2,18},{10... | collective-permute-start | bytes 147464 | tf_op jit(solution)/shard_map/ppermute | solution.py:553
  38.8 12.9 %copy-start.8 = (f32[4,32,512]{2,1,0:T(8,128)S(1)}, f32[4,32,512]{2,1,0:T(8,128)}, u32[]{:S(2)}) copy-start(f32[4,32,512]{2,1,0:T(8,128)} %refs_1_.18) | copy-start | bytes 786436
  39.1 8.9 %collective-permute-start.10 = (f32[1,3,32,128]{3,2,1,0:T(8,128)S(1)}, f32[1,3,32,128]{3,2,1,0:T(8,128)S(1)}, u32[]{:S(2)}, u32[]{:S(2)}) collective-permute-start(f32[1,3,32,128]{3,2,1,0:T(8,128)S(1)} %get-tuple-element.68), channel_id=1, source_target_pairs={{0,24},{8,16},{16,8},{24,0},{1,25},{9,17},{17,9},{25,1},{2,26},{10... | collective-permute-start | bytes 147464 | tf_op jit(solution)/shard_map/ppermute | solution.py:553
  39.6 8.4 %collective-permute-start.11 = (f32[1,3,32,128]{3,2,1,0:T(8,128)S(1)}, f32[1,3,32,128]{3,2,1,0:T(8,128)S(1)}, u32[]{:S(2)}, u32[]{:S(2)}) collective-permute-start(f32[1,3,32,128]{3,2,1,0:T(8,128)S(1)} %get-tuple-element.70), channel_id=1, source_target_pairs={{0,8},{8,0},{16,24},{24,16},{1,9},{9,1},{17,25},{25,17},{2,10},{10... | collective-permute-start | bytes 147464 | tf_op jit(solution)/shard_map/ppermute | solution.py:553
  40.7 8.2 %collective-permute-start.12 = (f32[1,3,32,128]{3,2,1,0:T(8,128)S(1)}, f32[1,3,32,128]{3,2,1,0:T(8,128)S(1)}, u32[]{:S(2)}, u32[]{:S(2)}) collective-permute-start(f32[1,3,32,128]{3,2,1,0:T(8,128)S(1)} %get-tuple-element.71), channel_id=1, source_target_pairs={{0,16},{8,24},{16,0},{24,8},{1,17},{9,25},{17,1},{25,9},{2,18},{10... | collective-permute-start | bytes 147464 | tf_op jit(solution)/shard_map/ppermute | solution.py:553
  46.9 4.7 %collective-permute-start.13 = (f32[1,3,32,128]{3,2,1,0:T(8,128)S(1)}, f32[1,3,32,128]{3,2,1,0:T(8,128)S(1)}, u32[]{:S(2)}, u32[]{:S(2)}) collective-permute-start(f32[1,3,32,128]{3,2,1,0:T(8,128)S(1)} %get-tuple-element.72), channel_id=1, source_target_pairs={{0,24},{8,16},{16,8},{24,0},{1,25},{9,17},{17,9},{25,1},{2,26},{10... | collective-permute-start | bytes 147464 | tf_op jit(solution)/shard_map/ppermute | solution.py:553

commit v2 on v1

--- a/solution.py
+++ b/solution.py
@@ -10,13 +10,19 @@
 LEVELS = 32
 LANES = 128
 HALO = 4
-VMEM_LIMIT = 16 * 1024 * 1024
+VMEM_LIMIT = 8 * 1024 * 1024
 F32 = jnp.float32
 
 
-def run_kernel(body, ins, outs, scratch=None, smem=(), name=None, flops=0):
-    scratch = scratch or {}
-    names = list(ins) + list(outs) + list(scratch)
+def run_kernel(body, ins, outs, scratch=None, spaces=None, copies=0, name=None, flops=0, final=False):
+    scratch, spaces = scratch or {}, spaces or {}
+    names = list(ins) + list(outs) + list(scratch) + ["done"]
+    ins = {
+        key: pltpu.with_memory_space_constraint(value, pltpu.HBM)
+        if spaces.get(key) == pltpu.HBM
+        else value
+        for key, value in ins.items()
+    }
 
     def kernel(*refs):
         body(dict(zip(names, refs)))
@@ -24,12 +30,18 @@
     results = pl.pallas_call(
         kernel,
         name=name,
-        out_shape=[jax.ShapeDtypeStruct(shape, F32) for shape in outs.values()],
+        out_shape=[
+            jax.ShapeDtypeStruct(shape, F32) if final else pltpu.VMEM(shape, kind)
+            for shape, kind in (
+                entry if isinstance(entry[0], tuple) else (entry, F32) for entry in outs.values()
+            )
+        ],
         in_specs=[
-            pl.BlockSpec(memory_space=pltpu.SMEM if key in smem else pltpu.VMEM) for key in ins
+            pl.BlockSpec(memory_space=spaces.get(key, pltpu.VMEM)) for key in ins
         ],
         out_specs=[pl.BlockSpec(memory_space=pltpu.VMEM)] * len(outs),
-        scratch_shapes=[pltpu.VMEM(shape, F32) for shape in scratch.values()],
+        scratch_shapes=list(scratch.values())
+        + [pltpu.SemaphoreType.DMA((copies,))] * (copies > 0),
         compiler_params=pltpu.CompilerParams(vmem_limit_bytes=VMEM_LIMIT),
         cost_estimate=pl.CostEstimate(flops=flops, bytes_accessed=flops // 8, transcendentals=0),
     )(*ins.values())
@@ -79,62 +91,109 @@
     return pltpu.roll(value, by % value.shape[axis], axis)
 
 
+UNITS = (
+    [("now", c, 0, 2) for c in range(2)]
+    + [("before", c, 0, 2) for c in range(2)]
+    + [(key, 0, 0, 2) for key in ("velocity", "eps", "delta", "tilt", "azimuth")]
+    + [("now", 0, 2, 1), ("now", 1, 2, 1)]
+)
+ITEMS = [("now", 0), ("now", 1), ("before", 0), ("before", 1)] + [
+    (key, 0) for key in ("velocity", "eps", "delta", "tilt", "azimuth")
+]
+
+
+def edge_rows():
+    placed, at = [], 0
+    for key, c, first, count in UNITS:
+        placed.append((key, c, first, count, at))
+        at += count
+    return placed, at
+
+
 def pack_edges(tile, raw):
-    shape = (9, tile.nx // 2, 2 * HALO, tile.nz)
+    placed, per_plane = edge_rows()
+    total = per_plane * tile.nx
+    assert total % 8 == 0
+    outs = {"even": (total, tile.nz), "odd": (total, tile.nz), "near": (2, tile.ny, tile.nz)}
+    if tile.far:
+        outs["far"] = outs["near"]
+    outs.update({key: (value.shape, value.dtype) for key, value in raw.items()})
 
     def body(r):
+        copies = []
+        for i, key in enumerate(raw):
+            copies.append(pltpu.make_async_copy(r[key + "_hbm"], r[key], r["done"].at[i]))
+            copies[-1].start()
+        for copy in copies:
+            copy.wait()
+        for c in range(2):
+            r["near"][c] = r["now"][0, c, tile.place(tile.nx - 1)]
+            if tile.far:
+                r["far"][c] = r["now"][0, c, tile.place(0)]
+
         odd = is_odd("gy") == 1
-        low_half = lax.broadcasted_iota(jnp.int32, (8, tile.nz), 0) < HALO
-
-        def rows(item, m, start):
+        sub = lax.broadcasted_iota(jnp.int32, (8, tile.nz), 0)
+
+        def rows_of(key, c, m, end):
             here = tile.place(m)
-            if item < 4:
-                ref = r["now"] if item < 2 else r["before"]
-                return ref[0, item % 2, here, pl.ds(start, 8), :]
-            ref = r[("velocity", "eps", "delta", "tilt", "azimuth")[item - 4]]
-            return ref[here, pl.ds(start, 8), :].astype(F32)
-
-        for item in range(9):
-            for pair in range(tile.nx // 2):
-                a, b = 2 * pair, 2 * pair + 1
-                top = jnp.where(
-                    low_half,
-                    rolled(rows(item, a, tile.ny - 8), HALO, 0),
-                    rows(item, b, tile.ny - 8),
-                )
-                bottom = jnp.where(low_half, rows(item, a, 0), rolled(rows(item, b, 0), HALO, 0))
-                r["even"][item, pair] = jnp.where(odd, bottom, top)
-                r["odd"][item, pair] = jnp.where(odd, top, bottom)
-
-    out = run_kernel(body, raw, {"even": shape, "odd": shape}, name="pack_edges", flops=10**6)
-    return out["even"], out["odd"]
-
-
-def halo_rows(tile, r, item, m):
+            rows = pl.ds(tile.ny - 8 if end == "_top" else 0, 8)
+            ref = r[key].at[0, c] if key in ("now", "before") else r[key]
+            return ref[here, rows, :].astype(F32)
+
+        for end in ("_top", "_low"):
+            blocks = [None] * (total // 8)
+            for m in range(tile.nx):
+                for key, c, first, count, at in placed:
+                    place = at + m * per_plane
+                    while count:
+                        slot, some = place % 8, min(count, 8 - place % 8)
+                        from_row = first if end == "_low" else 8 - first - some
+                        if end == "_top" and some < count:
+                            from_row = 8 - first - count
+                        block = rows_of(key, c, m, end)
+                        moved = rolled(block, slot - from_row, 0) if slot != from_row else block
+                        old = blocks[place // 8]
+                        blocks[place // 8] = (
+                            moved if old is None else jnp.where(sub >= slot, moved, old)
+                        )
+                        place, count, first = place + some, count - some, first + some
+            for i, block in enumerate(blocks):
+                rows = pl.ds(8 * i, 8)
+                if end == "_top":
+                    r["even"][rows, :] = block
+                    r["odd"][rows, :] = block
+                else:
+                    r["even"][rows, :] = jnp.where(odd, block, r["even"][rows, :])
+                    r["odd"][rows, :] = jnp.where(odd, r["odd"][rows, :], block)
+
+    ins = {key + "_hbm": value for key, value in raw.items()}
+    spaces = {key: pltpu.HBM for key in ins}
+    return run_kernel(
+        body, ins, outs, spaces=spaces, copies=len(raw), name="pack_edges", flops=10**6
+    )
+
+
+def halo_block(tile, r, key, c, m):
+    placed, per_plane = edge_rows()
     odd = is_odd("gy") == 1
-    low_half = lax.broadcasted_iota(jnp.int32, (8, tile.nz), 0) < HALO
-    even_got, odd_got = r["got_even"][item, m // 2], r["got_odd"][item, m // 2]
-    upper = jnp.where(odd, odd_got, even_got)
-    lower = jnp.where(odd, even_got, odd_got)
-    if m % 2 == 0:
-        return jnp.where(low_half, upper, rolled(lower, HALO, 0))
-    return jnp.where(low_half, rolled(upper, HALO, 0), lower)
-
-
-def edge_planes(tile, now, got_even, got_odd):
-    outs = {"near": (2, tile.rows, tile.nz)}
-    if tile.far:
-        outs["far"] = (2, tile.rows, tile.nz)
-
-    def body(r):
-        for key in outs:
-            m = tile.nx - 1 if key == "near" else 0
-            for c in range(2):
-                r[key][c, : tile.ny] = r["now"][0, c, tile.place(m)]
-                r[key][c, tile.ny :] = halo_rows(tile, r, c, m)
-
-    ins = {"now": now, "got_even": got_even, "got_odd": got_odd}
-    return run_kernel(body, ins, outs, name="edge_planes", flops=10**5)
+    sub = lax.broadcasted_iota(jnp.int32, (8, tile.nz), 0)
+    result = jnp.zeros((8, tile.nz), F32)
+    for name, part, first, count, at in placed:
+        if (name, part) != (key, c):
+            continue
+        place = at + m * per_plane
+        slot = place % 8
+        assert slot + count <= 8
+        rows = pl.ds(place - slot, 8)
+        even_got, odd_got = r["got_even"][rows, :], r["got_odd"][rows, :]
+        upper = jnp.where(odd, odd_got, even_got)
+        lower = jnp.where(odd, even_got, odd_got)
+        upper = rolled(upper, first - slot, 0) if slot != first else upper
+        bottom = 8 - first - count
+        lower = rolled(lower, bottom - slot, 0) if slot != bottom else lower
+        result = jnp.where((sub >= first) & (sub < first + count), upper, result)
+        result = jnp.where((sub >= bottom) & (sub < bottom + count), lower, result)
+    return result
 
 
 def angle_tables(rows):
@@ -181,10 +240,12 @@
     return 1.0 - 2.0 * is_odd("gx").astype(F32)
 
 
-def own_weights(tile, raw):
+def own_state(tile, raw, forward):
     coefs = ("velocity", "eps", "delta", "tilt", "azimuth")
 
     def body(r):
+        copy = pltpu.make_async_copy(r["forward_hbm"], r["forward"], r["done"].at[0])
+        copy.start()
         tables = angle_tables(8)
         sign = x_sign()
 
@@ -200,15 +261,18 @@
             return 0
 
         lax.fori_loop(0, tile.nx, plane, 0)
+        copy.wait()
 
     ins = {key: raw[key] for key in coefs}
-    out = run_kernel(
-        body, ins, {"w": (9, tile.nx, tile.ny, tile.nz)}, name="own_weights", flops=3 * 10**6
-    )
-    return out["w"]
-
-
-def surface_load(tile, cell, count, trace):
+    ins["forward_hbm"] = forward
+    outs = {"w": (9, tile.nx, tile.ny, tile.nz), "forward": (forward.shape, forward.dtype)}
+    return run_kernel(
+        body, ins, outs, spaces={"forward_hbm": pltpu.HBM}, copies=1, name="own_state",
+        flops=3 * 10**6,
+    )
+
+
+def surface_load(tile, cell, count, trace, after):
     channels = cell.shape[1]
     width = tile.ny * tile.gy
 
@@ -240,25 +304,31 @@
                 column = columns if t == 0 else rolled(columns, -t, 1)
                 r["surface"][t, m] = jnp.where(first, column, 0.0)
 
+    ins = {"cell": cell, "count": count, "trace": trace, "after": after}
+    outs = {"surface": (tile.steps, tile.nx, tile.rows, LANES)}
     out = run_kernel(
-        body,
-        {"cell": cell, "count": count, "trace": trace},
-        {"surface": (tile.steps, tile.nx, tile.rows, LANES)},
-        smem=("count",),
-        name="surface_load",
-        flops=2 * 10**6,
+        body, ins, outs, spaces={"count": pltpu.SMEM}, name="surface_load", flops=2 * 10**6
     )
     return out["surface"]
 
 
-def halo_state(tile, got_even, got_odd):
+def halo_state(tile, got_even, got_odd, after):
+    outs = {"uh": (4, tile.nx, 8, tile.nz), "wh": (9, tile.nx, 8, tile.nz), "near": (2, 8, tile.nz)}
+    if tile.far:
+        outs["far"] = outs["near"]
+
     def body(r):
         tables = angle_tables(8)
         sign = x_sign()
         for m in range(tile.nx):
-            for item in range(4):
-                r["uh"][item, m] = halo_rows(tile, r, item, m)
-            coefs = [halo_rows(tile, r, item, m) for item in range(4, 9)]
+            for item, (key, c) in enumerate(ITEMS[:4]):
+                block = halo_block(tile, r, key, c, m)
+                r["uh"][item, m] = block
+                if item < 2 and m == tile.nx - 1:
+                    r["near"][c] = block
+                if item < 2 and m == 0 and tile.far:
+                    r["far"][c] = block
+            coefs = [halo_block(tile, r, key, c, m) for key, c in ITEMS[4:]]
             for j in range(tile.nj):
                 part = [value[:, j * LANES : (j + 1) * LANES] for value in coefs]
                 store_weights(
@@ -266,17 +336,16 @@
                     part[3].astype(jnp.int32), part[4].astype(jnp.int32),
                 )
 
-    outs = {"uh": (4, tile.nx, 8, tile.nz), "wh": (9, tile.nx, 8, tile.nz)}
-    out = run_kernel(
-        body, {"got_even": got_even, "got_odd": got_odd}, outs, name="halo_state", flops=10**6
-    )
-    return out["uh"], out["wh"]
+    ins = {"got_even": got_even, "got_odd": got_odd, "after": after}
+    return run_kernel(body, ins, outs, name="halo_state", flops=10**6)
 
 
 class Stage:
-    def __init__(self, tile, state, ops, pieces, name):
+    def __init__(self, tile, state, ops, pieces, name, after=None):
         self.tile, self.state, self.ops, self.pieces, self.name = tile, state, ops, pieces, name
         self.ins, self.outs, self.scratch = {}, {}, {}
+        if after is not None:
+            self.ins["after"] = after
 
     def need(self, key):
         if key not in self.outs and key not in self.scratch:
@@ -292,7 +361,10 @@
                 if k == -1 and not tile.far:
                     continue
                 if k in (-1, tile.nx):
-                    self.need(("xf", t) if k == -1 else ("xn", t))
+                    key = "xf" if k == -1 else "xn"
+                    self.need((key, t))
+                    if t == 0:
+                        self.need((key + "h", t))
                 elif t == 0:
                     for key in ("now", "uh"):
                         self.need(key)
@@ -312,14 +384,19 @@
             self.outs[("u", t + 1, m)] = (2, rows, tile.nz)
             total = (tile.nj, 3, tile.ny, LANES)
             if last and any(m in planes for planes in self.pieces):
-                self.scratch[("g", t, m)] = total
+                self.scratch[("g", t, m)] = pltpu.VMEM(total, F32)
             else:
                 self.outs[("g", t, m)] = total
         for planes in self.pieces:
             for m in planes:
                 self.need(("g", tile.steps - 1, m))
-            for k in range(tile.src):
-                self.outs[("s", planes, k)] = (len(planes), 3, tile.ny, tile.nz // tile.src)
+            block = (len(planes), 3, tile.ny, tile.nz // tile.src)
+            if self.halved(planes):
+                self.outs[("keep", planes)] = (2, *block)
+                self.outs[("send", planes)] = (2, *block)
+            else:
+                for k in range(tile.src):
+                    self.outs[("s", planes, k)] = block
         flops = len(self.ops) * 2 * 10**6 + 10**5
         out = run_kernel(self.body, self.ins, self.outs, self.scratch, name=self.name, flops=flops)
         self.state.update(out)
@@ -334,17 +411,26 @@
             for i, m in enumerate(planes):
                 for k in range(tile.src):
                     owner = jnp.bitwise_xor(me, k)
+                    if self.halved(planes):
+                        target = r[("send" if k % 2 else "keep", planes)].at[k // 2]
+                    else:
+                        target = r[("s", planes, k)]
                     for part in range(per):
-                        r[("s", planes, k)][i, :, :, lanes_of(part)] = r[("g", tile.steps - 1, m)][
+                        target[i, :, :, lanes_of(part)] = r[("g", tile.steps - 1, m)][
                             owner * per + part
                         ]
 
+    def halved(self, planes):
+        return self.tile.src == 4 and self.tile.nx - 1 not in planes
+
     def field(self, r, t, m, c, j):
         tile, lanes = self.tile, lanes_of(j)
-        if m == -1:
-            return r[("xf", t)][c, :, lanes] if tile.far else None
-        if m == tile.nx:
-            return r[("xn", t)][c, :, lanes]
+        if m == -1 and not tile.far:
+            return None
+        if m in (-1, tile.nx):
+            key = "xf" if m == -1 else "xn"
+            block = r[(key, t)][c, :, lanes]
+            return jnp.concatenate([block, r[(key + "h", t)][c, :, lanes]], axis=0) if t == 0 else block
         if t > 0:
             return r[("u", t, m)][c, :, lanes]
         ref, item = (r["now"], c) if t == 0 else (r["before"], 2 + c)
@@ -442,13 +528,32 @@
                 r[("g", t, m)][j, k] = term
 
 
-def combine(tile, state, pieces, raw):
+def xor_swap(tile, block, k):
+    return lax.ppermute(block, "src", [(i, i ^ k) for i in range(tile.src)])
+
+
+def add_halves(keep, got):
+    block = keep.shape[1:]
+
+    def body(r):
+        r["own"][...] = r["keep"][0] + r["got"][0]
+        r["passed"][...] = r["keep"][1] + r["got"][1]
+
+    out = run_kernel(
+        body, {"keep": keep, "got": got}, {"own": block, "passed": block}, name="add_halves",
+        flops=10**5,
+    )
+    return out["own"], out["passed"]
+
+
+def combine(tile, state, pieces):
     depth = tile.nz // tile.src
-    ins = {key: raw[key] for key in ("velocity", "eps", "delta")}
+    ins = {key: state[key] for key in ("velocity", "eps", "delta")}
     for planes in pieces:
         ins[("s", planes, 0)] = state[("s", planes, 0)]
         for k in range(1, tile.src):
-            ins[("r", planes, k)] = state[("r", planes, k)]
+            if ("r", planes, k) in state:
+                ins[("r", planes, k)] = state[("r", planes, k)]
     shape = (tile.nx, tile.ny, depth)
 
     def body(r):
@@ -460,7 +565,8 @@
                 for item in range(3):
                     total = r[("s", planes, 0)][i, item]
                     for k in range(1, tile.src):
-                        total = total + r[("r", planes, k)][i, item]
+                        if ("r", planes, k) in r:
+                            total = total + r[("r", planes, k)][i, item]
                     sums.append(total)
                 velocity = r["velocity"][here, :, lanes]
                 root = jnp.sqrt(1.0 + 2.0 * r["delta"][here, :, lanes])
@@ -470,7 +576,7 @@
                 r["ge"][here] = 2.0 * speed_sq * sums[0]
                 r["gd"][here] = speed_sq / root * sums[1]
 
-    out = run_kernel(body, ins, {"gv": shape, "ge": shape, "gd": shape}, name="combine", flops=10**6)
+    out = run_kernel(body, ins, {"gv": shape, "ge": shape, "gd": shape}, name="combine", flops=10**6, final=True)
     return out["gv"], out["ge"], out["gd"]
 
 
@@ -483,7 +589,10 @@
                 r["out"][0, c, tile.place(m)] = r[key][c]
 
     outs = {"out": (1, 2, tile.nx, tile.ny, tile.nz)}
-    return run_kernel(body, {key: state[key] for key in keys}, outs, name="final_fields", flops=10**6)["out"]
+    out = run_kernel(
+        body, {key: state[key] for key in keys}, outs, name="final_fields", flops=10**6, final=True
+    )
+    return out["out"]
 
 
 def on_device(
@@ -510,32 +619,36 @@
         "tilt": tilt_level,
         "azimuth": azimuth_level,
     }
-    send_even, send_odd = pack_edges(tile, raw)
-    got_even = swap(send_even, "gy", tile.gy, 0)
-    got_odd = swap(send_odd, "gy", tile.gy, 1)
-    state = {"now": adjoint_now, "before": adjoint_before, "forward": forward_field}
-    state["w"] = own_weights(tile, raw)
-    state["surface"] = surface_load(tile, channel_cell, channel_count, residual_trace)
-
-    def exchange(t, near, far):
-        state[("xn", t)] = swap(near, "gx", tile.gx, 0)
+    edges = pack_edges(tile, raw)
+    state = {key: edges[key] for key in raw}
+
+    def exchange(key, t, near, far):
+        state[("xn" + key, t)] = swap(near, "gx", tile.gx, 0)
         if tile.far:
-            state[("xf", t)] = swap(far, "gx", tile.gx, 1)
-
-    edges = edge_planes(tile, adjoint_now, got_even, got_odd)
-    exchange(0, edges["near"], edges.get("far"))
-    state["uh"], state["wh"] = halo_state(tile, got_even, got_odd)
+            state[("xf" + key, t)] = swap(far, "gx", tile.gx, 1)
+
+    exchange("", 0, edges["near"], edges.get("far"))
+    got_odd = swap(edges["odd"], "gy", tile.gy, 1)
+    got_even = swap(edges["even"], "gy", tile.gy, 0)
+    state.update(own_state(tile, state, forward_field))
+    halo = halo_state(tile, got_even, got_odd, state["w"])
+    state["uh"], state["wh"] = halo["uh"], halo["wh"]
+    exchange("h", 0, halo["near"], halo.get("far"))
+    state["surface"] = surface_load(
+        tile, channel_cell, channel_count, residual_trace, halo["uh"]
+    )
 
     ops = [(t, m) for t in range(tile.steps) for m in range(tile.nx)]
     last = tile.steps - 1
     ready = {m: tile.phase(last, m) for m in range(tile.nx)}
     issue = {}
     for m in range(tile.nx):
-        issue.setdefault(max(ready[m], 1), []).append(m)
+        issue.setdefault(1 if ready[m] <= 1 else tile.steps, []).append(m)
     pieces = []
     edge = {tile.nx - 1} | ({0} if tile.far else set())
     for phase in range(tile.steps + 1):
         mine = [op for op in ops if tile.phase(*op) == phase]
+        after = state.get("token")
         front = [op for op in mine if phase > 0 and op[0] == phase - 1 and op[1] in edge]
         bulk = [op for op in mine if op not in front]
         done = [tuple(issue[phase])] if phase in issue else []
@@ -543,18 +656,22 @@
         if phase == tile.steps:
             front, bulk = mine, []
         if front:
-            Stage(tile, state, front, [] if bulk else done, f"front_{phase}").run()
+            Stage(tile, state, front, [] if bulk else done, f"front_{phase}", after).run()
             if phase < tile.steps:
-                exchange(phase, state[("u", phase, tile.nx - 1)], state.get(("u", phase, 0)))
+                exchange("", phase, state[("u", phase, tile.nx - 1)], state.get(("u", phase, 0)))
         if bulk:
             Stage(tile, state, bulk, done, f"bulk_{phase}").run()
+            state["token"] = state[("g", *next(op for op in bulk if ("g", *op) in state))]
         for planes in done:
-            for k in range(1, tile.src):
-                state[("r", planes, k)] = lax.ppermute(
-                    state[("s", planes, k)], "src", [(i, i ^ k) for i in range(tile.src)]
-                )
+            if ("send", planes) in state:
+                got = xor_swap(tile, state[("send", planes)], 1)
+                state[("s", planes, 0)], passed = add_halves(state[("keep", planes)], got)
+                state[("r", planes, 2)] = xor_swap(tile, passed, 2)
+            else:
+                for k in range(1, tile.src):
+                    state[("r", planes, k)] = xor_swap(tile, state[("s", planes, k)], k)
     following = final_fields(tile, state)
-    return (following, *combine(tile, state, pieces, raw))
+    return (following, *combine(tile, state, pieces))
 
 
 def solution(mesh):

time: 52.8 us -> 39.9 us (0.76)
  the two profiles are of different devices: /device:TPU:1 before, /device:TPU:2 now
where the time goes in v2:
time: 39.9 us; the launch traced here: 39.8 us
  starting transfers between devices  15.6 us (39%)
  waiting for transfers between devices  12.3 us (31%)
  Pallas kernels  10.5 us (26%)
  between operations  1.41 us (4%)
    pallas_call x13, Pallas kernels, run_kernel(): pl.pallas_call(kernel, name=name, out_shape=[jax.ShapeDtypeStruct(shape,...  10.5 us
    ppermute x5, starting transfers between devices, xor_swap(): return lax.ppermute(block, 'src', [(i, i ^ k) for i in range(tile.src)])  8.76 us
    ppermute x6, starting transfers between devices, swap(): return lax.ppermute(block, axis, pair_swaps(count, first))  6.81 us
    ppermute x6, waiting for transfers between devices, swap(): return lax.ppermute(block, axis, pair_swaps(count, first))  6.75 us
    ppermute x5, waiting for transfers between devices, xor_swap(): return lax.ppermute(block, 'src', [(i, i ^ k) for i in range(tile.src)])  5.52 us
  transfers between devices with their start and end apart: 11, of which 7 were waited for; matrix products, arithmetic and copies ran while one was open for 0% of the time, Pallas kernels for 19%

profile of v2, /device:TPU:2, one launch (start us, length us, event | category | flops | bytes accessed | tf_op | source)
XLA Modules:
  0.0 39.8 jit_solution(6357201805369732832)
XLA Ops:
  0.6 1.8 %pack_edges.1 = (f32[80,512]{1,0:T(8,128)S(1)}, f32[80,512]{1,0:T(8,128)S(1)}, f32[2,32,512]{2,1,0:T(8,128)S(1)}, f32[1,2,4,32,512]{4,3,2,1,0:T(8,128)S(1)}, f32...) custom-call(f32[1,2,4,32,512]{4,3,2,1,0:T(8,128)} %refs_0_.2, ...), custom_call_target="tpu_custom_call" | custom-call | flops 1000000 | bytes 125000 | tf_op jit(solution)/shard_map/pack_edges/pallas_call | solution.py:30
  2.4 0.1 collective-permute-start
  2.5 1.9 %collective-permute-start.1 = (f32[80,512]{1,0:T(8,128)S(1)}, f32[80,512]{1,0:T(8,128)S(1)}, u32[]{:S(2)}, u32[]{:S(2)}) collective-permute-start(f32[80,512]{1,0:T(8,128)S(1)} %get-tuple-element.58), channel_id=1, source_target_pairs={{1,2},{2,1},{5,6},{6,5},{9,10},{10,9},{13,14},{14,13},{17,18},{18,... | collective-permute-start | bytes 491528 | tf_op jit(solution)/shard_map/ppermute | solution.py:59
  4.4 2.2 %collective-permute-start.2 = (f32[2,32,512]{2,1,0:T(8,128)S(1)}, f32[2,32,512]{2,1,0:T(8,128)S(1)}, u32[]{:S(2)}, u32[]{:S(2)}) collective-permute-start(f32[2,32,512]{2,1,0:T(8,128)S(1)} %get-tuple-element.66), channel_id=1, source_target_pairs={{0,4},{4,0},{1,5},{5,1},{2,6},{6,2},{3,7},{7,3},{8,12},{12,8},{9,1... | collective-permute-start | bytes 393224 | tf_op jit(solution)/shard_map/ppermute | solution.py:59
  6.6 0.0 copy-start.1
  6.6 0.0 copy-start
  6.6 1.4 %own_state.1 = (f32[9,4,32,512]{3,2,1,0:T(8,128)S(1)}, bf16[3,1,2,4,32,512]{5,4,3,2,1,0:T(8,128)(2,1)S(1)}) custom-call(f32[4,32,512]{2,1,0:T(8,128)S(1)} %get-tuple-element.49.refs_0_, f32[4,32,512]{2,1,0:T(8,128)S(1)} %get-tuple-element.50.refs_1_, f32[4,32,512]{2,1,0:T(8,128)S(1)} %get-tuple-element.51.refs_2_, ...), custom_call_target="tpu_custom_call" | custom-call | flops 3000000 | bytes 375000 | tf_op jit(solution)/shard_map/own_state/pallas_call | solution.py:30
  8.0 0.0 collective-permute-done.refs_0_
  8.0 1.1 %collective-permute-done.1.refs_1_ = f32[80,512]{1,0:T(8,128)S(1)} collective-permute-done((f32[80,512]{1,0:T(8,128)S(1)}, f32[80,512]{1,0:T(8,128)S(1)}, u32[]{:S(2)}, u32[]{:S(2)}) %collective-permute-start.1) | collective-permute-done | bytes 163872 | tf_op jit(solution)/shard_map/ppermute | solution.py:59
  9.1 0.4 %halo_state.1 = (f32[4,4,8,512]{3,2,1,0:T(8,128)S(1)}, f32[9,4,8,512]{3,2,1,0:T(8,128)S(1)}, f32[2,8,512]{2,1,0:T(8,128)S(1)}) custom-call(f32[80,512]{1,0:T(8,128)S(1)} %collective-permute-done.refs_0_, f32[80,512]{1,0:T(8,128)S(1)} %collective-permute-done.1.refs_1_, f32[9,4,32,512]{3,2,1,0:T(8,128)S(1)} %get-tuple-element.54.refs_2_.refs_0_.refs_1_), custom_call_target="tpu_custom_call" | custom-call | flops 1000000 | bytes 125000 | tf_op jit(solution)/shard_map/halo_state/pallas_call | solution.py:30
  9.5 1.6 %collective-permute-start.3 = (f32[2,8,512]{2,1,0:T(8,128)S(1)}, f32[2,8,512]{2,1,0:T(8,128)S(1)}, u32[]{:S(2)}, u32[]{:S(2)}) collective-permute-start(f32[2,8,512]{2,1,0:T(8,128)S(1)} %get-tuple-element.67), channel_id=1, source_target_pairs={{0,4},{4,0},{1,5},{5,1},{2,6},{6,2},{3,7},{7,3},{8,12},{12,8},{9,1... | collective-permute-start | bytes 98312 | tf_op jit(solution)/shard_map/ppermute | solution.py:59
  11.8 0.0 copy-done.1
  11.8 0.0 copy-done
  11.8 1.0 %surface_load.1.refs_6_.refs_9_.refs_8_.refs_7_ = f32[3,4,40,128]{3,2,1,0:T(8,128)S(1)} custom-call(s32[1,1536]{1,0:T(1,128)S(1)} %copy-done, s32[1]{0:T(128)S(6)} %copy.16.refs_1_, f32[1,3,1536]{2,1,0:T(4,128)S(1)} %copy.15.refs_2_, f32[4,4,8,512]{3,2,1,0:T(8,128)S(1)} %get-tuple-element.59.refs_3_.refs_4_.refs_6_.refs_7_), custom_call_target="tpu_custom_call" | custom-call | flops 2000000 | bytes 250000 | tf_op jit(solution)/shard_map/surface_load/pallas_call | solution.py:30
  12.8 2.4 %bulk_0.1 = (f32[2,40,512]{2,1,0:T(8,128)}, f32[4,3,32,128]{3,2,1,0:T(8,128)S(1)}, f32[2,40,512]{2,1,0:T(8,128)S(1)}, f32[4,3,32,128]{3,2,1,0:T(8,128)}, f32[2,4...) custom-call(f32[9,4,32,512]{3,2,1,0:T(8,128)S(1)} %get-tuple-element, ...), custom_call_target="tpu_custom_call" | custom-call | flops 12100000 | bytes 1512500 | tf_op jit(solution)/shard_map/bulk_0/pallas_call | solution.py:30
  15.3 0.0 collective-permute-done.2.refs_5_
  15.3 0.0 collective-permute-done.3.refs_6_
  15.3 0.3 front_1.1
  15.6 0.6 %collective-permute-start.4 = (f32[2,40,512]{2,1,0:T(8,128)S(1)}, f32[2,40,512]{2,1,0:T(8,128)S(1)}, u32[]{:S(2)}, u32[]{:S(2)}) collective-permute-start(f32[2,40,512]{2,1,0:T(8,128)S(1)} %get-tuple-element.68.refs_4_.refs_6_), channel_id=1, source_target_pairs={{0,4},{4,0},{1,5},{5,1},{2,6},{6,2},{3,7},{7,3},{8,12},{12,8},{9,1... | collective-permute-start | bytes 491528 | tf_op jit(solution)/shard_map/ppermute | solution.py:59
  16.2 0.6 %bulk_1.1 = (f32[2,40,512]{2,1,0:T(8,128)S(1)}, f32[4,3,32,128]{3,2,1,0:T(8,128)S(1)}, f32[2,32,512]{2,1,0:T(8,128)S(1)}, f32[2,2,3,32,128]{4,3,2,1,0:T(8,128)S(1)}, f32[2,2,3,32,128]{4,3,2,1,0:T(8,128)S(1)}) custom-call(f32[9,4,32,512]{3,2,1,0:T(8,128)S(1)} %get-tuple-element.54.refs_2_.refs_0_.refs_1_, ...), custom_call_target="tpu_custom_call" | custom-call | flops 4100000 | bytes 512500 | tf_op jit(solution)/shard_map/bulk_1/pallas_call | solution.py:30
  16.8 1.6 %collective-permute-start.6 = (f32[2,2,3,32,128]{4,3,2,1,0:T(8,128)S(1)}, f32[2,2,3,32,128]{4,3,2,1,0:T(8,128)S(1)}, u32[]{:S(2)}, u32[]{:S(2)}) collective-permute-start(f32[2,2,3,32,128]{4,3,2,1,0:T(8,128)S(1)} %get-tuple-element.84), channel_id=1, source_target_pairs={{0,8},{8,0},{16,24},{24,16},{1,9},{9,1},{17,25},{25,17},{2,10},{10... | collective-permute-start | bytes 589832 | tf_op jit(solution)/shard_map/ppermute | solution.py:532
  18.5 3.9 %collective-permute-done.4.refs_5_ = f32[2,40,512]{2,1,0:T(8,128)S(1)} collective-permute-done((f32[2,40,512]{2,1,0:T(8,128)S(1)}, f32[2,40,512]{2,1,0:T(8,128)S(1)}, u32[]{:S(2)}, u32[]{:S(2)}) %collective-permute-start.4) | collective-permute-done | bytes 163872 | tf_op jit(solution)/shard_map/ppermute | solution.py:59
  22.3 0.3 front_2.1
  22.7 0.5 %collective-permute-start.5 = (f32[2,40,512]{2,1,0:T(8,128)S(1)}, f32[2,40,512]{2,1,0:T(8,128)S(1)}, u32[]{:S(2)}, u32[]{:S(2)}) collective-permute-start(f32[2,40,512]{2,1,0:T(8,128)S(1)} %get-tuple-element.78.refs_4_), channel_id=1, source_target_pairs={{0,4},{4,0},{1,5},{5,1},{2,6},{6,2},{3,7},{7,3},{8,12},{12,8},{9,1... | collective-permute-start | bytes 491528 | tf_op jit(solution)/shard_map/ppermute | solution.py:59
  23.1 0.3 bulk_2.1
  23.4 0.2 collective-permute-done.6.refs_1_
  23.6 2.7 %collective-permute-start.7 = (f32[2,3,32,128]{3,2,1,0:T(8,128)S(1)}, f32[2,3,32,128]{3,2,1,0:T(8,128)S(1)}, u32[]{:S(2)}, u32[]{:S(2)}) collective-permute-start(f32[2,3,32,128]{3,2,1,0:T(8,128)S(1)} %get-tuple-element.86), channel_id=1, source_target_pairs={{0,16},{8,24},{16,0},{24,8},{1,17},{9,25},{17,1},{25,9},{2,18},{10... | collective-permute-start | bytes 294920 | tf_op jit(solution)/shard_map/ppermute | solution.py:532
  26.3 1.8 %collective-permute-done.5.refs_5_ = f32[2,40,512]{2,1,0:T(8,128)S(1)} collective-permute-done((f32[2,40,512]{2,1,0:T(8,128)S(1)}, f32[2,40,512]{2,1,0:T(8,128)S(1)}, u32[]{:S(2)}, u32[]{:S(2)}) %collective-permute-start.5) | collective-permute-done | bytes 163872 | tf_op jit(solution)/shard_map/ppermute | solution.py:59
  28.1 0.3 front_3.1
  28.4 1.6 %collective-permute-start.8 = (f32[2,3,32,128]{3,2,1,0:T(8,128)S(1)}, f32[2,3,32,128]{3,2,1,0:T(8,128)S(1)}, u32[]{:S(2)}, u32[]{:S(2)}) collective-permute-start(f32[2,3,32,128]{3,2,1,0:T(8,128)S(1)} %get-tuple-element.88), channel_id=1, source_target_pairs={{0,8},{8,0},{16,24},{24,16},{1,9},{9,1},{17,25},{25,17},{2,10},{10... | collective-permute-start | bytes 294920 | tf_op jit(solution)/shard_map/ppermute | solution.py:532
  30.0 2.6 %collective-permute-start.9 = (f32[2,3,32,128]{3,2,1,0:T(8,128)S(1)}, f32[2,3,32,128]{3,2,1,0:T(8,128)S(1)}, u32[]{:S(2)}, u32[]{:S(2)}) collective-permute-start(f32[2,3,32,128]{3,2,1,0:T(8,128)S(1)} %get-tuple-element.89), channel_id=1, source_target_pairs={{0,16},{8,24},{16,0},{24,8},{1,17},{9,25},{17,1},{25,9},{2,18},{10... | collective-permute-start | bytes 294920 | tf_op jit(solution)/shard_map/ppermute | solution.py:532
  32.6 0.2 collective-permute-start.10
  32.8 0.8 %final_fields.1 = f32[1,2,4,32,512]{4,3,2,1,0:T(8,128)} custom-call(f32[2,32,512]{2,1,0:T(8,128)S(1)} %get-tuple-element.62.refs_0_, f32[2,32,512]{2,1,0:T(8,128)S(1)} %get-tuple-element.74.refs_1_, f32[2,32,512]{2,1,0:T(8,128)S(1)} %get-tuple-element.79.refs_2_, f32[2,32,512]{2,1,0:T(8,128)S(1)} %get-tuple-element.82.refs_3_), custom_call_target="tpu_custom_call" | custom-call | flops 1000000 | bytes 125000 | tf_op jit(solution)/shard_map/final_fields/pallas_call | solution.py:30
  33.7 0.0 collective-permute-done.7.refs_4_
  33.7 0.1 collective-permute-done.8.refs_6_
  33.8 2.8 %collective-permute-done.9.refs_7_ = f32[2,3,32,128]{3,2,1,0:T(8,128)S(1)} collective-permute-done((f32[2,3,32,128]{3,2,1,0:T(8,128)S(1)}, f32[2,3,32,128]{3,2,1,0:T(8,128)S(1)}, u32[]{:S(2)}, u32[]{:S(2)}) %collective-permute-start.9) | collective-permute-done | bytes 98336 | tf_op jit(solution)/shard_map/ppermute | solution.py:532
  36.6 2.4 %collective-permute-done.10.refs_8_ = f32[2,3,32,128]{3,2,1,0:T(8,128)S(1)} collective-permute-done((f32[2,3,32,128]{3,2,1,0:T(8,128)S(1)}, f32[2,3,32,128]{3,2,1,0:T(8,128)S(1)}, u32[]{:S(2)}, u32[]{:S(2)}) %collective-permute-start.10) | collective-permute-done | bytes 98336 | tf_op jit(solution)/shard_map/ppermute | solution.py:532
  39.0 0.7 %combine.1 = (f32[4,32,128]{2,1,0:T(8,128)}, f32[4,32,128]{2,1,0:T(8,128)}, f32[4,32,128]{2,1,0:T(8,128)}) custom-call(f32[4,32,512]{2,1,0:T(8,128)S(1)} %get-tuple-element.49.refs_0_, f32[4,32,512]{2,1,0:T(8,128)S(1)} %get-tuple-element.50.refs_1_, f32[4,32,512]{2,1,0:T(8,128)S(1)} %get-tuple-element.51.refs_2_, ...), custom_call_target="tpu_custom_call" | custom-call | flops 1000000 | bytes 125000 | tf_op jit(solution)/shard_map/combine/pallas_call | solution.py:30
  (2 shorter events, 0.0 us)
Async XLA Ops:
  2.4 5.6 %collective-permute-start = (f32[80,512]{1,0:T(8,128)S(1)}, f32[80,512]{1,0:T(8,128)S(1)}, u32[]{:S(2)}, u32[]{:S(2)}) collective-permute-start(f32[80,512]{1,0:T(8,128)S(1)} %get-tuple-element.57), channel_id=1, source_target_pairs={{0,1},{1,0},{2,3},{3,2},{4,5},{5,4},{6,7},{7,6},{8,9},{9,8},{10,11... | collective-permute-start | bytes 491528 | tf_op jit(solution)/shard_map/ppermute | solution.py:59
  2.5 6.6 %collective-permute-start.1 = (f32[80,512]{1,0:T(8,128)S(1)}, f32[80,512]{1,0:T(8,128)S(1)}, u32[]{:S(2)}, u32[]{:S(2)}) collective-permute-start(f32[80,512]{1,0:T(8,128)S(1)} %get-tuple-element.58), channel_id=1, source_target_pairs={{1,2},{2,1},{5,6},{6,5},{9,10},{10,9},{13,14},{14,13},{17,18},{18,... | collective-permute-start | bytes 491528 | tf_op jit(solution)/shard_map/ppermute | solution.py:59
  4.4 10.8 %collective-permute-start.2 = (f32[2,32,512]{2,1,0:T(8,128)S(1)}, f32[2,32,512]{2,1,0:T(8,128)S(1)}, u32[]{:S(2)}, u32[]{:S(2)}) collective-permute-start(f32[2,32,512]{2,1,0:T(8,128)S(1)} %get-tuple-element.66), channel_id=1, source_target_pairs={{0,4},{4,0},{1,5},{5,1},{2,6},{6,2},{3,7},{7,3},{8,12},{12,8},{9,1... | collective-permute-start | bytes 393224 | tf_op jit(solution)/shard_map/ppermute | solution.py:59
  6.6 5.2 %copy-start.1 = (f32[1,3,1536]{2,0,1:T(1,128)S(1)}, f32[1,3,1536]{2,0,1:T(1,128)}, u32[]{:S(2)}) copy-start(f32[1,3,1536]{2,0,1:T(1,128)} %param.21) | copy-start | bytes 55300
  6.6 5.2 %copy-start = (s32[1,1536]{1,0:T(1,128)S(1)}, s32[1,1536]{1,0:T(1,128)}, u32[]{:S(2)}) copy-start(s32[1,1536]{1,0:T(1,128)} %refs_0_.3) | copy-start | bytes 18436
  9.5 5.7 %collective-permute-start.3 = (f32[2,8,512]{2,1,0:T(8,128)S(1)}, f32[2,8,512]{2,1,0:T(8,128)S(1)}, u32[]{:S(2)}, u32[]{:S(2)}) collective-permute-start(f32[2,8,512]{2,1,0:T(8,128)S(1)} %get-tuple-element.67), channel_id=1, source_target_pairs={{0,4},{4,0},{1,5},{5,1},{2,6},{6,2},{3,7},{7,3},{8,12},{12,8},{9,1... | collective-permute-start | bytes 98312 | tf_op jit(solution)/shard_map/ppermute | solution.py:59
  15.6 6.7 %collective-permute-start.4 = (f32[2,40,512]{2,1,0:T(8,128)S(1)}, f32[2,40,512]{2,1,0:T(8,128)S(1)}, u32[]{:S(2)}, u32[]{:S(2)}) collective-permute-start(f32[2,40,512]{2,1,0:T(8,128)S(1)} %get-tuple-element.68.refs_4_.refs_6_), channel_id=1, source_target_pairs={{0,4},{4,0},{1,5},{5,1},{2,6},{6,2},{3,7},{7,3},{8,12},{12,8},{9,1... | collective-permute-start | bytes 491528 | tf_op jit(solution)/shard_map/ppermute | solution.py:59
  16.8 6.8 %collective-permute-start.6 = (f32[2,2,3,32,128]{4,3,2,1,0:T(8,128)S(1)}, f32[2,2,3,32,128]{4,3,2,1,0:T(8,128)S(1)}, u32[]{:S(2)}, u32[]{:S(2)}) collective-permute-start(f32[2,2,3,32,128]{4,3,2,1,0:T(8,128)S(1)} %get-tuple-element.84), channel_id=1, source_target_pairs={{0,8},{8,0},{16,24},{24,16},{1,9},{9,1},{17,25},{25,17},{2,10},{10... | collective-permute-start | bytes 589832 | tf_op jit(solution)/shard_map/ppermute | solution.py:532
  22.7 5.4 %collective-permute-start.5 = (f32[2,40,512]{2,1,0:T(8,128)S(1)}, f32[2,40,512]{2,1,0:T(8,128)S(1)}, u32[]{:S(2)}, u32[]{:S(2)}) collective-permute-start(f32[2,40,512]{2,1,0:T(8,128)S(1)} %get-tuple-element.78.refs_4_), channel_id=1, source_target_pairs={{0,4},{4,0},{1,5},{5,1},{2,6},{6,2},{3,7},{7,3},{8,12},{12,8},{9,1... | collective-permute-start | bytes 491528 | tf_op jit(solution)/shard_map/ppermute | solution.py:59
  23.6 10.1 %collective-permute-start.7 = (f32[2,3,32,128]{3,2,1,0:T(8,128)S(1)}, f32[2,3,32,128]{3,2,1,0:T(8,128)S(1)}, u32[]{:S(2)}, u32[]{:S(2)}) collective-permute-start(f32[2,3,32,128]{3,2,1,0:T(8,128)S(1)} %get-tuple-element.86), channel_id=1, source_target_pairs={{0,16},{8,24},{16,0},{24,8},{1,17},{9,25},{17,1},{25,9},{2,18},{10... | collective-permute-start | bytes 294920 | tf_op jit(solution)/shard_map/ppermute | solution.py:532
  28.4 5.4 %collective-permute-start.8 = (f32[2,3,32,128]{3,2,1,0:T(8,128)S(1)}, f32[2,3,32,128]{3,2,1,0:T(8,128)S(1)}, u32[]{:S(2)}, u32[]{:S(2)}) collective-permute-start(f32[2,3,32,128]{3,2,1,0:T(8,128)S(1)} %get-tuple-element.88), channel_id=1, source_target_pairs={{0,8},{8,0},{16,24},{24,16},{1,9},{9,1},{17,25},{25,17},{2,10},{10... | collective-permute-start | bytes 294920 | tf_op jit(solution)/shard_map/ppermute | solution.py:532
  30.0 6.6 %collective-permute-start.9 = (f32[2,3,32,128]{3,2,1,0:T(8,128)S(1)}, f32[2,3,32,128]{3,2,1,0:T(8,128)S(1)}, u32[]{:S(2)}, u32[]{:S(2)}) collective-permute-start(f32[2,3,32,128]{3,2,1,0:T(8,128)S(1)} %get-tuple-element.89), channel_id=1, source_target_pairs={{0,16},{8,24},{16,0},{24,8},{1,17},{9,25},{17,1},{25,9},{2,18},{10... | collective-permute-start | bytes 294920 | tf_op jit(solution)/shard_map/ppermute | solution.py:532
  32.6 6.4 %collective-permute-start.10 = (f32[2,3,32,128]{3,2,1,0:T(8,128)S(1)}, f32[2,3,32,128]{3,2,1,0:T(8,128)S(1)}, u32[]{:S(2)}, u32[]{:S(2)}) collective-permute-start(f32[2,3,32,128]{3,2,1,0:T(8,128)S(1)} %get-tuple-element.90), channel_id=1, source_target_pairs={{0,24},{8,16},{16,8},{24,0},{1,25},{9,17},{17,9},{25,1},{2,26},{10... | collective-permute-start | bytes 294920 | tf_op jit(solution)/shard_map/ppermute | solution.py:532

commit v3 on v2

--- a/solution.py
+++ b/solution.py
@@ -59,6 +59,17 @@
     return lax.ppermute(block, axis, pair_swaps(count, first))
 
 
+def swap_rows(tile, block, first):
+    pairs = dict(pair_swaps(tile.gy, first))
+    across = dict(pair_swaps(tile.src, 0))
+    joint = []
+    for s in range(tile.src):
+        for y in range(tile.gy):
+            target = (s, pairs[y]) if y in pairs else (across.get(s, s), y)
+            joint.append((s * tile.gy + y, target[0] * tile.gy + target[1]))
+    return lax.ppermute(block, ("src", "gy"), joint)
+
+
 def lanes_of(j):
     return pl.ds(j * LANES, LANES)
 
@@ -75,6 +86,17 @@
         self.rows = self.ny + 2 * HALO
         self.gx, self.gy, self.src = mesh.shape["gx"], mesh.shape["gy"], mesh.shape["src"]
         self.far = self.gx > 2
+        self.plan, self.second = self.reduction()
+
+    def reduction(self):
+        last = self.steps - 1
+        ready = [self.phase(last, m) for m in range(self.nx)]
+        if self.src == 4 and ready == [0, 1, 2, 3]:
+            return {(0, 1): (1, "a"), (2,): (2, "b"), (3,): (3, None)}, {"a": 2, "b": 3}
+        pieces = {}
+        for m, phase in enumerate(ready):
+            pieces.setdefault(phase, []).append(m)
+        return {tuple(planes): (phase, None) for phase, planes in pieces.items()}, {}
 
     def place(self, m):
         return m + is_odd("gx") * (self.nx - 1 - 2 * m)
@@ -86,85 +108,64 @@
             return 0
         return max(self.phase(t - 1, k) for k in (m - 1, m, m + 1))
 
+    def edge(self, m):
+        return m == self.nx - 1 or (m == 0 and self.far)
+
 
 def rolled(value, by, axis):
     return pltpu.roll(value, by % value.shape[axis], axis)
 
 
-UNITS = (
-    [("now", c, 0, 2) for c in range(2)]
-    + [("before", c, 0, 2) for c in range(2)]
-    + [(key, 0, 0, 2) for key in ("velocity", "eps", "delta", "tilt", "azimuth")]
-    + [("now", 0, 2, 1), ("now", 1, 2, 1)]
-)
 ITEMS = [("now", 0), ("now", 1), ("before", 0), ("before", 1)] + [
     (key, 0) for key in ("velocity", "eps", "delta", "tilt", "azimuth")
 ]
 
 
-def edge_rows():
-    placed, at = [], 0
-    for key, c, first, count in UNITS:
-        placed.append((key, c, first, count, at))
-        at += count
-    return placed, at
+def edge_rows(tile):
+    placed = [
+        (item, m, 0, 2, 2 * (item * tile.nx + m)) for item in range(len(ITEMS)) for m in range(tile.nx)
+    ]
+    base = 2 * len(ITEMS) * tile.nx
+    placed += [(item, m, 2, 1, base + item * tile.nx + m) for item in range(2) for m in range(tile.nx)]
+    return placed, base + 2 * tile.nx
 
 
 def pack_edges(tile, raw):
-    placed, per_plane = edge_rows()
-    total = per_plane * tile.nx
-    assert total % 8 == 0
+    placed, total = edge_rows(tile)
+    assert tile.nx % 4 == 0
     outs = {"even": (total, tile.nz), "odd": (total, tile.nz), "near": (2, tile.ny, tile.nz)}
     if tile.far:
         outs["far"] = outs["near"]
     outs.update({key: (value.shape, value.dtype) for key, value in raw.items()})
 
     def body(r):
-        copies = []
+        copies = {}
         for i, key in enumerate(raw):
-            copies.append(pltpu.make_async_copy(r[key + "_hbm"], r[key], r["done"].at[i]))
-            copies[-1].start()
-        for copy in copies:
-            copy.wait()
-        for c in range(2):
-            r["near"][c] = r["now"][0, c, tile.place(tile.nx - 1)]
-            if tile.far:
-                r["far"][c] = r["now"][0, c, tile.place(0)]
-
+            copies[key] = pltpu.make_async_copy(r[key + "_hbm"], r[key], r["done"].at[i])
+            copies[key].start()
         odd = is_odd("gy") == 1
         sub = lax.broadcasted_iota(jnp.int32, (8, tile.nz), 0)
-
-        def rows_of(key, c, m, end):
-            here = tile.place(m)
-            rows = pl.ds(tile.ny - 8 if end == "_top" else 0, 8)
+        blocks = {}
+        for item, m, first, count, place in placed:
+            key, c = ITEMS[item]
+            if key in copies:
+                copies.pop(key).wait()
+                if key == "now":
+                    for part in range(2):
+                        r["near"][part] = r["now"][0, part, tile.place(tile.nx - 1)]
+                        if tile.far:
+                            r["far"][part] = r["now"][0, part, tile.place(0)]
+            here, slot = tile.place(m), place % 8
             ref = r[key].at[0, c] if key in ("now", "before") else r[key]
-            return ref[here, rows, :].astype(F32)
-
-        for end in ("_top", "_low"):
-            blocks = [None] * (total // 8)
-            for m in range(tile.nx):
-                for key, c, first, count, at in placed:
-                    place = at + m * per_plane
-                    while count:
-                        slot, some = place % 8, min(count, 8 - place % 8)
-                        from_row = first if end == "_low" else 8 - first - some
-                        if end == "_top" and some < count:
-                            from_row = 8 - first - count
-                        block = rows_of(key, c, m, end)
-                        moved = rolled(block, slot - from_row, 0) if slot != from_row else block
-                        old = blocks[place // 8]
-                        blocks[place // 8] = (
-                            moved if old is None else jnp.where(sub >= slot, moved, old)
-                        )
-                        place, count, first = place + some, count - some, first + some
-            for i, block in enumerate(blocks):
-                rows = pl.ds(8 * i, 8)
-                if end == "_top":
-                    r["even"][rows, :] = block
-                    r["odd"][rows, :] = block
-                else:
-                    r["even"][rows, :] = jnp.where(odd, block, r["even"][rows, :])
-                    r["odd"][rows, :] = jnp.where(odd, r["odd"][rows, :], block)
+            for end, start, from_row in (("top", tile.ny - 8, 8 - first - count), ("low", 0, first)):
+                block = ref[here, pl.ds(start, 8), :].astype(F32)
+                moved = rolled(block, slot - from_row, 0) if slot != from_row else block
+                old = blocks.get(end)
+                blocks[end] = moved if slot == 0 else jnp.where(sub >= slot, moved, old)
+            if slot + count == 8:
+                rows = pl.ds(place - slot, 8)
+                r["even"][rows, :] = jnp.where(odd, blocks["low"], blocks["top"])
+                r["odd"][rows, :] = jnp.where(odd, blocks["top"], blocks["low"])
 
     ins = {key + "_hbm": value for key, value in raw.items()}
     spaces = {key: pltpu.HBM for key in ins}
@@ -173,17 +174,16 @@
     )
 
 
-def halo_block(tile, r, key, c, m):
-    placed, per_plane = edge_rows()
+def halo_block(tile, r, item, m):
     odd = is_odd("gy") == 1
+    has_upper = lax.axis_index("gy") < tile.gy - 1
+    has_lower = lax.axis_index("gy") > 0
     sub = lax.broadcasted_iota(jnp.int32, (8, tile.nz), 0)
     result = jnp.zeros((8, tile.nz), F32)
-    for name, part, first, count, at in placed:
-        if (name, part) != (key, c):
+    for i, plane, first, count, place in edge_rows(tile)[0]:
+        if (i, plane) != (item, m):
             continue
-        place = at + m * per_plane
         slot = place % 8
-        assert slot + count <= 8
         rows = pl.ds(place - slot, 8)
         even_got, odd_got = r["got_even"][rows, :], r["got_odd"][rows, :]
         upper = jnp.where(odd, odd_got, even_got)
@@ -191,8 +191,8 @@
         upper = rolled(upper, first - slot, 0) if slot != first else upper
         bottom = 8 - first - count
         lower = rolled(lower, bottom - slot, 0) if slot != bottom else lower
-        result = jnp.where((sub >= first) & (sub < first + count), upper, result)
-        result = jnp.where((sub >= bottom) & (sub < bottom + count), lower, result)
+        result = jnp.where((sub >= first) & (sub < first + count) & has_upper, upper, result)
+        result = jnp.where((sub >= bottom) & (sub < bottom + count) & has_lower, lower, result)
     return result
 
 
@@ -201,33 +201,25 @@
     theta = level * (0.5 * math.pi / LEVELS)
     azimuth = level * (2.0 * math.pi / LEVELS)
     sin_t, cos_t, sin_p, cos_p = jnp.sin(theta), jnp.cos(theta), jnp.sin(azimuth), jnp.cos(azimuth)
-    return (
-        sin_t * sin_t,
-        0.5 * sin_t * cos_t,
-        cos_t * cos_t,
-        cos_p * cos_p,
-        sin_p * sin_p,
-        0.5 * sin_p * cos_p,
-        sin_p,
-        cos_p,
-    )
+    return sin_t, cos_t, sin_p, cos_p
 
 
 def store_weights(out, m, rows, j, tables, sign, velocity, eps, delta, tilt, azimuth):
     def look(table, level):
         return jnp.take_along_axis(table, level, axis=1)
 
-    sin2_t, sincos_t, cos2_t = (look(tables[k], tilt) for k in range(3))
-    cos2_p, sin2_p, sincos_p, sin_p, cos_p = (look(tables[k], azimuth) for k in range(3, 8))
+    sin_t, cos_t = look(tables[0], tilt), look(tables[1], tilt)
+    sin_p, cos_p = look(tables[2], azimuth), look(tables[3], azimuth)
+    sin2_t, half_t = sin_t * sin_t, 0.5 * sin_t * cos_t
     speed_sq = velocity * velocity
     root = jnp.sqrt(1.0 + 2.0 * delta)
     values = (
-        sin2_t * cos2_p,
-        sin2_t * sin2_p,
-        cos2_t,
-        sign * (sin2_t * sincos_p),
-        sincos_t * sin_p,
-        sign * (sincos_t * cos_p),
+        sin2_t * (cos_p * cos_p),
+        sin2_t * (sin_p * sin_p),
+        cos_t * cos_t,
+        (0.5 * sign) * (sin2_t * (sin_p * cos_p)),
+        half_t * sin_p,
+        sign * (half_t * cos_p),
         speed_sq * (1.0 + 2.0 * eps),
         speed_sq * root,
         speed_sq,
@@ -281,7 +273,7 @@
         start_y = lax.axis_index("gy") * tile.ny
         cell_here = r["cell"][...]
         slots = lax.broadcasted_iota(jnp.int32, (1, channels), 1)
-        live = slots < r["count"][0]
+        live = slots < r["count"][...].reshape(1, 1)
         if width & (width - 1) == 0:
             row_of = cell_here & (width - 1)
         else:
@@ -290,25 +282,35 @@
         place = jnp.where(place >= tile.ny + HALO, place - tile.rows, place) + start_y
         onehot = jnp.where(row_of == place, 1.0, 0.0)
         first = lax.broadcasted_iota(jnp.int32, (tile.rows, LANES), 1) == 0
-        pad = jnp.zeros((LANES - tile.steps, channels), F32)
+        pad = jnp.zeros((8 - tile.steps, channels), F32)
         trace_here = r["trace"][0]
+        loads = []
         for m in range(tile.nx):
             low = (start_x + tile.place(m)) * width
             inside = live & (cell_here >= low) & (cell_here < low + width)
-            load = jnp.concatenate([jnp.where(inside, trace_here, 0.0), pad], axis=0)
-            columns = lax.dot_general(
-                onehot, load, (((1,), (1,)), ((), ())),
-                precision=lax.Precision.HIGHEST, preferred_element_type=F32,
-            )
+            loads += [jnp.where(inside, trace_here, 0.0), pad]
+        rest, parts = jnp.concatenate(loads, axis=0), []
+        for _ in range(3):
+            part = rest.astype(jnp.bfloat16)
+            rest = rest - part.astype(F32)
+            parts.append(part.astype(F32))
+        group = 8 * tile.nx
+        if 3 * group < LANES:
+            parts.append(jnp.zeros((LANES - 3 * group, channels), F32))
+        columns = lax.dot_general(
+            onehot.astype(jnp.bfloat16), jnp.concatenate(parts, axis=0).astype(jnp.bfloat16),
+            (((1,), (1,)), ((), ())), preferred_element_type=F32,
+        )
+        columns = columns + (rolled(columns, -group, 1) + rolled(columns, -2 * group, 1))
+        for m in range(tile.nx):
             for t in range(tile.steps):
-                column = columns if t == 0 else rolled(columns, -t, 1)
+                column = rolled(columns, -8 * m - t, 1) if m + t else columns
                 r["surface"][t, m] = jnp.where(first, column, 0.0)
 
+    assert tile.steps <= 8 and 24 * tile.nx <= LANES
     ins = {"cell": cell, "count": count, "trace": trace, "after": after}
     outs = {"surface": (tile.steps, tile.nx, tile.rows, LANES)}
-    out = run_kernel(
-        body, ins, outs, spaces={"count": pltpu.SMEM}, name="surface_load", flops=2 * 10**6
-    )
+    out = run_kernel(body, ins, outs, name="surface_load", flops=2 * 10**6)
     return out["surface"]
 
 
@@ -321,14 +323,14 @@
         tables = angle_tables(8)
         sign = x_sign()
         for m in range(tile.nx):
-            for item, (key, c) in enumerate(ITEMS[:4]):
-                block = halo_block(tile, r, key, c, m)
+            for item in range(4):
+                block = halo_block(tile, r, item, m)
                 r["uh"][item, m] = block
                 if item < 2 and m == tile.nx - 1:
-                    r["near"][c] = block
+                    r["near"][item] = block
                 if item < 2 and m == 0 and tile.far:
-                    r["far"][c] = block
-            coefs = [halo_block(tile, r, key, c, m) for key, c in ITEMS[4:]]
+                    r["far"][item] = block
+            coefs = [halo_block(tile, r, item, m) for item in range(4, 9)]
             for j in range(tile.nj):
                 part = [value[:, j * LANES : (j + 1) * LANES] for value in coefs]
                 store_weights(
@@ -382,6 +384,8 @@
                 self.need(("g", t - 1, m))
             rows = tile.ny if last else tile.rows
             self.outs[("u", t + 1, m)] = (2, rows, tile.nz)
+            if not last and tile.edge(m):
+                self.outs[("e", t + 1, m)] = (2 * tile.ny + 8, tile.nz)
             total = (tile.nj, 3, tile.ny, LANES)
             if last and any(m in planes for planes in self.pieces):
                 self.scratch[("g", t, m)] = pltpu.VMEM(total, F32)
@@ -421,7 +425,7 @@
                         ]
 
     def halved(self, planes):
-        return self.tile.src == 4 and self.tile.nx - 1 not in planes
+        return self.tile.plan[planes][1] is not None
 
     def field(self, r, t, m, c, j):
         tile, lanes = self.tile, lanes_of(j)
@@ -429,8 +433,15 @@
             return None
         if m in (-1, tile.nx):
             key = "xf" if m == -1 else "xn"
-            block = r[(key, t)][c, :, lanes]
-            return jnp.concatenate([block, r[(key + "h", t)][c, :, lanes]], axis=0) if t == 0 else block
+            if t == 0:
+                own, halo = r[(key, t)][c, :, lanes], r[(key + "h", t)][c, :, lanes]
+            else:
+                own = r[(key, t)][pl.ds(c * tile.ny, tile.ny), lanes]
+                halo = r[(key, t)][pl.ds(2 * tile.ny, 8), lanes]
+                if c == 1:
+                    sub = lax.broadcasted_iota(jnp.int32, (8, LANES), 0)
+                    halo = jnp.where(sub < HALO, rolled(halo, -2, 0), rolled(halo, 2, 0))
+            return jnp.concatenate([own, halo], axis=0)
         if t > 0:
             return r[("u", t, m)][c, :, lanes]
         ref, item = (r["now"], c) if t == 0 else (r["before"], 2 + c)
@@ -513,6 +524,14 @@
                 new_p = new_p + r["surface"][t, m][:rows]
             r[("u", t + 1, m)][0, :, lanes_of(j)] = new_p
             r[("u", t + 1, m)][1, :, lanes_of(j)] = new_q
+            if ("e", t + 1, m) in r:
+                edge, lanes = r[("e", t + 1, m)], lanes_of(j)
+                edge[: tile.ny, lanes] = new_p[: tile.ny]
+                edge[tile.ny : 2 * tile.ny, lanes] = new_q[: tile.ny]
+                sub = lax.broadcasted_iota(jnp.int32, (8, LANES), 0)
+                p_rows, q_rows = new_p[tile.ny :], new_q[tile.ny :]
+                q_rows = jnp.where(sub < HALO, rolled(q_rows, 2, 0), rolled(q_rows, -2, 0))
+                edge[2 * tile.ny :, lanes] = jnp.where((sub < 2) | (sub >= 6), p_rows, q_rows)
             here = tile.place(m)
             forward_p = r["forward"][t, 0, 0, here, :, lanes_of(j)].astype(F32)
             forward_q = r["forward"][t, 0, 1, here, :, lanes_of(j)].astype(F32)
@@ -532,28 +551,39 @@
     return lax.ppermute(block, "src", [(i, i ^ k) for i in range(tile.src)])
 
 
-def add_halves(keep, got):
-    block = keep.shape[1:]
+def add_halves(tile, state, pieces, after):
+    ins, outs, count = {"after": after}, {}, 0
+    for planes in pieces:
+        ins[("keep", planes)], ins[("got", planes)] = state[("keep", planes)], state[("got", planes)]
+        outs[("s", planes, 0)] = state[("keep", planes)].shape[1:]
+        count += len(planes)
+    outs["passed"] = (count, *outs[("s", pieces[0], 0)][1:])
 
     def body(r):
-        r["own"][...] = r["keep"][0] + r["got"][0]
-        r["passed"][...] = r["keep"][1] + r["got"][1]
-
-    out = run_kernel(
-        body, {"keep": keep, "got": got}, {"own": block, "passed": block}, name="add_halves",
-        flops=10**5,
-    )
-    return out["own"], out["passed"]
+        at = 0
+        for planes in pieces:
+            keep, got = r[("keep", planes)], r[("got", planes)]
+            r[("s", planes, 0)][...] = keep[0] + got[0]
+            r["passed"][at : at + len(planes)] = keep[1] + got[1]
+            at += len(planes)
+
+    state.update(run_kernel(body, ins, outs, name="add_halves", flops=10**5))
+    passed = xor_swap(tile, state["passed"], 2)
+    at = 0
+    for planes in pieces:
+        state[("r", planes, 2)] = (passed, at)
+        at += len(planes)
 
 
 def combine(tile, state, pieces):
     depth = tile.nz // tile.src
     ins = {key: state[key] for key in ("velocity", "eps", "delta")}
+    starts = {}
     for planes in pieces:
         ins[("s", planes, 0)] = state[("s", planes, 0)]
         for k in range(1, tile.src):
             if ("r", planes, k) in state:
-                ins[("r", planes, k)] = state[("r", planes, k)]
+                ins[("r", planes, k)], starts[(planes, k)] = state[("r", planes, k)]
     shape = (tile.nx, tile.ny, depth)
 
     def body(r):
@@ -565,8 +595,8 @@
                 for item in range(3):
                     total = r[("s", planes, 0)][i, item]
                     for k in range(1, tile.src):
-                        if ("r", planes, k) in r:
-                            total = total + r[("r", planes, k)][i, item]
+                        if (planes, k) in starts:
+                            total = total + r[("r", planes, k)][starts[(planes, k)] + i, item]
                     sums.append(total)
                 velocity = r["velocity"][here, :, lanes]
                 root = jnp.sqrt(1.0 + 2.0 * r["delta"][here, :, lanes])
@@ -627,49 +657,44 @@
         if tile.far:
             state[("xf" + key, t)] = swap(far, "gx", tile.gx, 1)
 
+    got_even = swap_rows(tile, edges["even"], 0)
     exchange("", 0, edges["near"], edges.get("far"))
-    got_odd = swap(edges["odd"], "gy", tile.gy, 1)
-    got_even = swap(edges["even"], "gy", tile.gy, 0)
+    got_odd = swap_rows(tile, edges["odd"], 1)
     state.update(own_state(tile, state, forward_field))
-    halo = halo_state(tile, got_even, got_odd, state["w"])
+    state["surface"] = surface_load(
+        tile, channel_cell, channel_count, residual_trace, state["w"]
+    )
+    halo = halo_state(tile, got_even, got_odd, state["surface"])
     state["uh"], state["wh"] = halo["uh"], halo["wh"]
     exchange("h", 0, halo["near"], halo.get("far"))
-    state["surface"] = surface_load(
-        tile, channel_cell, channel_count, residual_trace, halo["uh"]
-    )
 
     ops = [(t, m) for t in range(tile.steps) for m in range(tile.nx)]
-    last = tile.steps - 1
-    ready = {m: tile.phase(last, m) for m in range(tile.nx)}
-    issue = {}
-    for m in range(tile.nx):
-        issue.setdefault(1 if ready[m] <= 1 else tile.steps, []).append(m)
-    pieces = []
-    edge = {tile.nx - 1} | ({0} if tile.far else set())
+    pieces = list(tile.plan)
     for phase in range(tile.steps + 1):
-        mine = [op for op in ops if tile.phase(*op) == phase]
-        after = state.get("token")
-        front = [op for op in mine if phase > 0 and op[0] == phase - 1 and op[1] in edge]
+        mine = [op for op in ops if max(tile.phase(*op), op[0] // 2) == phase]
+        front = [op for op in mine if phase > 0 and op[0] == phase - 1 and tile.edge(op[1])]
         bulk = [op for op in mine if op not in front]
-        done = [tuple(issue[phase])] if phase in issue else []
-        pieces += done
+        done = [planes for planes in pieces if tile.plan[planes][0] == phase]
         if phase == tile.steps:
             front, bulk = mine, []
         if front:
-            Stage(tile, state, front, [] if bulk else done, f"front_{phase}", after).run()
+            Stage(tile, state, front, [] if bulk else done, f"front_{phase}", state.get("token")).run()
+            state["token"] = state[("u", phase, tile.nx - 1)]
             if phase < tile.steps:
-                exchange("", phase, state[("u", phase, tile.nx - 1)], state.get(("u", phase, 0)))
+                exchange("", phase, state[("e", phase, tile.nx - 1)], state.get(("e", phase, 0)))
         if bulk:
             Stage(tile, state, bulk, done, f"bulk_{phase}").run()
-            state["token"] = state[("g", *next(op for op in bulk if ("g", *op) in state))]
+            state["token"] = state[("u", bulk[0][0] + 1, bulk[0][1])]
         for planes in done:
             if ("send", planes) in state:
-                got = xor_swap(tile, state[("send", planes)], 1)
-                state[("s", planes, 0)], passed = add_halves(state[("keep", planes)], got)
-                state[("r", planes, 2)] = xor_swap(tile, passed, 2)
-            else:
-                for k in range(1, tile.src):
-                    state[("r", planes, k)] = xor_swap(tile, state[("s", planes, k)], k)
+                state[("got", planes)] = xor_swap(tile, state[("send", planes)], 1)
+                continue
+            for k in range(1, tile.src):
+                state[("r", planes, k)] = (xor_swap(tile, state[("s", planes, k)], k), 0)
+        for name, when in tile.second.items():
+            if when == phase:
+                carried = [planes for planes in pieces if tile.plan[planes][1] == name]
+                add_halves(tile, state, carried, state["token"])
     following = final_fields(tile, state)
     return (following, *combine(tile, state, pieces))
 

time: 39.9 us -> 37.4 us (0.937)
  the two profiles are of different devices: /device:TPU:2 before, /device:TPU:0 now
where the time goes in v3:
time: 37.4 us; the launch traced here: 37.2 us
  starting transfers between devices  20.3 us (54%)
  Pallas kernels  9.64 us (26%)
  waiting for transfers between devices  5.83 us (16%)
  between operations  1.43 us (4%)
    ppermute x7, starting transfers between devices, xor_swap(): return lax.ppermute(block, 'src', [(i, i ^ k) for i in range(tile.src)])  11.4 us
    pallas_call x14, Pallas kernels, run_kernel(): pl.pallas_call(kernel, name=name, out_shape=[jax.ShapeDtypeStruct(shape,...  9.64 us
    ppermute x4, starting transfers between devices, swap(): return lax.ppermute(block, axis, pair_swaps(count, first))  5.69 us
    ppermute x7, waiting for transfers between devices, xor_swap(): return lax.ppermute(block, 'src', [(i, i ^ k) for i in range(tile.src)])  4.1 us
    ppermute x2, starting transfers between devices, swap_rows(): return lax.ppermute(block, ('src', 'gy'), joint)  3.17 us
    ppermute x4, waiting for transfers between devices, swap(): return lax.ppermute(block, axis, pair_swaps(count, first))  1.72 us
  transfers between devices with their start and end apart: 13, of which 5 were waited for; matrix products, arithmetic and copies ran while one was open for 0% of the time, Pallas kernels for 19%

profile of v3, /device:TPU:0, one launch (start us, length us, event | category | flops | bytes accessed | tf_op | source)
XLA Modules:
  0.0 37.2 jit_solution(13085926101655389164)
XLA Ops:
  0.6 0.0 copy-start.1
  0.6 0.0 copy-start
  0.7 1.7 %pack_edges.1 = (f32[80,512]{1,0:T(8,128)S(1)}, f32[80,512]{1,0:T(8,128)S(1)}, f32[2,32,512]{2,1,0:T(8,128)S(1)}, f32[1,2,4,32,512]{4,3,2,1,0:T(8,128)S(1)}, f32...) custom-call(f32[1,2,4,32,512]{4,3,2,1,0:T(8,128)} %refs_0_.2, ...), custom_call_target="tpu_custom_call" | custom-call | flops 1000000 | bytes 125000 | tf_op jit(solution)/shard_map/pack_edges/pallas_call | solution.py:30
  2.3 0.5 %collective-permute-start = (f32[80,512]{1,0:T(8,128)S(1)}, f32[80,512]{1,0:T(8,128)S(1)}, u32[]{:S(2)}, u32[]{:S(2)}) collective-permute-start(f32[80,512]{1,0:T(8,128)S(1)} %get-tuple-element.62), channel_id=1, source_target_pairs={{0,1},{1,0},{2,3},{3,2},{8,9},{9,8},{10,11},{11,10},{16,17},{17,16... | collective-permute-start | bytes 491528 | tf_op jit(solution)/shard_map/ppermute | solution.py:70
  2.9 2.6 %collective-permute-start.1 = (f32[80,512]{1,0:T(8,128)S(1)}, f32[80,512]{1,0:T(8,128)S(1)}, u32[]{:S(2)}, u32[]{:S(2)}) collective-permute-start(f32[80,512]{1,0:T(8,128)S(1)} %get-tuple-element.63), channel_id=1, source_target_pairs={{0,8},{1,2},{2,1},{3,11},{8,0},{9,10},{10,9},{11,3},{16,24},{17,18... | collective-permute-start | bytes 491528 | tf_op jit(solution)/shard_map/ppermute | solution.py:70
  5.5 1.5 %collective-permute-start.2 = (f32[2,32,512]{2,1,0:T(8,128)S(1)}, f32[2,32,512]{2,1,0:T(8,128)S(1)}, u32[]{:S(2)}, u32[]{:S(2)}) collective-permute-start(f32[2,32,512]{2,1,0:T(8,128)S(1)} %get-tuple-element.70), channel_id=1, source_target_pairs={{0,4},{4,0},{1,5},{5,1},{2,6},{6,2},{3,7},{7,3},{8,12},{12,8},{9,1... | collective-permute-start | bytes 393224 | tf_op jit(solution)/shard_map/ppermute | solution.py:59
  7.7 0.0 copy-done.1
  7.7 1.1 %own_state.1 = (f32[9,4,32,512]{3,2,1,0:T(8,128)S(1)}, bf16[3,1,2,4,32,512]{5,4,3,2,1,0:T(8,128)(2,1)S(1)}) custom-call(f32[4,32,512]{2,1,0:T(8,128)S(1)} %get-tuple-element.54.refs_0_, f32[4,32,512]{2,1,0:T(8,128)S(1)} %get-tuple-element.55.refs_1_, f32[4,32,512]{2,1,0:T(8,128)S(1)} %get-tuple-element.56.refs_2_, ...), custom_call_target="tpu_custom_call" | custom-call | flops 3000000 | bytes 375000 | tf_op jit(solution)/shard_map/own_state/pallas_call | solution.py:30
  8.9 0.0 copy-done
  8.9 0.5 %surface_load.1.refs_2_.refs_6_.refs_9_.refs_8_.refs_7_ = f32[3,4,40,128]{3,2,1,0:T(8,128)S(1)} custom-call(s32[1,1536]{1,0:T(1,128)S(1)} %copy-done, s32[1]{0:T(128)S(6)} %copy.16.refs_1_, f32[1,3,1536]{2,1,0:T(4,128)S(1)} %copy.15.refs_2_, f32[9,4,32,512]{3,2,1,0:T(8,128)S(1)} %get-tuple-element.59.refs_3_.refs_0_.refs_1_), custom_call_target="tpu_custom_call" | custom-call | flops 2000000 | bytes 250000 | tf_op jit(solution)/shard_map/surface_load/pallas_call | solution.py:30
  9.4 0.0 collective-permute-done.refs_0_
  9.4 0.0 collective-permute-done.1.refs_1_
  9.4 0.3 halo_state.1
  9.7 1.4 %collective-permute-start.3 = (f32[2,8,512]{2,1,0:T(8,128)S(1)}, f32[2,8,512]{2,1,0:T(8,128)S(1)}, u32[]{:S(2)}, u32[]{:S(2)}) collective-permute-start(f32[2,8,512]{2,1,0:T(8,128)S(1)} %get-tuple-element.71), channel_id=1, source_target_pairs={{0,4},{4,0},{1,5},{5,1},{2,6},{6,2},{3,7},{7,3},{8,12},{12,8},{9,1... | collective-permute-start | bytes 98312 | tf_op jit(solution)/shard_map/ppermute | solution.py:59
  11.2 2.2 %bulk_0.1 = (f32[2,40,512]{2,1,0:T(8,128)S(1)}, f32[4,3,32,128]{3,2,1,0:T(8,128)}, f32[2,40,512]{2,1,0:T(8,128)S(1)}, f32[4,3,32,128]{3,2,1,0:T(8,128)}, f32[2,4...) custom-call(f32[9,4,32,512]{3,2,1,0:T(8,128)S(1)} %get-tuple-element, ...), custom_call_target="tpu_custom_call" | custom-call | flops 10100000 | bytes 1262500 | tf_op jit(solution)/shard_map/bulk_0/pallas_call | solution.py:30
  13.4 0.0 collective-permute-done.2.refs_5_
  13.4 0.3 collective-permute-done.3.refs_6_
  13.7 0.3 front_1.1
  14.1 1.4 %collective-permute-start.4 = (f32[72,512]{1,0:T(8,128)S(1)}, f32[72,512]{1,0:T(8,128)S(1)}, u32[]{:S(2)}, u32[]{:S(2)}) collective-permute-start(f32[72,512]{1,0:T(8,128)S(1)} %get-tuple-element.81), channel_id=1, source_target_pairs={{0,4},{4,0},{1,5},{5,1},{2,6},{6,2},{3,7},{7,3},{8,12},{12,8},{9,1... | collective-permute-start | bytes 442376 | tf_op jit(solution)/shard_map/ppermute | solution.py:59
  15.5 0.9 %bulk_1.1 = (f32[2,40,512]{2,1,0:T(8,128)S(1)}, f32[4,3,32,128]{3,2,1,0:T(8,128)S(1)}, f32[2,32,512]{2,1,0:T(8,128)S(1)}, f32[2,32,512]{2,1,0:T(8,128)S(1)}, f32...) custom-call(f32[9,4,32,512]{3,2,1,0:T(8,128)S(1)} %get-tuple-element.59.refs_3_.refs_0_.refs_1_, ...), custom_call_target="tpu_custom_call" | custom-call | flops 6100000 | bytes 762500 | tf_op jit(solution)/shard_map/bulk_1/pallas_call | solution.py:30
  16.4 1.6 %collective-permute-start.6 = (f32[2,2,3,32,128]{4,3,2,1,0:T(8,128)S(1)}, f32[2,2,3,32,128]{4,3,2,1,0:T(8,128)S(1)}, u32[]{:S(2)}, u32[]{:S(2)}) collective-permute-start(f32[2,2,3,32,128]{4,3,2,1,0:T(8,128)S(1)} %get-tuple-element.90), channel_id=1, source_target_pairs={{0,8},{8,0},{16,24},{24,16},{1,9},{9,1},{17,25},{25,17},{2,10},{10... | collective-permute-start | bytes 589832 | tf_op jit(solution)/shard_map/ppermute | solution.py:551
  18.0 1.4 %collective-permute-done.4.refs_5_ = f32[72,512]{1,0:T(8,128)S(1)} collective-permute-done((f32[72,512]{1,0:T(8,128)S(1)}, f32[72,512]{1,0:T(8,128)S(1)}, u32[]{:S(2)}, u32[]{:S(2)}) %collective-permute-start.4) | collective-permute-done | bytes 147488 | tf_op jit(solution)/shard_map/ppermute | solution.py:59
  19.4 0.3 front_2.1
  19.7 1.3 %collective-permute-start.5 = (f32[72,512]{1,0:T(8,128)S(1)}, f32[72,512]{1,0:T(8,128)S(1)}, u32[]{:S(2)}, u32[]{:S(2)}) collective-permute-start(f32[72,512]{1,0:T(8,128)S(1)} %get-tuple-element.86), channel_id=1, source_target_pairs={{0,4},{4,0},{1,5},{5,1},{2,6},{6,2},{3,7},{7,3},{8,12},{12,8},{9,1... | collective-permute-start | bytes 442376 | tf_op jit(solution)/shard_map/ppermute | solution.py:59
  21.0 0.3 bulk_2.1
  21.4 1.6 %collective-permute-start.8 = (f32[2,1,3,32,128]{4,3,2,1,0:T(8,128)S(1)}, f32[2,1,3,32,128]{4,3,2,1,0:T(8,128)S(1)}, u32[]{:S(2)}, u32[]{:S(2)}) collective-permute-start(f32[2,1,3,32,128]{4,3,2,1,0:T(8,128)S(1)} %get-tuple-element.94), channel_id=1, source_target_pairs={{0,8},{8,0},{16,24},{24,16},{1,9},{9,1},{17,25},{25,17},{2,10},{10... | collective-permute-start | bytes 294920 | tf_op jit(solution)/shard_map/ppermute | solution.py:551
  23.0 0.0 collective-permute-done.6.refs_2_
  23.0 2.7 %collective-permute-start.7 = (f32[2,3,32,128]{3,2,1,0:T(8,128)S(1)}, f32[2,3,32,128]{3,2,1,0:T(8,128)S(1)}, u32[]{:S(2)}, u32[]{:S(2)}) collective-permute-start(f32[2,3,32,128]{3,2,1,0:T(8,128)S(1)} %get-tuple-element.92), channel_id=1, source_target_pairs={{0,16},{8,24},{16,0},{24,8},{1,17},{9,25},{17,1},{25,9},{2,18},{10... | collective-permute-start | bytes 294920 | tf_op jit(solution)/shard_map/ppermute | solution.py:551
  25.7 0.0 collective-permute-done.5.refs_5_
  25.7 0.3 front_3.1
  26.0 1.3 %collective-permute-start.10 = (f32[1,3,32,128]{3,2,1,0:T(8,128)S(1)}, f32[1,3,32,128]{3,2,1,0:T(8,128)S(1)}, u32[]{:S(2)}, u32[]{:S(2)}) collective-permute-start(f32[1,3,32,128]{3,2,1,0:T(8,128)S(1)} %get-tuple-element.98), channel_id=1, source_target_pairs={{0,8},{8,0},{16,24},{24,16},{1,9},{9,1},{17,25},{25,17},{2,10},{10... | collective-permute-start | bytes 147464 | tf_op jit(solution)/shard_map/ppermute | solution.py:551
  27.3 2.2 %collective-permute-start.11 = (f32[1,3,32,128]{3,2,1,0:T(8,128)S(1)}, f32[1,3,32,128]{3,2,1,0:T(8,128)S(1)}, u32[]{:S(2)}, u32[]{:S(2)}) collective-permute-start(f32[1,3,32,128]{3,2,1,0:T(8,128)S(1)} %get-tuple-element.99), channel_id=1, source_target_pairs={{0,16},{8,24},{16,0},{24,8},{1,17},{9,25},{17,1},{25,9},{2,18},{10... | collective-permute-start | bytes 147464 | tf_op jit(solution)/shard_map/ppermute | solution.py:551
  29.5 1.0 %collective-permute-start.12 = (f32[1,3,32,128]{3,2,1,0:T(8,128)S(1)}, f32[1,3,32,128]{3,2,1,0:T(8,128)S(1)}, u32[]{:S(2)}, u32[]{:S(2)}) collective-permute-start(f32[1,3,32,128]{3,2,1,0:T(8,128)S(1)} %get-tuple-element.100), channel_id=1, source_target_pairs={{0,24},{8,16},{16,8},{24,0},{1,25},{9,17},{17,9},{25,1},{2,26},{10... | collective-permute-start | bytes 147464 | tf_op jit(solution)/shard_map/ppermute | solution.py:551
  30.5 0.0 collective-permute-done.8.refs_2_
  30.5 1.0 %collective-permute-start.9 = (f32[1,3,32,128]{3,2,1,0:T(8,128)S(1)}, f32[1,3,32,128]{3,2,1,0:T(8,128)S(1)}, u32[]{:S(2)}, u32[]{:S(2)}) collective-permute-start(f32[1,3,32,128]{3,2,1,0:T(8,128)S(1)} %get-tuple-element.96), channel_id=1, source_target_pairs={{0,16},{8,24},{16,0},{24,8},{1,17},{9,25},{17,1},{25,9},{2,18},{10... | collective-permute-start | bytes 147464 | tf_op jit(solution)/shard_map/ppermute | solution.py:551
  31.5 0.8 %final_fields.1 = f32[1,2,4,32,512]{4,3,2,1,0:T(8,128)} custom-call(f32[2,32,512]{2,1,0:T(8,128)S(1)} %get-tuple-element.78.refs_0_, f32[2,32,512]{2,1,0:T(8,128)S(1)} %get-tuple-element.79.refs_1_, f32[2,32,512]{2,1,0:T(8,128)S(1)} %get-tuple-element.85.refs_0_.refs_2_, f32[2,32,512]{2,1,0:T(8,128)S(1)} %get-tuple-element.88.refs_3_.refs_0_), custom_call_target="tpu_custom_call" | custom-call | flops 1000000 | bytes 125000 | tf_op jit(solution)/shard_map/final_fields/pallas_call | solution.py:30
  32.4 0.0 collective-permute-done.7.refs_4_
  32.4 0.0 collective-permute-done.10.refs_8_
  32.4 1.5 %collective-permute-done.11.refs_9_ = f32[1,3,32,128]{3,2,1,0:T(8,128)S(1)} collective-permute-done((f32[1,3,32,128]{3,2,1,0:T(8,128)S(1)}, f32[1,3,32,128]{3,2,1,0:T(8,128)S(1)}, u32[]{:S(2)}, u32[]{:S(2)}) %collective-permute-start.11) | collective-permute-done | bytes 49184 | tf_op jit(solution)/shard_map/ppermute | solution.py:551
  33.9 1.6 %collective-permute-done.12.refs_10_ = f32[1,3,32,128]{3,2,1,0:T(8,128)S(1)} collective-permute-done((f32[1,3,32,128]{3,2,1,0:T(8,128)S(1)}, f32[1,3,32,128]{3,2,1,0:T(8,128)S(1)}, u32[]{:S(2)}, u32[]{:S(2)}) %collective-permute-start.12) | collective-permute-done | bytes 49184 | tf_op jit(solution)/shard_map/ppermute | solution.py:551
  35.4 1.0 %collective-permute-done.9.refs_6_ = f32[1,3,32,128]{3,2,1,0:T(8,128)S(1)} collective-permute-done((f32[1,3,32,128]{3,2,1,0:T(8,128)S(1)}, f32[1,3,32,128]{3,2,1,0:T(8,128)S(1)}, u32[]{:S(2)}, u32[]{:S(2)}) %collective-permute-start.9) | collective-permute-done | bytes 49184 | tf_op jit(solution)/shard_map/ppermute | solution.py:551
  36.5 0.7 %combine.1 = (f32[4,32,128]{2,1,0:T(8,128)}, f32[4,32,128]{2,1,0:T(8,128)}, f32[4,32,128]{2,1,0:T(8,128)}) custom-call(f32[4,32,512]{2,1,0:T(8,128)S(1)} %get-tuple-element.54.refs_0_, f32[4,32,512]{2,1,0:T(8,128)S(1)} %get-tuple-element.55.refs_1_, f32[4,32,512]{2,1,0:T(8,128)S(1)} %get-tuple-element.56.refs_2_, ...), custom_call_target="tpu_custom_call" | custom-call | flops 1000000 | bytes 125000 | tf_op jit(solution)/shard_map/combine/pallas_call | solution.py:30
  (3 shorter events, 0.0 us)
Async XLA Ops:
  0.6 7.1 %copy-start.1 = (f32[1,3,1536]{2,0,1:T(1,128)S(1)}, f32[1,3,1536]{2,0,1:T(1,128)}, u32[]{:S(2)}) copy-start(f32[1,3,1536]{2,0,1:T(1,128)} %param.21) | copy-start | bytes 55300
  0.6 8.2 %copy-start = (s32[1,1536]{1,0:T(1,128)S(1)}, s32[1,1536]{1,0:T(1,128)}, u32[]{:S(2)}) copy-start(s32[1,1536]{1,0:T(1,128)} %refs_0_.3) | copy-start | bytes 18436
  2.3 7.0 %collective-permute-start = (f32[80,512]{1,0:T(8,128)S(1)}, f32[80,512]{1,0:T(8,128)S(1)}, u32[]{:S(2)}, u32[]{:S(2)}) collective-permute-start(f32[80,512]{1,0:T(8,128)S(1)} %get-tuple-element.62), channel_id=1, source_target_pairs={{0,1},{1,0},{2,3},{3,2},{8,9},{9,8},{10,11},{11,10},{16,17},{17,16... | collective-permute-start | bytes 491528 | tf_op jit(solution)/shard_map/ppermute | solution.py:70
  2.9 6.5 %collective-permute-start.1 = (f32[80,512]{1,0:T(8,128)S(1)}, f32[80,512]{1,0:T(8,128)S(1)}, u32[]{:S(2)}, u32[]{:S(2)}) collective-permute-start(f32[80,512]{1,0:T(8,128)S(1)} %get-tuple-element.63), channel_id=1, source_target_pairs={{0,8},{1,2},{2,1},{3,11},{8,0},{9,10},{10,9},{11,3},{16,24},{17,18... | collective-permute-start | bytes 491528 | tf_op jit(solution)/shard_map/ppermute | solution.py:70
  5.5 7.8 %collective-permute-start.2 = (f32[2,32,512]{2,1,0:T(8,128)S(1)}, f32[2,32,512]{2,1,0:T(8,128)S(1)}, u32[]{:S(2)}, u32[]{:S(2)}) collective-permute-start(f32[2,32,512]{2,1,0:T(8,128)S(1)} %get-tuple-element.70), channel_id=1, source_target_pairs={{0,4},{4,0},{1,5},{5,1},{2,6},{6,2},{3,7},{7,3},{8,12},{12,8},{9,1... | collective-permute-start | bytes 393224 | tf_op jit(solution)/shard_map/ppermute | solution.py:59
  9.7 4.0 %collective-permute-start.3 = (f32[2,8,512]{2,1,0:T(8,128)S(1)}, f32[2,8,512]{2,1,0:T(8,128)S(1)}, u32[]{:S(2)}, u32[]{:S(2)}) collective-permute-start(f32[2,8,512]{2,1,0:T(8,128)S(1)} %get-tuple-element.71), channel_id=1, source_target_pairs={{0,4},{4,0},{1,5},{5,1},{2,6},{6,2},{3,7},{7,3},{8,12},{12,8},{9,1... | collective-permute-start | bytes 98312 | tf_op jit(solution)/shard_map/ppermute | solution.py:59
  14.1 5.3 %collective-permute-start.4 = (f32[72,512]{1,0:T(8,128)S(1)}, f32[72,512]{1,0:T(8,128)S(1)}, u32[]{:S(2)}, u32[]{:S(2)}) collective-permute-start(f32[72,512]{1,0:T(8,128)S(1)} %get-tuple-element.81), channel_id=1, source_target_pairs={{0,4},{4,0},{1,5},{5,1},{2,6},{6,2},{3,7},{7,3},{8,12},{12,8},{9,1... | collective-permute-start | bytes 442376 | tf_op jit(solution)/shard_map/ppermute | solution.py:59
  16.4 6.6 %collective-permute-start.6 = (f32[2,2,3,32,128]{4,3,2,1,0:T(8,128)S(1)}, f32[2,2,3,32,128]{4,3,2,1,0:T(8,128)S(1)}, u32[]{:S(2)}, u32[]{:S(2)}) collective-permute-start(f32[2,2,3,32,128]{4,3,2,1,0:T(8,128)S(1)} %get-tuple-element.90), channel_id=1, source_target_pairs={{0,8},{8,0},{16,24},{24,16},{1,9},{9,1},{17,25},{25,17},{2,10},{10... | collective-permute-start | bytes 589832 | tf_op jit(solution)/shard_map/ppermute | solution.py:551
  19.7 5.9 %collective-permute-start.5 = (f32[72,512]{1,0:T(8,128)S(1)}, f32[72,512]{1,0:T(8,128)S(1)}, u32[]{:S(2)}, u32[]{:S(2)}) collective-permute-start(f32[72,512]{1,0:T(8,128)S(1)} %get-tuple-element.86), channel_id=1, source_target_pairs={{0,4},{4,0},{1,5},{5,1},{2,6},{6,2},{3,7},{7,3},{8,12},{12,8},{9,1... | collective-permute-start | bytes 442376 | tf_op jit(solution)/shard_map/ppermute | solution.py:59
  21.4 9.1 %collective-permute-start.8 = (f32[2,1,3,32,128]{4,3,2,1,0:T(8,128)S(1)}, f32[2,1,3,32,128]{4,3,2,1,0:T(8,128)S(1)}, u32[]{:S(2)}, u32[]{:S(2)}) collective-permute-start(f32[2,1,3,32,128]{4,3,2,1,0:T(8,128)S(1)} %get-tuple-element.94), channel_id=1, source_target_pairs={{0,8},{8,0},{16,24},{24,16},{1,9},{9,1},{17,25},{25,17},{2,10},{10... | collective-permute-start | bytes 294920 | tf_op jit(solution)/shard_map/ppermute | solution.py:551
  23.0 9.3 %collective-permute-start.7 = (f32[2,3,32,128]{3,2,1,0:T(8,128)S(1)}, f32[2,3,32,128]{3,2,1,0:T(8,128)S(1)}, u32[]{:S(2)}, u32[]{:S(2)}) collective-permute-start(f32[2,3,32,128]{3,2,1,0:T(8,128)S(1)} %get-tuple-element.92), channel_id=1, source_target_pairs={{0,16},{8,24},{16,0},{24,8},{1,17},{9,25},{17,1},{25,9},{2,18},{10... | collective-permute-start | bytes 294920 | tf_op jit(solution)/shard_map/ppermute | solution.py:551
  26.0 6.3 %collective-permute-start.10 = (f32[1,3,32,128]{3,2,1,0:T(8,128)S(1)}, f32[1,3,32,128]{3,2,1,0:T(8,128)S(1)}, u32[]{:S(2)}, u32[]{:S(2)}) collective-permute-start(f32[1,3,32,128]{3,2,1,0:T(8,128)S(1)} %get-tuple-element.98), channel_id=1, source_target_pairs={{0,8},{8,0},{16,24},{24,16},{1,9},{9,1},{17,25},{25,17},{2,10},{10... | collective-permute-start | bytes 147464 | tf_op jit(solution)/shard_map/ppermute | solution.py:551
  27.3 6.6 %collective-permute-start.11 = (f32[1,3,32,128]{3,2,1,0:T(8,128)S(1)}, f32[1,3,32,128]{3,2,1,0:T(8,128)S(1)}, u32[]{:S(2)}, u32[]{:S(2)}) collective-permute-start(f32[1,3,32,128]{3,2,1,0:T(8,128)S(1)} %get-tuple-element.99), channel_id=1, source_target_pairs={{0,16},{8,24},{16,0},{24,8},{1,17},{9,25},{17,1},{25,9},{2,18},{10... | collective-permute-start | bytes 147464 | tf_op jit(solution)/shard_map/ppermute | solution.py:551
  29.5 5.9 %collective-permute-start.12 = (f32[1,3,32,128]{3,2,1,0:T(8,128)S(1)}, f32[1,3,32,128]{3,2,1,0:T(8,128)S(1)}, u32[]{:S(2)}, u32[]{:S(2)}) collective-permute-start(f32[1,3,32,128]{3,2,1,0:T(8,128)S(1)} %get-tuple-element.100), channel_id=1, source_target_pairs={{0,24},{8,16},{16,8},{24,0},{1,25},{9,17},{17,9},{25,1},{2,26},{10... | collective-permute-start | bytes 147464 | tf_op jit(solution)/shard_map/ppermute | solution.py:551
  30.5 6.0 %collective-permute-start.9 = (f32[1,3,32,128]{3,2,1,0:T(8,128)S(1)}, f32[1,3,32,128]{3,2,1,0:T(8,128)S(1)}, u32[]{:S(2)}, u32[]{:S(2)}) collective-permute-start(f32[1,3,32,128]{3,2,1,0:T(8,128)S(1)} %get-tuple-element.96), channel_id=1, source_target_pairs={{0,16},{8,24},{16,0},{24,8},{1,17},{9,25},{17,1},{25,9},{2,18},{10... | collective-permute-start | bytes 147464 | tf_op jit(solution)/shard_map/ppermute | solution.py:551

commit v4 on v3

--- a/solution.py
+++ b/solution.py
@@ -10,6 +10,11 @@
 LEVELS = 32
 LANES = 128
 HALO = 4
+ORDER = (2, 3, 1)
+WAVE = (
+    {(0, 1): (1, "a"), (2,): (2, "b"), (3,): (3, None)},
+    {"a": (2, 2, False), "b": (3, 2, True)},
+)
 VMEM_LIMIT = 8 * 1024 * 1024
 F32 = jnp.float32
 
@@ -92,7 +97,7 @@
         last = self.steps - 1
         ready = [self.phase(last, m) for m in range(self.nx)]
         if self.src == 4 and ready == [0, 1, 2, 3]:
-            return {(0, 1): (1, "a"), (2,): (2, "b"), (3,): (3, None)}, {"a": 2, "b": 3}
+            return WAVE
         pieces = {}
         for m, phase in enumerate(ready):
             pieces.setdefault(phase, []).append(m)
@@ -133,7 +138,7 @@
 def pack_edges(tile, raw):
     placed, total = edge_rows(tile)
     assert tile.nx % 4 == 0
-    outs = {"even": (total, tile.nz), "odd": (total, tile.nz), "near": (2, tile.ny, tile.nz)}
+    outs = {"odd": (total, tile.nz), "even": (total, tile.nz), "near": (2, tile.ny, tile.nz)}
     if tile.far:
         outs["far"] = outs["near"]
     outs.update({key: (value.shape, value.dtype) for key, value in raw.items()})
@@ -314,22 +319,29 @@
     return out["surface"]
 
 
-def halo_state(tile, got_even, got_odd, after):
-    outs = {"uh": (4, tile.nx, 8, tile.nz), "wh": (9, tile.nx, 8, tile.nz), "near": (2, 8, tile.nz)}
+def halo_edges(tile, got_even, got_odd, after):
+    outs = {"near": (2, 8, tile.nz)}
     if tile.far:
         outs["far"] = outs["near"]
+
+    def body(r):
+        for key in outs:
+            for c in range(2):
+                r[key][c] = halo_block(tile, r, c, tile.nx - 1 if key == "near" else 0)
+
+    ins = {"got_odd": got_odd, "got_even": got_even, "after": after}
+    return run_kernel(body, ins, outs, name="halo_edges", flops=10**5)
+
+
+def halo_state(tile, got_even, got_odd, after):
+    outs = {"uh": (4, tile.nx, 8, tile.nz), "wh": (9, tile.nx, 8, tile.nz)}
 
     def body(r):
         tables = angle_tables(8)
         sign = x_sign()
         for m in range(tile.nx):
             for item in range(4):
-                block = halo_block(tile, r, item, m)
-                r["uh"][item, m] = block
-                if item < 2 and m == tile.nx - 1:
-                    r["near"][item] = block
-                if item < 2 and m == 0 and tile.far:
-                    r["far"][item] = block
+                r["uh"][item, m] = halo_block(tile, r, item, m)
             coefs = [halo_block(tile, r, item, m) for item in range(4, 9)]
             for j in range(tile.nj):
                 part = [value[:, j * LANES : (j + 1) * LANES] for value in coefs]
@@ -338,7 +350,7 @@
                     part[3].astype(jnp.int32), part[4].astype(jnp.int32),
                 )
 
-    ins = {"got_even": got_even, "got_odd": got_odd, "after": after}
+    ins = {"got_odd": got_odd, "got_even": got_even, "after": after}
     return run_kernel(body, ins, outs, name="halo_state", flops=10**6)
 
 
@@ -416,7 +428,10 @@
                 for k in range(tile.src):
                     owner = jnp.bitwise_xor(me, k)
                     if self.halved(planes):
-                        target = r[("send" if k % 2 else "keep", planes)].at[k // 2]
+                        second = tile.second[tile.plan[planes][1]][1]
+                        first = 1 if second > 1 else 2
+                        kind = "keep" if k in (0, second) else "send"
+                        target = r[(kind, planes)].at[0 if k in (0, first) else 1]
                     else:
                         target = r[("s", planes, k)]
                     for part in range(per):
@@ -551,8 +566,12 @@
     return lax.ppermute(block, "src", [(i, i ^ k) for i in range(tile.src)])
 
 
-def add_halves(tile, state, pieces, after):
-    ins, outs, count = {"after": after}, {}, 0
+def second_round(tile, state, pieces, k, after, along):
+    ins, outs, start = {"after": after}, {}, 0
+    if along is not None:
+        ins["along"] = state[("s", along, k)]
+        start = len(along)
+    count = start
     for planes in pieces:
         ins[("keep", planes)], ins[("got", planes)] = state[("keep", planes)], state[("got", planes)]
         outs[("s", planes, 0)] = state[("keep", planes)].shape[1:]
@@ -560,18 +579,22 @@
     outs["passed"] = (count, *outs[("s", pieces[0], 0)][1:])
 
     def body(r):
-        at = 0
+        if along is not None:
+            r["passed"][:start] = r["along"][...]
+        at = start
         for planes in pieces:
             keep, got = r[("keep", planes)], r[("got", planes)]
             r[("s", planes, 0)][...] = keep[0] + got[0]
             r["passed"][at : at + len(planes)] = keep[1] + got[1]
             at += len(planes)
 
-    state.update(run_kernel(body, ins, outs, name="add_halves", flops=10**5))
-    passed = xor_swap(tile, state["passed"], 2)
-    at = 0
+    state.update(run_kernel(body, ins, outs, name="second_round", flops=10**5))
+    got = xor_swap(tile, state["passed"], k)
+    at = start
+    if along is not None:
+        state[("r", along, k)] = (got, 0)
     for planes in pieces:
-        state[("r", planes, 2)] = (passed, at)
+        state[("r", planes, k)] = (got, at)
         at += len(planes)
 
 
@@ -579,11 +602,12 @@
     depth = tile.nz // tile.src
     ins = {key: state[key] for key in ("velocity", "eps", "delta")}
     starts = {}
+    for k in ORDER:
+        for planes in pieces:
+            if ("r", planes, k) in state:
+                ins[("r", planes, k)], starts[(planes, k)] = state[("r", planes, k)]
     for planes in pieces:
         ins[("s", planes, 0)] = state[("s", planes, 0)]
-        for k in range(1, tile.src):
-            if ("r", planes, k) in state:
-                ins[("r", planes, k)], starts[(planes, k)] = state[("r", planes, k)]
     shape = (tile.nx, tile.ny, depth)
 
     def body(r):
@@ -617,6 +641,7 @@
         for m, key in enumerate(keys):
             for c in range(2):
                 r["out"][0, c, tile.place(m)] = r[key][c]
+
 
     outs = {"out": (1, 2, tile.nx, tile.ny, tile.nz)}
     out = run_kernel(
@@ -657,16 +682,16 @@
         if tile.far:
             state[("xf" + key, t)] = swap(far, "gx", tile.gx, 1)
 
+    got_odd = swap_rows(tile, edges["odd"], 1)
     got_even = swap_rows(tile, edges["even"], 0)
     exchange("", 0, edges["near"], edges.get("far"))
-    got_odd = swap_rows(tile, edges["odd"], 1)
     state.update(own_state(tile, state, forward_field))
     state["surface"] = surface_load(
         tile, channel_cell, channel_count, residual_trace, state["w"]
     )
-    halo = halo_state(tile, got_even, got_odd, state["surface"])
-    state["uh"], state["wh"] = halo["uh"], halo["wh"]
+    halo = halo_edges(tile, got_even, got_odd, state["surface"])
     exchange("h", 0, halo["near"], halo.get("far"))
+    state.update(halo_state(tile, got_even, got_odd, halo["near"]))
 
     ops = [(t, m) for t in range(tile.steps) for m in range(tile.nx)]
     pieces = list(tile.plan)
@@ -685,16 +710,24 @@
         if bulk:
             Stage(tile, state, bulk, done, f"bulk_{phase}").run()
             state["token"] = state[("u", bulk[0][0] + 1, bulk[0][1])]
+        later = [(name, k) for name, (when, k, _) in tile.second.items() if when == phase]
+        direct = [planes for planes in done if tile.plan[planes][1] is None]
+        joined = [k for name, k in later if tile.second[name][2] and direct]
         for planes in done:
-            if ("send", planes) in state:
-                state[("got", planes)] = xor_swap(tile, state[("send", planes)], 1)
+            if planes not in direct:
+                first = 1 if tile.second[tile.plan[planes][1]][1] > 1 else 2
+                state[("got", planes)] = xor_swap(tile, state[("send", planes)], first)
                 continue
-            for k in range(1, tile.src):
-                state[("r", planes, k)] = (xor_swap(tile, state[("s", planes, k)], k), 0)
-        for name, when in tile.second.items():
-            if when == phase:
-                carried = [planes for planes in pieces if tile.plan[planes][1] == name]
-                add_halves(tile, state, carried, state["token"])
+            for k in range(tile.src - 1, 0, -1):
+                if k not in joined:
+                    state[("r", planes, k)] = (xor_swap(tile, state[("s", planes, k)], k), 0)
+        for name, k in later:
+            group = [planes for planes in pieces if tile.plan[planes][1] == name]
+            along = direct[0] if k in joined else None
+            after = state["token"]
+            second_round(tile, state, group, k, after, along)
+            if phase < tile.steps:
+                state["token"] = state["passed"]
     following = final_fields(tile, state)
     return (following, *combine(tile, state, pieces))
 

time: 37.4 us -> 36 us (0.963)
  starting transfers between devices: 20.3 us -> 19.2 us
  waiting for transfers between devices: 5.83 us -> 5.42 us
    ppermute x7 -> x6, starting transfers between devices: 11.4 us -> 10.4 us  [xor_swap(): return lax.ppermute(block, 'src', [(i, i ^ k) for i in range(tile.src)])]
    ppermute x4, waiting for transfers between devices: 1.72 us -> 1.3 us  [swap(): return lax.ppermute(block, axis, pair_swaps(count, first))]
    pallas_call x14 -> x15, Pallas kernels: 9.64 us -> 9.68 us  [run_kernel(): pl.pallas_call(kernel, name=name, out_shape=[jax.ShapeDtypeStruct(shape,...]
    ppermute x7 -> x6, waiting for transfers between devices: 4.1 us -> 4.11 us  [xor_swap(): return lax.ppermute(block, 'src', [(i, i ^ k) for i in range(tile.src)])]
  transfers between devices with their start and end apart: 13 -> 12, of which waited for: 5 -> 4; matrix products, arithmetic and copies ran while one was open for 0% -> 0% of each run, Pallas kernels for 19% -> 19%
where the time goes in v4:
time: 36 us; the launch traced here: 35.8 us
  starting transfers between devices  19.2 us (53%)
  Pallas kernels  9.68 us (27%)
  waiting for transfers between devices  5.42 us (15%)
  between operations  1.43 us (4%)
    ppermute x6, starting transfers between devices, xor_swap(): return lax.ppermute(block, 'src', [(i, i ^ k) for i in range(tile.src)])  10.4 us
    pallas_call x15, Pallas kernels, run_kernel(): pl.pallas_call(kernel, name=name, out_shape=[jax.ShapeDtypeStruct(shape,...  9.68 us
    ppermute x4, starting transfers between devices, swap(): return lax.ppermute(block, axis, pair_swaps(count, first))  5.73 us
    ppermute x6, waiting for transfers between devices, xor_swap(): return lax.ppermute(block, 'src', [(i, i ^ k) for i in range(tile.src)])  4.11 us
    ppermute x2, starting transfers between devices, swap_rows(): return lax.ppermute(block, ('src', 'gy'), joint)  3.12 us
    ppermute x4, waiting for transfers between devices, swap(): return lax.ppermute(block, axis, pair_swaps(count, first))  1.3 us
  transfers between devices with their start and end apart: 12, of which 4 were waited for; matrix products, arithmetic and copies ran while one was open for 0% of the time, Pallas kernels for 19%

profile of v4, /device:TPU:0, one launch (start us, length us, event | category | flops | bytes accessed | tf_op | source)
XLA Modules:
  0.0 35.8 jit_solution(10142520536884635768)
XLA Ops:
  0.6 0.0 copy-start.1
  0.6 0.0 copy-start
  0.7 1.7 %pack_edges.1 = (f32[80,512]{1,0:T(8,128)S(1)}, f32[80,512]{1,0:T(8,128)S(1)}, f32[2,32,512]{2,1,0:T(8,128)S(1)}, f32[1,2,4,32,512]{4,3,2,1,0:T(8,128)S(1)}, f32...) custom-call(f32[1,2,4,32,512]{4,3,2,1,0:T(8,128)} %refs_0_.2, ...), custom_call_target="tpu_custom_call" | custom-call | flops 1000000 | bytes 125000 | tf_op jit(solution)/shard_map/pack_edges/pallas_call | solution.py:35
  2.3 3.1 %collective-permute-start = (f32[80,512]{1,0:T(8,128)S(1)}, f32[80,512]{1,0:T(8,128)S(1)}, u32[]{:S(2)}, u32[]{:S(2)}) collective-permute-start(f32[80,512]{1,0:T(8,128)S(1)} %get-tuple-element.61), channel_id=1, source_target_pairs={{0,8},{1,2},{2,1},{3,11},{8,0},{9,10},{10,9},{11,3},{16,24},{17,18... | collective-permute-start | bytes 491528 | tf_op jit(solution)/shard_map/ppermute | solution.py:75
  5.4 0.0 collective-permute-start.1
  5.5 1.5 %collective-permute-start.2 = (f32[2,32,512]{2,1,0:T(8,128)S(1)}, f32[2,32,512]{2,1,0:T(8,128)S(1)}, u32[]{:S(2)}, u32[]{:S(2)}) collective-permute-start(f32[2,32,512]{2,1,0:T(8,128)S(1)} %get-tuple-element.69), channel_id=1, source_target_pairs={{0,4},{4,0},{1,5},{5,1},{2,6},{6,2},{3,7},{7,3},{8,12},{12,8},{9,1... | collective-permute-start | bytes 393224 | tf_op jit(solution)/shard_map/ppermute | solution.py:64
  7.6 0.0 copy-done.1
  7.7 1.1 %own_state.1 = (f32[9,4,32,512]{3,2,1,0:T(8,128)S(1)}, bf16[3,1,2,4,32,512]{5,4,3,2,1,0:T(8,128)(2,1)S(1)}) custom-call(f32[4,32,512]{2,1,0:T(8,128)S(1)} %get-tuple-element.53.refs_0_, f32[4,32,512]{2,1,0:T(8,128)S(1)} %get-tuple-element.54.refs_1_, f32[4,32,512]{2,1,0:T(8,128)S(1)} %get-tuple-element.55.refs_2_, ...), custom_call_target="tpu_custom_call" | custom-call | flops 3000000 | bytes 375000 | tf_op jit(solution)/shard_map/own_state/pallas_call | solution.py:35
  8.8 0.0 copy-done
  8.8 0.5 %surface_load.1.refs_2_.refs_6_.refs_9_.refs_8_.refs_7_ = f32[3,4,40,128]{3,2,1,0:T(8,128)S(1)} custom-call(s32[1,1536]{1,0:T(1,128)S(1)} %copy-done, s32[1]{0:T(128)S(6)} %copy.16.refs_1_, f32[1,3,1536]{2,1,0:T(4,128)S(1)} %copy.15.refs_2_, f32[9,4,32,512]{3,2,1,0:T(8,128)S(1)} %get-tuple-element.58.refs_3_.refs_0_.refs_1_), custom_call_target="tpu_custom_call" | custom-call | flops 2000000 | bytes 250000 | tf_op jit(solution)/shard_map/surface_load/pallas_call | solution.py:35
  9.3 0.0 collective-permute-done.refs_0_
  9.3 0.0 collective-permute-done.1.refs_1_
  9.4 1.4 %collective-permute-start.3 = (f32[2,8,512]{2,1,0:T(8,128)S(1)}, f32[2,8,512]{2,1,0:T(8,128)S(1)}, u32[]{:S(2)}, u32[]{:S(2)}) collective-permute-start(f32[2,8,512]{2,1,0:T(8,128)S(1)} %halo_edges.1.refs_2_), channel_id=1, source_target_pairs={{0,4},{4,0},{1,5},{5,1},{2,6},{6,2},{3,7},{7,3},{8,12},{12,8},{9,1... | collective-permute-start | bytes 98312 | tf_op jit(solution)/shard_map/ppermute | solution.py:64
  10.8 0.3 halo_state.1
  11.1 2.2 %bulk_0.1 = (f32[2,40,512]{2,1,0:T(8,128)S(1)}, f32[4,3,32,128]{3,2,1,0:T(8,128)}, f32[2,40,512]{2,1,0:T(8,128)S(1)}, f32[4,3,32,128]{3,2,1,0:T(8,128)}, f32[2,4...) custom-call(f32[9,4,32,512]{3,2,1,0:T(8,128)S(1)} %get-tuple-element, ...), custom_call_target="tpu_custom_call" | custom-call | flops 10100000 | bytes 1262500 | tf_op jit(solution)/shard_map/bulk_0/pallas_call | solution.py:35
  13.3 0.0 collective-permute-done.2.refs_5_
  13.3 0.0 collective-permute-done.3.refs_6_
  13.4 0.3 front_1.1
  13.7 1.4 %collective-permute-start.4 = (f32[72,512]{1,0:T(8,128)S(1)}, f32[72,512]{1,0:T(8,128)S(1)}, u32[]{:S(2)}, u32[]{:S(2)}) collective-permute-start(f32[72,512]{1,0:T(8,128)S(1)} %get-tuple-element.79), channel_id=1, source_target_pairs={{0,4},{4,0},{1,5},{5,1},{2,6},{6,2},{3,7},{7,3},{8,12},{12,8},{9,1... | collective-permute-start | bytes 442376 | tf_op jit(solution)/shard_map/ppermute | solution.py:64
  15.1 0.9 %bulk_1.1 = (f32[2,40,512]{2,1,0:T(8,128)S(1)}, f32[4,3,32,128]{3,2,1,0:T(8,128)S(1)}, f32[2,32,512]{2,1,0:T(8,128)S(1)}, f32[2,32,512]{2,1,0:T(8,128)S(1)}, f32...) custom-call(f32[9,4,32,512]{3,2,1,0:T(8,128)S(1)} %get-tuple-element.58.refs_3_.refs_0_.refs_1_, ...), custom_call_target="tpu_custom_call" | custom-call | flops 6100000 | bytes 762500 | tf_op jit(solution)/shard_map/bulk_1/pallas_call | solution.py:35
  16.0 1.6 %collective-permute-start.5 = (f32[2,2,3,32,128]{4,3,2,1,0:T(8,128)S(1)}, f32[2,2,3,32,128]{4,3,2,1,0:T(8,128)S(1)}, u32[]{:S(2)}, u32[]{:S(2)}) collective-permute-start(f32[2,2,3,32,128]{4,3,2,1,0:T(8,128)S(1)} %get-tuple-element.85), channel_id=1, source_target_pairs={{0,8},{8,0},{16,24},{24,16},{1,9},{9,1},{17,25},{25,17},{2,10},{10... | collective-permute-start | bytes 589832 | tf_op jit(solution)/shard_map/ppermute | solution.py:566
  17.7 1.3 %collective-permute-done.4.refs_5_ = f32[72,512]{1,0:T(8,128)S(1)} collective-permute-done((f32[72,512]{1,0:T(8,128)S(1)}, f32[72,512]{1,0:T(8,128)S(1)}, u32[]{:S(2)}, u32[]{:S(2)}) %collective-permute-start.4) | collective-permute-done | bytes 147488 | tf_op jit(solution)/shard_map/ppermute | solution.py:64
  18.9 0.3 front_2.1
  19.3 1.4 %collective-permute-start.6 = (f32[72,512]{1,0:T(8,128)S(1)}, f32[72,512]{1,0:T(8,128)S(1)}, u32[]{:S(2)}, u32[]{:S(2)}) collective-permute-start(f32[72,512]{1,0:T(8,128)S(1)} %get-tuple-element.87), channel_id=1, source_target_pairs={{0,4},{4,0},{1,5},{5,1},{2,6},{6,2},{3,7},{7,3},{8,12},{12,8},{9,1... | collective-permute-start | bytes 442376 | tf_op jit(solution)/shard_map/ppermute | solution.py:64
  20.7 0.3 bulk_2.1
  21.0 1.6 %collective-permute-start.8 = (f32[2,1,3,32,128]{4,3,2,1,0:T(8,128)S(1)}, f32[2,1,3,32,128]{4,3,2,1,0:T(8,128)S(1)}, u32[]{:S(2)}, u32[]{:S(2)}) collective-permute-start(f32[2,1,3,32,128]{4,3,2,1,0:T(8,128)S(1)} %get-tuple-element.92), channel_id=1, source_target_pairs={{0,8},{8,0},{16,24},{24,16},{1,9},{9,1},{17,25},{25,17},{2,10},{10... | collective-permute-start | bytes 294920 | tf_op jit(solution)/shard_map/ppermute | solution.py:566
  22.6 0.0 collective-permute-done.5.refs_2_
  22.7 2.7 %collective-permute-start.7 = (f32[2,3,32,128]{3,2,1,0:T(8,128)S(1)}, f32[2,3,32,128]{3,2,1,0:T(8,128)S(1)}, u32[]{:S(2)}, u32[]{:S(2)}) collective-permute-start(f32[2,3,32,128]{3,2,1,0:T(8,128)S(1)} %get-tuple-element.86.refs_0_), channel_id=1, source_target_pairs={{0,16},{8,24},{16,0},{24,8},{1,17},{9,25},{17,1},{25,9},{2,18},{10... | collective-permute-start | bytes 294920 | tf_op jit(solution)/shard_map/ppermute | solution.py:566
  25.3 0.0 collective-permute-done.6.refs_5_
  25.3 0.3 front_3.1
  25.7 0.0 collective-permute-done.8.refs_3_
  25.7 2.7 %collective-permute-start.9 = (f32[2,3,32,128]{3,2,1,0:T(8,128)S(1)}, f32[2,3,32,128]{3,2,1,0:T(8,128)S(1)}, u32[]{:S(2)}, u32[]{:S(2)}) collective-permute-start(f32[2,3,32,128]{3,2,1,0:T(8,128)S(1)} %get-tuple-element.93), channel_id=1, source_target_pairs={{0,16},{8,24},{16,0},{24,8},{1,17},{9,25},{17,1},{25,9},{2,18},{10... | collective-permute-start | bytes 294920 | tf_op jit(solution)/shard_map/ppermute | solution.py:566
  28.4 1.4 %collective-permute-start.10 = (f32[1,3,32,128]{3,2,1,0:T(8,128)S(1)}, f32[1,3,32,128]{3,2,1,0:T(8,128)S(1)}, u32[]{:S(2)}, u32[]{:S(2)}) collective-permute-start(f32[1,3,32,128]{3,2,1,0:T(8,128)S(1)} %get-tuple-element.94), channel_id=1, source_target_pairs={{0,24},{8,16},{16,8},{24,0},{1,25},{9,17},{17,9},{25,1},{2,26},{10... | collective-permute-start | bytes 147464 | tf_op jit(solution)/shard_map/ppermute | solution.py:566
  29.8 0.3 collective-permute-start.11
  30.1 0.8 %final_fields.1 = f32[1,2,4,32,512]{4,3,2,1,0:T(8,128)} custom-call(f32[2,32,512]{2,1,0:T(8,128)S(1)} %get-tuple-element.76.refs_0_, f32[2,32,512]{2,1,0:T(8,128)S(1)} %get-tuple-element.77.refs_1_, f32[2,32,512]{2,1,0:T(8,128)S(1)} %get-tuple-element.83.refs_0_.refs_2_, f32[2,32,512]{2,1,0:T(8,128)S(1)} %get-tuple-element.89.refs_3_.refs_0_), custom_call_target="tpu_custom_call" | custom-call | flops 1000000 | bytes 125000 | tf_op jit(solution)/shard_map/final_fields/pallas_call | solution.py:35
  30.9 1.9 %collective-permute-done.7.refs_3_ = f32[2,3,32,128]{3,2,1,0:T(8,128)S(1)} collective-permute-done((f32[2,3,32,128]{3,2,1,0:T(8,128)S(1)}, f32[2,3,32,128]{3,2,1,0:T(8,128)S(1)}, u32[]{:S(2)}, u32[]{:S(2)}) %collective-permute-start.7) | collective-permute-done | bytes 98336 | tf_op jit(solution)/shard_map/ppermute | solution.py:566
  32.8 1.6 %collective-permute-done.10.refs_6_ = f32[1,3,32,128]{3,2,1,0:T(8,128)S(1)} collective-permute-done((f32[1,3,32,128]{3,2,1,0:T(8,128)S(1)}, f32[1,3,32,128]{3,2,1,0:T(8,128)S(1)}, u32[]{:S(2)}, u32[]{:S(2)}) %collective-permute-start.10) | collective-permute-done | bytes 49184 | tf_op jit(solution)/shard_map/ppermute | solution.py:566
  34.4 0.6 %collective-permute-done.11.refs_7_ = f32[1,3,32,128]{3,2,1,0:T(8,128)S(1)} collective-permute-done((f32[1,3,32,128]{3,2,1,0:T(8,128)S(1)}, f32[1,3,32,128]{3,2,1,0:T(8,128)S(1)}, u32[]{:S(2)}, u32[]{:S(2)}) %collective-permute-start.11) | collective-permute-done | bytes 49184 | tf_op jit(solution)/shard_map/ppermute | solution.py:566
  35.0 0.0 collective-permute-done.9.refs_4_.refs_5_
  35.0 0.7 %combine.1 = (f32[4,32,128]{2,1,0:T(8,128)}, f32[4,32,128]{2,1,0:T(8,128)}, f32[4,32,128]{2,1,0:T(8,128)}) custom-call(f32[4,32,512]{2,1,0:T(8,128)S(1)} %get-tuple-element.53.refs_0_, f32[4,32,512]{2,1,0:T(8,128)S(1)} %get-tuple-element.54.refs_1_, f32[4,32,512]{2,1,0:T(8,128)S(1)} %get-tuple-element.55.refs_2_, ...), custom_call_target="tpu_custom_call" | custom-call | flops 1000000 | bytes 125000 | tf_op jit(solution)/shard_map/combine/pallas_call | solution.py:35
  (4 shorter events, 0.1 us)
Async XLA Ops:
  0.6 7.0 %copy-start.1 = (f32[1,3,1536]{2,0,1:T(1,128)S(1)}, f32[1,3,1536]{2,0,1:T(1,128)}, u32[]{:S(2)}) copy-start(f32[1,3,1536]{2,0,1:T(1,128)} %param.21) | copy-start | bytes 55300
  0.6 8.2 %copy-start = (s32[1,1536]{1,0:T(1,128)S(1)}, s32[1,1536]{1,0:T(1,128)}, u32[]{:S(2)}) copy-start(s32[1,1536]{1,0:T(1,128)} %refs_0_.3) | copy-start | bytes 18436
  2.3 7.0 %collective-permute-start = (f32[80,512]{1,0:T(8,128)S(1)}, f32[80,512]{1,0:T(8,128)S(1)}, u32[]{:S(2)}, u32[]{:S(2)}) collective-permute-start(f32[80,512]{1,0:T(8,128)S(1)} %get-tuple-element.61), channel_id=1, source_target_pairs={{0,8},{1,2},{2,1},{3,11},{8,0},{9,10},{10,9},{11,3},{16,24},{17,18... | collective-permute-start | bytes 491528 | tf_op jit(solution)/shard_map/ppermute | solution.py:75
  5.4 3.9 %collective-permute-start.1 = (f32[80,512]{1,0:T(8,128)S(1)}, f32[80,512]{1,0:T(8,128)S(1)}, u32[]{:S(2)}, u32[]{:S(2)}) collective-permute-start(f32[80,512]{1,0:T(8,128)S(1)} %get-tuple-element.62), channel_id=1, source_target_pairs={{0,1},{1,0},{2,3},{3,2},{8,9},{9,8},{10,11},{11,10},{16,17},{17,16... | collective-permute-start | bytes 491528 | tf_op jit(solution)/shard_map/ppermute | solution.py:75
  5.5 7.9 %collective-permute-start.2 = (f32[2,32,512]{2,1,0:T(8,128)S(1)}, f32[2,32,512]{2,1,0:T(8,128)S(1)}, u32[]{:S(2)}, u32[]{:S(2)}) collective-permute-start(f32[2,32,512]{2,1,0:T(8,128)S(1)} %get-tuple-element.69), channel_id=1, source_target_pairs={{0,4},{4,0},{1,5},{5,1},{2,6},{6,2},{3,7},{7,3},{8,12},{12,8},{9,1... | collective-permute-start | bytes 393224 | tf_op jit(solution)/shard_map/ppermute | solution.py:64
  9.4 4.0 %collective-permute-start.3 = (f32[2,8,512]{2,1,0:T(8,128)S(1)}, f32[2,8,512]{2,1,0:T(8,128)S(1)}, u32[]{:S(2)}, u32[]{:S(2)}) collective-permute-start(f32[2,8,512]{2,1,0:T(8,128)S(1)} %halo_edges.1.refs_2_), channel_id=1, source_target_pairs={{0,4},{4,0},{1,5},{5,1},{2,6},{6,2},{3,7},{7,3},{8,12},{12,8},{9,1... | collective-permute-start | bytes 98312 | tf_op jit(solution)/shard_map/ppermute | solution.py:64
  13.7 5.2 %collective-permute-start.4 = (f32[72,512]{1,0:T(8,128)S(1)}, f32[72,512]{1,0:T(8,128)S(1)}, u32[]{:S(2)}, u32[]{:S(2)}) collective-permute-start(f32[72,512]{1,0:T(8,128)S(1)} %get-tuple-element.79), channel_id=1, source_target_pairs={{0,4},{4,0},{1,5},{5,1},{2,6},{6,2},{3,7},{7,3},{8,12},{12,8},{9,1... | collective-permute-start | bytes 442376 | tf_op jit(solution)/shard_map/ppermute | solution.py:64
  16.0 6.6 %collective-permute-start.5 = (f32[2,2,3,32,128]{4,3,2,1,0:T(8,128)S(1)}, f32[2,2,3,32,128]{4,3,2,1,0:T(8,128)S(1)}, u32[]{:S(2)}, u32[]{:S(2)}) collective-permute-start(f32[2,2,3,32,128]{4,3,2,1,0:T(8,128)S(1)} %get-tuple-element.85), channel_id=1, source_target_pairs={{0,8},{8,0},{16,24},{24,16},{1,9},{9,1},{17,25},{25,17},{2,10},{10... | collective-permute-start | bytes 589832 | tf_op jit(solution)/shard_map/ppermute | solution.py:566
  19.3 6.1 %collective-permute-start.6 = (f32[72,512]{1,0:T(8,128)S(1)}, f32[72,512]{1,0:T(8,128)S(1)}, u32[]{:S(2)}, u32[]{:S(2)}) collective-permute-start(f32[72,512]{1,0:T(8,128)S(1)} %get-tuple-element.87), channel_id=1, source_target_pairs={{0,4},{4,0},{1,5},{5,1},{2,6},{6,2},{3,7},{7,3},{8,12},{12,8},{9,1... | collective-permute-start | bytes 442376 | tf_op jit(solution)/shard_map/ppermute | solution.py:64
  21.0 4.7 %collective-permute-start.8 = (f32[2,1,3,32,128]{4,3,2,1,0:T(8,128)S(1)}, f32[2,1,3,32,128]{4,3,2,1,0:T(8,128)S(1)}, u32[]{:S(2)}, u32[]{:S(2)}) collective-permute-start(f32[2,1,3,32,128]{4,3,2,1,0:T(8,128)S(1)} %get-tuple-element.92), channel_id=1, source_target_pairs={{0,8},{8,0},{16,24},{24,16},{1,9},{9,1},{17,25},{25,17},{2,10},{10... | collective-permute-start | bytes 294920 | tf_op jit(solution)/shard_map/ppermute | solution.py:566
  22.7 10.2 %collective-permute-start.7 = (f32[2,3,32,128]{3,2,1,0:T(8,128)S(1)}, f32[2,3,32,128]{3,2,1,0:T(8,128)S(1)}, u32[]{:S(2)}, u32[]{:S(2)}) collective-permute-start(f32[2,3,32,128]{3,2,1,0:T(8,128)S(1)} %get-tuple-element.86.refs_0_), channel_id=1, source_target_pairs={{0,16},{8,24},{16,0},{24,8},{1,17},{9,25},{17,1},{25,9},{2,18},{10... | collective-permute-start | bytes 294920 | tf_op jit(solution)/shard_map/ppermute | solution.py:566
  25.7 9.3 %collective-permute-start.9 = (f32[2,3,32,128]{3,2,1,0:T(8,128)S(1)}, f32[2,3,32,128]{3,2,1,0:T(8,128)S(1)}, u32[]{:S(2)}, u32[]{:S(2)}) collective-permute-start(f32[2,3,32,128]{3,2,1,0:T(8,128)S(1)} %get-tuple-element.93), channel_id=1, source_target_pairs={{0,16},{8,24},{16,0},{24,8},{1,17},{9,25},{17,1},{25,9},{2,18},{10... | collective-permute-start | bytes 294920 | tf_op jit(solution)/shard_map/ppermute | solution.py:566
  28.4 6.1 %collective-permute-start.10 = (f32[1,3,32,128]{3,2,1,0:T(8,128)S(1)}, f32[1,3,32,128]{3,2,1,0:T(8,128)S(1)}, u32[]{:S(2)}, u32[]{:S(2)}) collective-permute-start(f32[1,3,32,128]{3,2,1,0:T(8,128)S(1)} %get-tuple-element.94), channel_id=1, source_target_pairs={{0,24},{8,16},{16,8},{24,0},{1,25},{9,17},{17,9},{25,1},{2,26},{10... | collective-permute-start | bytes 147464 | tf_op jit(solution)/shard_map/ppermute | solution.py:566
  29.8 5.3 %collective-permute-start.11 = (f32[1,3,32,128]{3,2,1,0:T(8,128)S(1)}, f32[1,3,32,128]{3,2,1,0:T(8,128)S(1)}, u32[]{:S(2)}, u32[]{:S(2)}) collective-permute-start(f32[1,3,32,128]{3,2,1,0:T(8,128)S(1)} %get-tuple-element.95), channel_id=1, source_target_pairs={{0,8},{8,0},{16,24},{24,16},{1,9},{9,1},{17,25},{25,17},{2,10},{10... | collective-permute-start | bytes 147464 | tf_op jit(solution)/shard_map/ppermute | solution.py:566

commit v5 on v4

--- a/solution.py
+++ b/solution.py
@@ -10,10 +10,10 @@
 LEVELS = 32
 LANES = 128
 HALO = 4
-ORDER = (2, 3, 1)
+ORDER = (3, 2, 1)
 WAVE = (
     {(0, 1): (1, "a"), (2,): (2, "b"), (3,): (3, None)},
-    {"a": (2, 2, False), "b": (3, 2, True)},
+    {"a": (2, 2, False), "b": (3, 3, True)},
 )
 VMEM_LIMIT = 8 * 1024 * 1024
 F32 = jnp.float32

time: 36 us -> 35.9 us (level)
  transfers between devices with their start and end apart: 12 -> 12, of which waited for: 4 -> 3; matrix products, arithmetic and copies ran while one was open for 0% -> 0% of each run, Pallas kernels for 19% -> 19%
where the time goes in v5:
time: 35.9 us; the launch traced here: 35.7 us
  starting transfers between devices  19.3 us (54%)
  Pallas kernels  9.68 us (27%)
  waiting for transfers between devices  5.32 us (15%)
  between operations  1.43 us (4%)
    ppermute x6, starting transfers between devices, xor_swap(): return lax.ppermute(block, 'src', [(i, i ^ k) for i in range(tile.src)])  10.4 us
    pallas_call x15, Pallas kernels, run_kernel(): pl.pallas_call(kernel, name=name, out_shape=[jax.ShapeDtypeStruct(shape,...  9.68 us
    ppermute x4, starting transfers between devices, swap(): return lax.ppermute(block, axis, pair_swaps(count, first))  5.73 us
    ppermute x6, waiting for transfers between devices, xor_swap(): return lax.ppermute(block, 'src', [(i, i ^ k) for i in range(tile.src)])  4.01 us
    ppermute x2, starting transfers between devices, swap_rows(): return lax.ppermute(block, ('src', 'gy'), joint)  3.12 us
    ppermute x4, waiting for transfers between devices, swap(): return lax.ppermute(block, axis, pair_swaps(count, first))  1.3 us
  transfers between devices with their start and end apart: 12, of which 3 were waited for; matrix products, arithmetic and copies ran while one was open for 0% of the time, Pallas kernels for 19%

profile of v5, /device:TPU:0, one launch (start us, length us, event | category | flops | bytes accessed | tf_op | source)
XLA Modules:
  0.0 35.7 jit_solution(17615884304286515187)
XLA Ops:
  0.6 0.0 copy-start.1
  0.6 0.0 copy-start
  0.7 1.7 %pack_edges.1 = (f32[80,512]{1,0:T(8,128)S(1)}, f32[80,512]{1,0:T(8,128)S(1)}, f32[2,32,512]{2,1,0:T(8,128)S(1)}, f32[1,2,4,32,512]{4,3,2,1,0:T(8,128)S(1)}, f32...) custom-call(f32[1,2,4,32,512]{4,3,2,1,0:T(8,128)} %refs_0_.2, ...), custom_call_target="tpu_custom_call" | custom-call | flops 1000000 | bytes 125000 | tf_op jit(solution)/shard_map/pack_edges/pallas_call | solution.py:35
  2.3 3.1 %collective-permute-start = (f32[80,512]{1,0:T(8,128)S(1)}, f32[80,512]{1,0:T(8,128)S(1)}, u32[]{:S(2)}, u32[]{:S(2)}) collective-permute-start(f32[80,512]{1,0:T(8,128)S(1)} %get-tuple-element.61), channel_id=1, source_target_pairs={{0,8},{1,2},{2,1},{3,11},{8,0},{9,10},{10,9},{11,3},{16,24},{17,18... | collective-permute-start | bytes 491528 | tf_op jit(solution)/shard_map/ppermute | solution.py:75
  5.4 0.0 collective-permute-start.1
  5.5 1.5 %collective-permute-start.2 = (f32[2,32,512]{2,1,0:T(8,128)S(1)}, f32[2,32,512]{2,1,0:T(8,128)S(1)}, u32[]{:S(2)}, u32[]{:S(2)}) collective-permute-start(f32[2,32,512]{2,1,0:T(8,128)S(1)} %get-tuple-element.69), channel_id=1, source_target_pairs={{0,4},{4,0},{1,5},{5,1},{2,6},{6,2},{3,7},{7,3},{8,12},{12,8},{9,1... | collective-permute-start | bytes 393224 | tf_op jit(solution)/shard_map/ppermute | solution.py:64
  7.6 0.0 copy-done.1
  7.7 1.1 %own_state.1 = (f32[9,4,32,512]{3,2,1,0:T(8,128)S(1)}, bf16[3,1,2,4,32,512]{5,4,3,2,1,0:T(8,128)(2,1)S(1)}) custom-call(f32[4,32,512]{2,1,0:T(8,128)S(1)} %get-tuple-element.53.refs_0_, f32[4,32,512]{2,1,0:T(8,128)S(1)} %get-tuple-element.54.refs_1_, f32[4,32,512]{2,1,0:T(8,128)S(1)} %get-tuple-element.55.refs_2_, ...), custom_call_target="tpu_custom_call" | custom-call | flops 3000000 | bytes 375000 | tf_op jit(solution)/shard_map/own_state/pallas_call | solution.py:35
  8.8 0.0 copy-done
  8.8 0.5 %surface_load.1.refs_2_.refs_6_.refs_9_.refs_8_.refs_7_ = f32[3,4,40,128]{3,2,1,0:T(8,128)S(1)} custom-call(s32[1,1536]{1,0:T(1,128)S(1)} %copy-done, s32[1]{0:T(128)S(6)} %copy.16.refs_1_, f32[1,3,1536]{2,1,0:T(4,128)S(1)} %copy.15.refs_2_, f32[9,4,32,512]{3,2,1,0:T(8,128)S(1)} %get-tuple-element.58.refs_3_.refs_0_.refs_1_), custom_call_target="tpu_custom_call" | custom-call | flops 2000000 | bytes 250000 | tf_op jit(solution)/shard_map/surface_load/pallas_call | solution.py:35
  9.3 0.0 collective-permute-done.refs_0_
  9.3 0.0 collective-permute-done.1.refs_1_
  9.4 1.4 %collective-permute-start.3 = (f32[2,8,512]{2,1,0:T(8,128)S(1)}, f32[2,8,512]{2,1,0:T(8,128)S(1)}, u32[]{:S(2)}, u32[]{:S(2)}) collective-permute-start(f32[2,8,512]{2,1,0:T(8,128)S(1)} %halo_edges.1.refs_2_), channel_id=1, source_target_pairs={{0,4},{4,0},{1,5},{5,1},{2,6},{6,2},{3,7},{7,3},{8,12},{12,8},{9,1... | collective-permute-start | bytes 98312 | tf_op jit(solution)/shard_map/ppermute | solution.py:64
  10.8 0.3 halo_state.1
  11.1 2.2 %bulk_0.1 = (f32[2,40,512]{2,1,0:T(8,128)S(1)}, f32[4,3,32,128]{3,2,1,0:T(8,128)}, f32[2,40,512]{2,1,0:T(8,128)S(1)}, f32[4,3,32,128]{3,2,1,0:T(8,128)}, f32[2,4...) custom-call(f32[9,4,32,512]{3,2,1,0:T(8,128)S(1)} %get-tuple-element, ...), custom_call_target="tpu_custom_call" | custom-call | flops 10100000 | bytes 1262500 | tf_op jit(solution)/shard_map/bulk_0/pallas_call | solution.py:35
  13.3 0.0 collective-permute-done.2.refs_5_
  13.3 0.0 collective-permute-done.3.refs_6_
  13.4 0.3 front_1.1
  13.7 1.4 %collective-permute-start.4 = (f32[72,512]{1,0:T(8,128)S(1)}, f32[72,512]{1,0:T(8,128)S(1)}, u32[]{:S(2)}, u32[]{:S(2)}) collective-permute-start(f32[72,512]{1,0:T(8,128)S(1)} %get-tuple-element.79), channel_id=1, source_target_pairs={{0,4},{4,0},{1,5},{5,1},{2,6},{6,2},{3,7},{7,3},{8,12},{12,8},{9,1... | collective-permute-start | bytes 442376 | tf_op jit(solution)/shard_map/ppermute | solution.py:64
  15.1 0.9 %bulk_1.1 = (f32[2,40,512]{2,1,0:T(8,128)S(1)}, f32[4,3,32,128]{3,2,1,0:T(8,128)S(1)}, f32[2,32,512]{2,1,0:T(8,128)S(1)}, f32[2,32,512]{2,1,0:T(8,128)S(1)}, f32...) custom-call(f32[9,4,32,512]{3,2,1,0:T(8,128)S(1)} %get-tuple-element.58.refs_3_.refs_0_.refs_1_, ...), custom_call_target="tpu_custom_call" | custom-call | flops 6100000 | bytes 762500 | tf_op jit(solution)/shard_map/bulk_1/pallas_call | solution.py:35
  16.0 1.6 %collective-permute-start.5 = (f32[2,2,3,32,128]{4,3,2,1,0:T(8,128)S(1)}, f32[2,2,3,32,128]{4,3,2,1,0:T(8,128)S(1)}, u32[]{:S(2)}, u32[]{:S(2)}) collective-permute-start(f32[2,2,3,32,128]{4,3,2,1,0:T(8,128)S(1)} %get-tuple-element.85), channel_id=1, source_target_pairs={{0,8},{8,0},{16,24},{24,16},{1,9},{9,1},{17,25},{25,17},{2,10},{10... | collective-permute-start | bytes 589832 | tf_op jit(solution)/shard_map/ppermute | solution.py:566
  17.7 1.3 %collective-permute-done.4.refs_5_ = f32[72,512]{1,0:T(8,128)S(1)} collective-permute-done((f32[72,512]{1,0:T(8,128)S(1)}, f32[72,512]{1,0:T(8,128)S(1)}, u32[]{:S(2)}, u32[]{:S(2)}) %collective-permute-start.4) | collective-permute-done | bytes 147488 | tf_op jit(solution)/shard_map/ppermute | solution.py:64
  18.9 0.3 front_2.1
  19.3 1.4 %collective-permute-start.6 = (f32[72,512]{1,0:T(8,128)S(1)}, f32[72,512]{1,0:T(8,128)S(1)}, u32[]{:S(2)}, u32[]{:S(2)}) collective-permute-start(f32[72,512]{1,0:T(8,128)S(1)} %get-tuple-element.87), channel_id=1, source_target_pairs={{0,4},{4,0},{1,5},{5,1},{2,6},{6,2},{3,7},{7,3},{8,12},{12,8},{9,1... | collective-permute-start | bytes 442376 | tf_op jit(solution)/shard_map/ppermute | solution.py:64
  20.7 0.3 bulk_2.1
  21.0 1.6 %collective-permute-start.7 = (f32[2,1,3,32,128]{4,3,2,1,0:T(8,128)S(1)}, f32[2,1,3,32,128]{4,3,2,1,0:T(8,128)S(1)}, u32[]{:S(2)}, u32[]{:S(2)}) collective-permute-start(f32[2,1,3,32,128]{4,3,2,1,0:T(8,128)S(1)} %get-tuple-element.92), channel_id=1, source_target_pairs={{0,8},{8,0},{16,24},{24,16},{1,9},{9,1},{17,25},{25,17},{2,10},{10... | collective-permute-start | bytes 294920 | tf_op jit(solution)/shard_map/ppermute | solution.py:566
  22.6 0.0 collective-permute-done.5.refs_2_
  22.7 2.7 %collective-permute-start.9 = (f32[2,3,32,128]{3,2,1,0:T(8,128)S(1)}, f32[2,3,32,128]{3,2,1,0:T(8,128)S(1)}, u32[]{:S(2)}, u32[]{:S(2)}) collective-permute-start(f32[2,3,32,128]{3,2,1,0:T(8,128)S(1)} %get-tuple-element.86.refs_0_), channel_id=1, source_target_pairs={{0,16},{8,24},{16,0},{24,8},{1,17},{9,25},{17,1},{25,9},{2,18},{10... | collective-permute-start | bytes 294920 | tf_op jit(solution)/shard_map/ppermute | solution.py:566
  25.3 0.0 collective-permute-done.6.refs_5_
  25.3 0.3 front_3.1
  25.6 0.0 collective-permute-done.7.refs_3_
  25.7 3.8 %collective-permute-start.8 = (f32[2,3,32,128]{3,2,1,0:T(8,128)S(1)}, f32[2,3,32,128]{3,2,1,0:T(8,128)S(1)}, u32[]{:S(2)}, u32[]{:S(2)}) collective-permute-start(f32[2,3,32,128]{3,2,1,0:T(8,128)S(1)} %get-tuple-element.93), channel_id=1, source_target_pairs={{0,24},{8,16},{16,8},{24,0},{1,25},{9,17},{17,9},{25,1},{2,26},{10... | collective-permute-start | bytes 294920 | tf_op jit(solution)/shard_map/ppermute | solution.py:566
  29.5 0.0 collective-permute-start.10
  29.5 0.6 %collective-permute-start.11 = (f32[1,3,32,128]{3,2,1,0:T(8,128)S(1)}, f32[1,3,32,128]{3,2,1,0:T(8,128)S(1)}, u32[]{:S(2)}, u32[]{:S(2)}) collective-permute-start(f32[1,3,32,128]{3,2,1,0:T(8,128)S(1)} %get-tuple-element.95), channel_id=1, source_target_pairs={{0,8},{8,0},{16,24},{24,16},{1,9},{9,1},{17,25},{25,17},{2,10},{10... | collective-permute-start | bytes 147464 | tf_op jit(solution)/shard_map/ppermute | solution.py:566
  30.2 0.8 %final_fields.1 = f32[1,2,4,32,512]{4,3,2,1,0:T(8,128)} custom-call(f32[2,32,512]{2,1,0:T(8,128)S(1)} %get-tuple-element.76.refs_0_, f32[2,32,512]{2,1,0:T(8,128)S(1)} %get-tuple-element.77.refs_1_, f32[2,32,512]{2,1,0:T(8,128)S(1)} %get-tuple-element.83.refs_0_.refs_2_, f32[2,32,512]{2,1,0:T(8,128)S(1)} %get-tuple-element.89.refs_3_.refs_0_), custom_call_target="tpu_custom_call" | custom-call | flops 1000000 | bytes 125000 | tf_op jit(solution)/shard_map/final_fields/pallas_call | solution.py:35
  31.0 1.8 %collective-permute-done.9.refs_5_ = f32[2,3,32,128]{3,2,1,0:T(8,128)S(1)} collective-permute-done((f32[2,3,32,128]{3,2,1,0:T(8,128)S(1)}, f32[2,3,32,128]{3,2,1,0:T(8,128)S(1)}, u32[]{:S(2)}, u32[]{:S(2)}) %collective-permute-start.9) | collective-permute-done | bytes 98336 | tf_op jit(solution)/shard_map/ppermute | solution.py:566
  32.8 2.2 %collective-permute-done.10.refs_6_ = f32[1,3,32,128]{3,2,1,0:T(8,128)S(1)} collective-permute-done((f32[1,3,32,128]{3,2,1,0:T(8,128)S(1)}, f32[1,3,32,128]{3,2,1,0:T(8,128)S(1)}, u32[]{:S(2)}, u32[]{:S(2)}) %collective-permute-start.10) | collective-permute-done | bytes 49184 | tf_op jit(solution)/shard_map/ppermute | solution.py:566
  35.0 0.0 collective-permute-done.11.refs_7_
  35.0 0.0 collective-permute-done.8.refs_3_.refs_4_
  35.0 0.7 %combine.1 = (f32[4,32,128]{2,1,0:T(8,128)}, f32[4,32,128]{2,1,0:T(8,128)}, f32[4,32,128]{2,1,0:T(8,128)}) custom-call(f32[4,32,512]{2,1,0:T(8,128)S(1)} %get-tuple-element.53.refs_0_, f32[4,32,512]{2,1,0:T(8,128)S(1)} %get-tuple-element.54.refs_1_, f32[4,32,512]{2,1,0:T(8,128)S(1)} %get-tuple-element.55.refs_2_, ...), custom_call_target="tpu_custom_call" | custom-call | flops 1000000 | bytes 125000 | tf_op jit(solution)/shard_map/combine/pallas_call | solution.py:35
  (4 shorter events, 0.1 us)
Async XLA Ops:
  0.6 7.0 %copy-start.1 = (f32[1,3,1536]{2,0,1:T(1,128)S(1)}, f32[1,3,1536]{2,0,1:T(1,128)}, u32[]{:S(2)}) copy-start(f32[1,3,1536]{2,0,1:T(1,128)} %param.21) | copy-start | bytes 55300
  0.6 8.2 %copy-start = (s32[1,1536]{1,0:T(1,128)S(1)}, s32[1,1536]{1,0:T(1,128)}, u32[]{:S(2)}) copy-start(s32[1,1536]{1,0:T(1,128)} %refs_0_.3) | copy-start | bytes 18436
  2.3 7.0 %collective-permute-start = (f32[80,512]{1,0:T(8,128)S(1)}, f32[80,512]{1,0:T(8,128)S(1)}, u32[]{:S(2)}, u32[]{:S(2)}) collective-permute-start(f32[80,512]{1,0:T(8,128)S(1)} %get-tuple-element.61), channel_id=1, source_target_pairs={{0,8},{1,2},{2,1},{3,11},{8,0},{9,10},{10,9},{11,3},{16,24},{17,18... | collective-permute-start | bytes 491528 | tf_op jit(solution)/shard_map/ppermute | solution.py:75
  5.4 3.9 %collective-permute-start.1 = (f32[80,512]{1,0:T(8,128)S(1)}, f32[80,512]{1,0:T(8,128)S(1)}, u32[]{:S(2)}, u32[]{:S(2)}) collective-permute-start(f32[80,512]{1,0:T(8,128)S(1)} %get-tuple-element.62), channel_id=1, source_target_pairs={{0,1},{1,0},{2,3},{3,2},{8,9},{9,8},{10,11},{11,10},{16,17},{17,16... | collective-permute-start | bytes 491528 | tf_op jit(solution)/shard_map/ppermute | solution.py:75
  5.5 7.9 %collective-permute-start.2 = (f32[2,32,512]{2,1,0:T(8,128)S(1)}, f32[2,32,512]{2,1,0:T(8,128)S(1)}, u32[]{:S(2)}, u32[]{:S(2)}) collective-permute-start(f32[2,32,512]{2,1,0:T(8,128)S(1)} %get-tuple-element.69), channel_id=1, source_target_pairs={{0,4},{4,0},{1,5},{5,1},{2,6},{6,2},{3,7},{7,3},{8,12},{12,8},{9,1... | collective-permute-start | bytes 393224 | tf_op jit(solution)/shard_map/ppermute | solution.py:64
  9.4 4.0 %collective-permute-start.3 = (f32[2,8,512]{2,1,0:T(8,128)S(1)}, f32[2,8,512]{2,1,0:T(8,128)S(1)}, u32[]{:S(2)}, u32[]{:S(2)}) collective-permute-start(f32[2,8,512]{2,1,0:T(8,128)S(1)} %halo_edges.1.refs_2_), channel_id=1, source_target_pairs={{0,4},{4,0},{1,5},{5,1},{2,6},{6,2},{3,7},{7,3},{8,12},{12,8},{9,1... | collective-permute-start | bytes 98312 | tf_op jit(solution)/shard_map/ppermute | solution.py:64
  13.7 5.2 %collective-permute-start.4 = (f32[72,512]{1,0:T(8,128)S(1)}, f32[72,512]{1,0:T(8,128)S(1)}, u32[]{:S(2)}, u32[]{:S(2)}) collective-permute-start(f32[72,512]{1,0:T(8,128)S(1)} %get-tuple-element.79), channel_id=1, source_target_pairs={{0,4},{4,0},{1,5},{5,1},{2,6},{6,2},{3,7},{7,3},{8,12},{12,8},{9,1... | collective-permute-start | bytes 442376 | tf_op jit(solution)/shard_map/ppermute | solution.py:64
  16.0 6.6 %collective-permute-start.5 = (f32[2,2,3,32,128]{4,3,2,1,0:T(8,128)S(1)}, f32[2,2,3,32,128]{4,3,2,1,0:T(8,128)S(1)}, u32[]{:S(2)}, u32[]{:S(2)}) collective-permute-start(f32[2,2,3,32,128]{4,3,2,1,0:T(8,128)S(1)} %get-tuple-element.85), channel_id=1, source_target_pairs={{0,8},{8,0},{16,24},{24,16},{1,9},{9,1},{17,25},{25,17},{2,10},{10... | collective-permute-start | bytes 589832 | tf_op jit(solution)/shard_map/ppermute | solution.py:566
  19.3 6.1 %collective-permute-start.6 = (f32[72,512]{1,0:T(8,128)S(1)}, f32[72,512]{1,0:T(8,128)S(1)}, u32[]{:S(2)}, u32[]{:S(2)}) collective-permute-start(f32[72,512]{1,0:T(8,128)S(1)} %get-tuple-element.87), channel_id=1, source_target_pairs={{0,4},{4,0},{1,5},{5,1},{2,6},{6,2},{3,7},{7,3},{8,12},{12,8},{9,1... | collective-permute-start | bytes 442376 | tf_op jit(solution)/shard_map/ppermute | solution.py:64
  21.0 4.7 %collective-permute-start.7 = (f32[2,1,3,32,128]{4,3,2,1,0:T(8,128)S(1)}, f32[2,1,3,32,128]{4,3,2,1,0:T(8,128)S(1)}, u32[]{:S(2)}, u32[]{:S(2)}) collective-permute-start(f32[2,1,3,32,128]{4,3,2,1,0:T(8,128)S(1)} %get-tuple-element.92), channel_id=1, source_target_pairs={{0,8},{8,0},{16,24},{24,16},{1,9},{9,1},{17,25},{25,17},{2,10},{10... | collective-permute-start | bytes 294920 | tf_op jit(solution)/shard_map/ppermute | solution.py:566
  22.7 10.1 %collective-permute-start.9 = (f32[2,3,32,128]{3,2,1,0:T(8,128)S(1)}, f32[2,3,32,128]{3,2,1,0:T(8,128)S(1)}, u32[]{:S(2)}, u32[]{:S(2)}) collective-permute-start(f32[2,3,32,128]{3,2,1,0:T(8,128)S(1)} %get-tuple-element.86.refs_0_), channel_id=1, source_target_pairs={{0,16},{8,24},{16,0},{24,8},{1,17},{9,25},{17,1},{25,9},{2,18},{10... | collective-permute-start | bytes 294920 | tf_op jit(solution)/shard_map/ppermute | solution.py:566
  25.7 9.3 %collective-permute-start.8 = (f32[2,3,32,128]{3,2,1,0:T(8,128)S(1)}, f32[2,3,32,128]{3,2,1,0:T(8,128)S(1)}, u32[]{:S(2)}, u32[]{:S(2)}) collective-permute-start(f32[2,3,32,128]{3,2,1,0:T(8,128)S(1)} %get-tuple-element.93), channel_id=1, source_target_pairs={{0,24},{8,16},{16,8},{24,0},{1,25},{9,17},{17,9},{25,1},{2,26},{10... | collective-permute-start | bytes 294920 | tf_op jit(solution)/shard_map/ppermute | solution.py:566
  29.5 5.5 %collective-permute-start.10 = (f32[1,3,32,128]{3,2,1,0:T(8,128)S(1)}, f32[1,3,32,128]{3,2,1,0:T(8,128)S(1)}, u32[]{:S(2)}, u32[]{:S(2)}) collective-permute-start(f32[1,3,32,128]{3,2,1,0:T(8,128)S(1)} %get-tuple-element.94), channel_id=1, source_target_pairs={{0,16},{8,24},{16,0},{24,8},{1,17},{9,25},{17,1},{25,9},{2,18},{10... | collective-permute-start | bytes 147464 | tf_op jit(solution)/shard_map/ppermute | solution.py:566
  29.5 5.5 %collective-permute-start.11 = (f32[1,3,32,128]{3,2,1,0:T(8,128)S(1)}, f32[1,3,32,128]{3,2,1,0:T(8,128)S(1)}, u32[]{:S(2)}, u32[]{:S(2)}) collective-permute-start(f32[1,3,32,128]{3,2,1,0:T(8,128)S(1)} %get-tuple-element.95), channel_id=1, source_target_pairs={{0,8},{8,0},{16,24},{24,16},{1,9},{9,1},{17,25},{25,17},{2,10},{10... | collective-permute-start | bytes 147464 | tf_op jit(solution)/shard_map/ppermute | solution.py:566

commit v6 on v5

--- a/solution.py
+++ b/solution.py
@@ -371,8 +371,12 @@
             last = t == tile.steps - 1
             for key in ("w", "forward"):
                 self.need(key)
+            if ("part", t, m) in self.state:
+                self.need(("part", t, m))
             for k in (m - 1, m, m + 1):
                 if k == -1 and not tile.far:
+                    continue
+                if k == m - 1 and ("part", t, m) in self.state:
                     continue
                 if k in (-1, tile.nx):
                     key = "xf" if k == -1 else "xn"
@@ -464,77 +468,91 @@
             [ref[0, c, tile.place(m), :, lanes], r["uh"][item, m, :, lanes]], axis=0
         )
 
+    def operators(self, r, t, m, rows, weight, local, above):
+        tile = self.tile
+        lane = lax.broadcasted_iota(jnp.int32, (tile.rows, LANES), 1)
+        at_first, at_last = lane == 0, lane == LANES - 1
+
+        def deeper(blocks):
+            moved = [rolled(block, -1, 1) for block in blocks] + [0.0]
+            return [jnp.where(at_last, moved[j + 1], moved[j]) for j in range(tile.nj)]
+
+        def shallower(blocks):
+            moved = [rolled(block, 1, 1) for block in blocks] + [0.0]
+            return [jnp.where(at_first, moved[j - 1], moved[j]) for j in range(tile.nj)]
+
+        def both(block):
+            return rolled(block, -1, 0)[:rows], rolled(block, 1, 0)[:rows]
+
+        centers, halves, shifted = [], [], []
+        for c in range(2):
+            total_x, diff_x = [], []
+            for j in range(tile.nj):
+                up = self.field(r, t, m + 1, c, j) if above else None
+                down = self.field(r, t, m - 1, c, j) if local else None
+                if down is None:
+                    total_x.append(up)
+                    diff_x.append(up)
+                else:
+                    total_x.append(down if up is None else up + down)
+                    diff_x.append(-down if up is None else up - down)
+            halves.append((total_x, diff_x))
+            moved = [deeper(diff_x), shallower(diff_x)]
+            if local:
+                centers.append([self.field(r, t, m, c, j) for j in range(tile.nj)])
+                moved += [deeper(centers[c]), shallower(centers[c])]
+            shifted.append(moved)
+
+        for j in range(tile.nj):
+            weights = [weight(k, j) for k in range(6)]
+            results = []
+            for c in range(2):
+                total_x, diff_x = halves[c][0][j][:rows], halves[c][1][j]
+                mixed_xz = (shifted[c][0][j] - shifted[c][1][j])[:rows]
+                up, down = both(diff_x)
+                axial = weights[0] * total_x + weights[3] * (up - down) + weights[5] * mixed_xz
+                laplace = total_x
+                if local:
+                    center = centers[c][j]
+                    below, above_z = shifted[c][2][j], shifted[c][3][j]
+                    total_z, slope_z = (below + above_z)[:rows], below - above_z
+                    up, down = both(center)
+                    total_y = up + down
+                    up, down = both(slope_z)
+                    axial = axial + (
+                        weights[1] * total_y + weights[2] * total_z + weights[4] * (up - down)
+                    )
+                    center = center[:rows]
+                    laplace = laplace + total_y + total_z - 4.0 * center
+                    results.append(laplace - axial if c == 0 else axial - 2.0 * center)
+                else:
+                    results.append(laplace - axial if c == 0 else axial)
+            yield results
+
+    def weight_of(self, r, m, last):
+        def weight(k, j):
+            own = r["w"][k, m, :, lanes_of(j)]
+            return own if last else jnp.concatenate([own, r["wh"][k, m, :, lanes_of(j)]], axis=0)
+
+        return weight
+
     def update(self, r, t, m):
         tile = self.tile
         last = t == tile.steps - 1
         rows = tile.ny if last else tile.rows
-        lane = lax.broadcasted_iota(jnp.int32, (tile.rows, LANES), 1)
-        at_first, at_last = lane == 0, lane == LANES - 1
-
-        def weight(k, j):
-            own = r["w"][k, m, :, lanes_of(j)]
-            return own if last else jnp.concatenate([own, r["wh"][k, m, :, lanes_of(j)]], axis=0)
-
-        centers, halves = [], []
-        for c in range(2):
-            center = [self.field(r, t, m, c, j) for j in range(tile.nj)]
-            total_x, diff_x = [], []
-            for j in range(tile.nj):
-                above, below = self.field(r, t, m + 1, c, j), self.field(r, t, m - 1, c, j)
-                total_x.append(above if below is None else above + below)
-                diff_x.append(above if below is None else above - below)
-            centers.append(center)
-            halves.append((total_x, diff_x))
-
-        def deeper(blocks):
-            moved = [rolled(block, -1, 1) for block in blocks] + [0.0]
-            return [jnp.where(at_last, moved[j + 1], moved[j]) for j in range(tile.nj)]
-
-        def shallower(blocks):
-            moved = [rolled(block, 1, 1) for block in blocks] + [0.0]
-            return [jnp.where(at_first, moved[j - 1], moved[j]) for j in range(tile.nj)]
-
-        shifted = []
-        for c in range(2):
-            diff_x = halves[c][1]
-            shifted.append(
-                (deeper(centers[c]), shallower(centers[c]), deeper(diff_x), shallower(diff_x))
-            )
-
-        def both(block):
-            return rolled(block, -1, 0)[:rows], rolled(block, 1, 0)[:rows]
-
+        weight = self.weight_of(r, m, last)
+        ahead = ("part", t, m) in r
+        spatial = self.operators(r, t, m, rows, weight, not ahead, True)
         for j in range(tile.nj):
-            weights = [weight(k, j) for k in range(6)]
-            results = []
-            for c in range(2):
-                center = centers[c][j]
-                total_x, diff_x = halves[c][0][j], halves[c][1][j]
-                below, above, diff_below, diff_above = (part[j] for part in shifted[c])
-                total_z, slope_z = (below + above)[:rows], below - above
-                mixed_xz = (diff_below - diff_above)[:rows]
-                up, down = both(center)
-                total_y = up + down
-                up, down = both(diff_x)
-                mixed_xy = up - down
-                up, down = both(slope_z)
-                mixed_yz = up - down
-                total_x, center = total_x[:rows], center[:rows]
-                axial = (
-                    weights[0] * total_x + weights[1] * total_y + weights[2] * total_z
-                    + weights[3] * mixed_xy + weights[4] * mixed_yz + weights[5] * mixed_xz
-                )
-                if c == 0:
-                    results.append(total_x + total_y + total_z - 4.0 * center - axial)
-                else:
-                    results.append(axial - 2.0 * center)
-            horiz, axial = results
+            horiz, axial = next(spatial)
+            if ahead:
+                horiz = horiz + r[("part", t, m)][0, :, lanes_of(j)]
+                axial = axial + r[("part", t, m)][1, :, lanes_of(j)]
+            centers = [self.field(r, t, m, c, j)[:rows] for c in range(2)]
             stretched, rooted, speed_sq = (weight(k, j) for k in range(6, 9))
             before = [self.field(r, t - 1, m, c, j)[:rows] for c in range(2)]
-            new_p = (
-                2.0 * centers[0][j][:rows] - before[0] + stretched * horiz + rooted * axial
-            )
-            new_q = 2.0 * centers[1][j][:rows] - before[1] + rooted * horiz + speed_sq * axial
+            new_p = 2.0 * centers[0] - before[0] + stretched * horiz + rooted * axial
+            new_q = 2.0 * centers[1] - before[1] + rooted * horiz + speed_sq * axial
             if j == 0:
                 new_p = new_p + r["surface"][t, m][:rows]
             r[("u", t + 1, m)][0, :, lanes_of(j)] = new_p
@@ -560,6 +578,27 @@
                 if t > 0:
                     term = term + r[("g", t - 1, m)][j, k]
                 r[("g", t, m)][j, k] = term
+
+
+def run_ahead(tile, state, ops, name):
+    stage = Stage(tile, state, [], [], name)
+    ins, outs = {"w": state["w"], "wh": state["wh"]}, {}
+    for t, m in ops:
+        for k in (m - 1, m):
+            ins[("u", t, k)] = state[("u", t, k)]
+        rows = tile.ny if t == tile.steps - 1 else tile.rows
+        outs[("part", t, m)] = (2, rows, tile.nz)
+
+    def body(r):
+        for t, m in ops:
+            last = t == tile.steps - 1
+            rows = tile.ny if last else tile.rows
+            spatial = stage.operators(r, t, m, rows, stage.weight_of(r, m, last), True, False)
+            for j, (horiz, axial) in enumerate(spatial):
+                r[("part", t, m)][0, :, lanes_of(j)] = horiz
+                r[("part", t, m)][1, :, lanes_of(j)] = axial
+
+    state.update(run_kernel(body, ins, outs, name=name, flops=10**6))
 
 
 def xor_swap(tile, block, k):
@@ -721,6 +760,8 @@
             for k in range(tile.src - 1, 0, -1):
                 if k not in joined:
                     state[("r", planes, k)] = (xor_swap(tile, state[("s", planes, k)], k), 0)
+        if phase == 1 and not tile.far and tile.steps == 3:
+            run_ahead(tile, state, [(1, tile.nx - 1), (2, tile.nx - 2)], "ahead")
         for name, k in later:
             group = [planes for planes in pieces if tile.plan[planes][1] == name]
             along = direct[0] if k in joined else None

time: 35.9 us -> 35.9 us (level)
  waiting for transfers between devices: 5.32 us -> 4.96 us
    ppermute x4, waiting for transfers between devices: 1.3 us -> 0.9 us  [swap(): return lax.ppermute(block, axis, pair_swaps(count, first))]
    pallas_call x15 -> x16, Pallas kernels: 9.68 us -> 9.85 us  [run_kernel(): pl.pallas_call(kernel, name=name, out_shape=[jax.ShapeDtypeStruct(shape,...]
  transfers between devices with their start and end apart: 12 -> 12, of which waited for: 3 -> 4; matrix products, arithmetic and copies ran while one was open for 0% -> 0% of each run, Pallas kernels for 19% -> 20%
where the time goes in v6:
time: 35.9 us; the launch traced here: 35.7 us
  starting transfers between devices  19.5 us (54%)
  Pallas kernels  9.85 us (27%)
  waiting for transfers between devices  4.96 us (14%)
  between operations  1.45 us (4%)
    ppermute x6, starting transfers between devices, xor_swap(): return lax.ppermute(block, 'src', [(i, i ^ k) for i in range(tile.src)])  10.6 us
    pallas_call x16, Pallas kernels, run_kernel(): pl.pallas_call(kernel, name=name, out_shape=[jax.ShapeDtypeStruct(shape,...  9.85 us
    ppermute x4, starting transfers between devices, swap(): return lax.ppermute(block, axis, pair_swaps(count, first))  5.73 us
    ppermute x6, waiting for transfers between devices, xor_swap(): return lax.ppermute(block, 'src', [(i, i ^ k) for i in range(tile.src)])  4.06 us
    ppermute x2, starting transfers between devices, swap_rows(): return lax.ppermute(block, ('src', 'gy'), joint)  3.12 us
    ppermute x4, waiting for transfers between devices, swap(): return lax.ppermute(block, axis, pair_swaps(count, first))  0.9 us
  transfers between devices with their start and end apart: 12, of which 4 were waited for; matrix products, arithmetic and copies ran while one was open for 0% of the time, Pallas kernels for 20%

profile of v6, /device:TPU:0, one launch (start us, length us, event | category | flops | bytes accessed | tf_op | source)
XLA Modules:
  0.0 35.7 jit_solution(17745907014786584132)
XLA Ops:
  0.6 0.0 copy-start.1
  0.6 0.0 copy-start
  0.7 1.7 %pack_edges.1 = (f32[80,512]{1,0:T(8,128)S(1)}, f32[80,512]{1,0:T(8,128)S(1)}, f32[2,32,512]{2,1,0:T(8,128)S(1)}, f32[1,2,4,32,512]{4,3,2,1,0:T(8,128)S(1)}, f32...) custom-call(f32[1,2,4,32,512]{4,3,2,1,0:T(8,128)} %refs_0_.2, ...), custom_call_target="tpu_custom_call" | custom-call | flops 1000000 | bytes 125000 | tf_op jit(solution)/shard_map/pack_edges/pallas_call | solution.py:35
  2.3 3.1 %collective-permute-start = (f32[80,512]{1,0:T(8,128)S(1)}, f32[80,512]{1,0:T(8,128)S(1)}, u32[]{:S(2)}, u32[]{:S(2)}) collective-permute-start(f32[80,512]{1,0:T(8,128)S(1)} %get-tuple-element.63), channel_id=1, source_target_pairs={{0,8},{1,2},{2,1},{3,11},{8,0},{9,10},{10,9},{11,3},{16,24},{17,18... | collective-permute-start | bytes 491528 | tf_op jit(solution)/shard_map/ppermute | solution.py:75
  5.4 0.0 collective-permute-start.1
  5.5 1.5 %collective-permute-start.2 = (f32[2,32,512]{2,1,0:T(8,128)S(1)}, f32[2,32,512]{2,1,0:T(8,128)S(1)}, u32[]{:S(2)}, u32[]{:S(2)}) collective-permute-start(f32[2,32,512]{2,1,0:T(8,128)S(1)} %get-tuple-element.71), channel_id=1, source_target_pairs={{0,4},{4,0},{1,5},{5,1},{2,6},{6,2},{3,7},{7,3},{8,12},{12,8},{9,1... | collective-permute-start | bytes 393224 | tf_op jit(solution)/shard_map/ppermute | solution.py:64
  7.6 0.0 copy-done.1
  7.7 1.1 %own_state.1 = (f32[9,4,32,512]{3,2,1,0:T(8,128)S(1)}, bf16[3,1,2,4,32,512]{5,4,3,2,1,0:T(8,128)(2,1)S(1)}) custom-call(f32[4,32,512]{2,1,0:T(8,128)S(1)} %get-tuple-element.55.refs_0_, f32[4,32,512]{2,1,0:T(8,128)S(1)} %get-tuple-element.56.refs_1_, f32[4,32,512]{2,1,0:T(8,128)S(1)} %get-tuple-element.57.refs_2_, ...), custom_call_target="tpu_custom_call" | custom-call | flops 3000000 | bytes 375000 | tf_op jit(solution)/shard_map/own_state/pallas_call | solution.py:35
  8.8 0.0 copy-done
  8.8 0.5 %surface_load.1.refs_2_.refs_6_.refs_9_.refs_8_.refs_7_ = f32[3,4,40,128]{3,2,1,0:T(8,128)S(1)} custom-call(s32[1,1536]{1,0:T(1,128)S(1)} %copy-done, s32[1]{0:T(128)S(6)} %copy.16.refs_1_, f32[1,3,1536]{2,1,0:T(4,128)S(1)} %copy.15.refs_2_, f32[9,4,32,512]{3,2,1,0:T(8,128)S(1)} %get-tuple-element.60.refs_3_.refs_0_.refs_1_), custom_call_target="tpu_custom_call" | custom-call | flops 2000000 | bytes 250000 | tf_op jit(solution)/shard_map/surface_load/pallas_call | solution.py:35
  9.3 0.0 collective-permute-done.refs_0_
  9.3 0.0 collective-permute-done.1.refs_1_
  9.4 1.4 %collective-permute-start.3 = (f32[2,8,512]{2,1,0:T(8,128)S(1)}, f32[2,8,512]{2,1,0:T(8,128)S(1)}, u32[]{:S(2)}, u32[]{:S(2)}) collective-permute-start(f32[2,8,512]{2,1,0:T(8,128)S(1)} %halo_edges.1.refs_2_), channel_id=1, source_target_pairs={{0,4},{4,0},{1,5},{5,1},{2,6},{6,2},{3,7},{7,3},{8,12},{12,8},{9,1... | collective-permute-start | bytes 98312 | tf_op jit(solution)/shard_map/ppermute | solution.py:64
  10.8 0.3 halo_state.1
  11.1 2.1 %bulk_0.1 = (f32[2,40,512]{2,1,0:T(8,128)S(1)}, f32[4,3,32,128]{3,2,1,0:T(8,128)}, f32[2,40,512]{2,1,0:T(8,128)S(1)}, f32[4,3,32,128]{3,2,1,0:T(8,128)}, f32[2,4...) custom-call(f32[9,4,32,512]{3,2,1,0:T(8,128)S(1)} %get-tuple-element, ...), custom_call_target="tpu_custom_call" | custom-call | flops 10100000 | bytes 1262500 | tf_op jit(solution)/shard_map/bulk_0/pallas_call | solution.py:35
  13.3 0.0 collective-permute-done.2.refs_5_
  13.3 0.1 collective-permute-done.3.refs_6_
  13.4 0.3 front_1.1
  13.7 1.4 %collective-permute-start.4 = (f32[72,512]{1,0:T(8,128)S(1)}, f32[72,512]{1,0:T(8,128)S(1)}, u32[]{:S(2)}, u32[]{:S(2)}) collective-permute-start(f32[72,512]{1,0:T(8,128)S(1)} %get-tuple-element.83), channel_id=1, source_target_pairs={{0,4},{4,0},{1,5},{5,1},{2,6},{6,2},{3,7},{7,3},{8,12},{12,8},{9,1... | collective-permute-start | bytes 442376 | tf_op jit(solution)/shard_map/ppermute | solution.py:64
  15.1 0.9 %bulk_1.1 = (f32[2,40,512]{2,1,0:T(8,128)S(1)}, f32[4,3,32,128]{3,2,1,0:T(8,128)S(1)}, f32[2,32,512]{2,1,0:T(8,128)S(1)}, f32[2,32,512]{2,1,0:T(8,128)S(1)}, f32...) custom-call(f32[9,4,32,512]{3,2,1,0:T(8,128)S(1)} %get-tuple-element.60.refs_3_.refs_0_.refs_1_, ...), custom_call_target="tpu_custom_call" | custom-call | flops 6100000 | bytes 762500 | tf_op jit(solution)/shard_map/bulk_1/pallas_call | solution.py:35
  16.0 1.6 %collective-permute-start.5 = (f32[2,2,3,32,128]{4,3,2,1,0:T(8,128)S(1)}, f32[2,2,3,32,128]{4,3,2,1,0:T(8,128)S(1)}, u32[]{:S(2)}, u32[]{:S(2)}) collective-permute-start(f32[2,2,3,32,128]{4,3,2,1,0:T(8,128)S(1)} %get-tuple-element.89), channel_id=1, source_target_pairs={{0,8},{8,0},{16,24},{24,16},{1,9},{9,1},{17,25},{25,17},{2,10},{10... | collective-permute-start | bytes 589832 | tf_op jit(solution)/shard_map/ppermute | solution.py:605
  17.7 0.5 %ahead.1 = (f32[2,40,512]{2,1,0:T(8,128)S(1)}, f32[2,32,512]{2,1,0:T(8,128)S(1)}) custom-call(f32[9,4,32,512]{3,2,1,0:T(8,128)S(1)} %get-tuple-element.60.refs_3_.refs_0_.refs_1_, f32[9,4,8,512]{3,2,1,0:T(8,128)S(1)} %get-tuple-element.67.refs_5_.refs_8_.refs_7_.refs_1_, f32[2,40,512]{2,1,0:T(8,128)S(1)} %get-tuple-element.69.refs_3_.refs_2_.refs_5_, ...), custom_call_target="tpu_custom_call" | custom-call | flops 1000000 | bytes 125000 | tf_op jit(solution)/shard_map/ahead/pallas_call | solution.py:35
  18.2 0.8 %collective-permute-done.4.refs_5_ = f32[72,512]{1,0:T(8,128)S(1)} collective-permute-done((f32[72,512]{1,0:T(8,128)S(1)}, f32[72,512]{1,0:T(8,128)S(1)}, u32[]{:S(2)}, u32[]{:S(2)}) %collective-permute-start.4) | collective-permute-done | bytes 147488 | tf_op jit(solution)/shard_map/ppermute | solution.py:64
  18.9 0.2 front_2.1
  19.1 1.4 %collective-permute-start.6 = (f32[72,512]{1,0:T(8,128)S(1)}, f32[72,512]{1,0:T(8,128)S(1)}, u32[]{:S(2)}, u32[]{:S(2)}) collective-permute-start(f32[72,512]{1,0:T(8,128)S(1)} %get-tuple-element.91), channel_id=1, source_target_pairs={{0,4},{4,0},{1,5},{5,1},{2,6},{6,2},{3,7},{7,3},{8,12},{12,8},{9,1... | collective-permute-start | bytes 442376 | tf_op jit(solution)/shard_map/ppermute | solution.py:64
  20.6 0.2 bulk_2.1
  20.7 1.6 %collective-permute-start.7 = (f32[2,1,3,32,128]{4,3,2,1,0:T(8,128)S(1)}, f32[2,1,3,32,128]{4,3,2,1,0:T(8,128)S(1)}, u32[]{:S(2)}, u32[]{:S(2)}) collective-permute-start(f32[2,1,3,32,128]{4,3,2,1,0:T(8,128)S(1)} %get-tuple-element.96), channel_id=1, source_target_pairs={{0,8},{8,0},{16,24},{24,16},{1,9},{9,1},{17,25},{25,17},{2,10},{10... | collective-permute-start | bytes 294920 | tf_op jit(solution)/shard_map/ppermute | solution.py:605
  22.4 0.0 collective-permute-done.5.refs_2_
  22.4 2.7 %collective-permute-start.9 = (f32[2,3,32,128]{3,2,1,0:T(8,128)S(1)}, f32[2,3,32,128]{3,2,1,0:T(8,128)S(1)}, u32[]{:S(2)}, u32[]{:S(2)}) collective-permute-start(f32[2,3,32,128]{3,2,1,0:T(8,128)S(1)} %get-tuple-element.90.refs_0_), channel_id=1, source_target_pairs={{0,16},{8,24},{16,0},{24,8},{1,17},{9,25},{17,1},{25,9},{2,18},{10... | collective-permute-start | bytes 294920 | tf_op jit(solution)/shard_map/ppermute | solution.py:605
  25.1 0.0 collective-permute-done.6.refs_5_
  25.1 0.3 front_3.1
  25.4 0.0 collective-permute-done.7.refs_3_
  25.4 4.0 %collective-permute-start.8 = (f32[2,3,32,128]{3,2,1,0:T(8,128)S(1)}, f32[2,3,32,128]{3,2,1,0:T(8,128)S(1)}, u32[]{:S(2)}, u32[]{:S(2)}) collective-permute-start(f32[2,3,32,128]{3,2,1,0:T(8,128)S(1)} %get-tuple-element.97), channel_id=1, source_target_pairs={{0,24},{8,16},{16,8},{24,0},{1,25},{9,17},{17,9},{25,1},{2,26},{10... | collective-permute-start | bytes 294920 | tf_op jit(solution)/shard_map/ppermute | solution.py:605
  29.5 0.0 collective-permute-start.10
  29.5 0.6 %collective-permute-start.11 = (f32[1,3,32,128]{3,2,1,0:T(8,128)S(1)}, f32[1,3,32,128]{3,2,1,0:T(8,128)S(1)}, u32[]{:S(2)}, u32[]{:S(2)}) collective-permute-start(f32[1,3,32,128]{3,2,1,0:T(8,128)S(1)} %get-tuple-element.99), channel_id=1, source_target_pairs={{0,8},{8,0},{16,24},{24,16},{1,9},{9,1},{17,25},{25,17},{2,10},{10... | collective-permute-start | bytes 147464 | tf_op jit(solution)/shard_map/ppermute | solution.py:605
  30.1 0.8 %final_fields.1 = f32[1,2,4,32,512]{4,3,2,1,0:T(8,128)} custom-call(f32[2,32,512]{2,1,0:T(8,128)S(1)} %get-tuple-element.78.refs_0_, f32[2,32,512]{2,1,0:T(8,128)S(1)} %get-tuple-element.79.refs_1_, f32[2,32,512]{2,1,0:T(8,128)S(1)} %get-tuple-element.87.refs_0_.refs_2_, f32[2,32,512]{2,1,0:T(8,128)S(1)} %get-tuple-element.93.refs_3_.refs_0_), custom_call_target="tpu_custom_call" | custom-call | flops 1000000 | bytes 125000 | tf_op jit(solution)/shard_map/final_fields/pallas_call | solution.py:35
  31.0 2.3 %collective-permute-done.9.refs_5_ = f32[2,3,32,128]{3,2,1,0:T(8,128)S(1)} collective-permute-done((f32[2,3,32,128]{3,2,1,0:T(8,128)S(1)}, f32[2,3,32,128]{3,2,1,0:T(8,128)S(1)}, u32[]{:S(2)}, u32[]{:S(2)}) %collective-permute-start.9) | collective-permute-done | bytes 98336 | tf_op jit(solution)/shard_map/ppermute | solution.py:605
  33.3 1.7 %collective-permute-done.10.refs_6_ = f32[1,3,32,128]{3,2,1,0:T(8,128)S(1)} collective-permute-done((f32[1,3,32,128]{3,2,1,0:T(8,128)S(1)}, f32[1,3,32,128]{3,2,1,0:T(8,128)S(1)}, u32[]{:S(2)}, u32[]{:S(2)}) %collective-permute-start.10) | collective-permute-done | bytes 49184 | tf_op jit(solution)/shard_map/ppermute | solution.py:605
  35.0 0.0 collective-permute-done.11.refs_7_
  35.0 0.0 collective-permute-done.8.refs_3_.refs_4_
  35.0 0.7 %combine.1 = (f32[4,32,128]{2,1,0:T(8,128)}, f32[4,32,128]{2,1,0:T(8,128)}, f32[4,32,128]{2,1,0:T(8,128)}) custom-call(f32[4,32,512]{2,1,0:T(8,128)S(1)} %get-tuple-element.55.refs_0_, f32[4,32,512]{2,1,0:T(8,128)S(1)} %get-tuple-element.56.refs_1_, f32[4,32,512]{2,1,0:T(8,128)S(1)} %get-tuple-element.57.refs_2_, ...), custom_call_target="tpu_custom_call" | custom-call | flops 1000000 | bytes 125000 | tf_op jit(solution)/shard_map/combine/pallas_call | solution.py:35
  (4 shorter events, 0.1 us)
Async XLA Ops:
  0.6 7.0 %copy-start.1 = (f32[1,3,1536]{2,0,1:T(1,128)S(1)}, f32[1,3,1536]{2,0,1:T(1,128)}, u32[]{:S(2)}) copy-start(f32[1,3,1536]{2,0,1:T(1,128)} %param.21) | copy-start | bytes 55300
  0.6 8.2 %copy-start = (s32[1,1536]{1,0:T(1,128)S(1)}, s32[1,1536]{1,0:T(1,128)}, u32[]{:S(2)}) copy-start(s32[1,1536]{1,0:T(1,128)} %refs_0_.3) | copy-start | bytes 18436
  2.3 7.0 %collective-permute-start = (f32[80,512]{1,0:T(8,128)S(1)}, f32[80,512]{1,0:T(8,128)S(1)}, u32[]{:S(2)}, u32[]{:S(2)}) collective-permute-start(f32[80,512]{1,0:T(8,128)S(1)} %get-tuple-element.63), channel_id=1, source_target_pairs={{0,8},{1,2},{2,1},{3,11},{8,0},{9,10},{10,9},{11,3},{16,24},{17,18... | collective-permute-start | bytes 491528 | tf_op jit(solution)/shard_map/ppermute | solution.py:75
  5.4 3.9 %collective-permute-start.1 = (f32[80,512]{1,0:T(8,128)S(1)}, f32[80,512]{1,0:T(8,128)S(1)}, u32[]{:S(2)}, u32[]{:S(2)}) collective-permute-start(f32[80,512]{1,0:T(8,128)S(1)} %get-tuple-element.64), channel_id=1, source_target_pairs={{0,1},{1,0},{2,3},{3,2},{8,9},{9,8},{10,11},{11,10},{16,17},{17,16... | collective-permute-start | bytes 491528 | tf_op jit(solution)/shard_map/ppermute | solution.py:75
  5.5 7.8 %collective-permute-start.2 = (f32[2,32,512]{2,1,0:T(8,128)S(1)}, f32[2,32,512]{2,1,0:T(8,128)S(1)}, u32[]{:S(2)}, u32[]{:S(2)}) collective-permute-start(f32[2,32,512]{2,1,0:T(8,128)S(1)} %get-tuple-element.71), channel_id=1, source_target_pairs={{0,4},{4,0},{1,5},{5,1},{2,6},{6,2},{3,7},{7,3},{8,12},{12,8},{9,1... | collective-permute-start | bytes 393224 | tf_op jit(solution)/shard_map/ppermute | solution.py:64
  9.4 4.0 %collective-permute-start.3 = (f32[2,8,512]{2,1,0:T(8,128)S(1)}, f32[2,8,512]{2,1,0:T(8,128)S(1)}, u32[]{:S(2)}, u32[]{:S(2)}) collective-permute-start(f32[2,8,512]{2,1,0:T(8,128)S(1)} %halo_edges.1.refs_2_), channel_id=1, source_target_pairs={{0,4},{4,0},{1,5},{5,1},{2,6},{6,2},{3,7},{7,3},{8,12},{12,8},{9,1... | collective-permute-start | bytes 98312 | tf_op jit(solution)/shard_map/ppermute | solution.py:64
  13.7 5.2 %collective-permute-start.4 = (f32[72,512]{1,0:T(8,128)S(1)}, f32[72,512]{1,0:T(8,128)S(1)}, u32[]{:S(2)}, u32[]{:S(2)}) collective-permute-start(f32[72,512]{1,0:T(8,128)S(1)} %get-tuple-element.83), channel_id=1, source_target_pairs={{0,4},{4,0},{1,5},{5,1},{2,6},{6,2},{3,7},{7,3},{8,12},{12,8},{9,1... | collective-permute-start | bytes 442376 | tf_op jit(solution)/shard_map/ppermute | solution.py:64
  16.0 6.4 %collective-permute-start.5 = (f32[2,2,3,32,128]{4,3,2,1,0:T(8,128)S(1)}, f32[2,2,3,32,128]{4,3,2,1,0:T(8,128)S(1)}, u32[]{:S(2)}, u32[]{:S(2)}) collective-permute-start(f32[2,2,3,32,128]{4,3,2,1,0:T(8,128)S(1)} %get-tuple-element.89), channel_id=1, source_target_pairs={{0,8},{8,0},{16,24},{24,16},{1,9},{9,1},{17,25},{25,17},{2,10},{10... | collective-permute-start | bytes 589832 | tf_op jit(solution)/shard_map/ppermute | solution.py:605
  19.1 5.9 %collective-permute-start.6 = (f32[72,512]{1,0:T(8,128)S(1)}, f32[72,512]{1,0:T(8,128)S(1)}, u32[]{:S(2)}, u32[]{:S(2)}) collective-permute-start(f32[72,512]{1,0:T(8,128)S(1)} %get-tuple-element.91), channel_id=1, source_target_pairs={{0,4},{4,0},{1,5},{5,1},{2,6},{6,2},{3,7},{7,3},{8,12},{12,8},{9,1... | collective-permute-start | bytes 442376 | tf_op jit(solution)/shard_map/ppermute | solution.py:64
  20.7 4.7 %collective-permute-start.7 = (f32[2,1,3,32,128]{4,3,2,1,0:T(8,128)S(1)}, f32[2,1,3,32,128]{4,3,2,1,0:T(8,128)S(1)}, u32[]{:S(2)}, u32[]{:S(2)}) collective-permute-start(f32[2,1,3,32,128]{4,3,2,1,0:T(8,128)S(1)} %get-tuple-element.96), channel_id=1, source_target_pairs={{0,8},{8,0},{16,24},{24,16},{1,9},{9,1},{17,25},{25,17},{2,10},{10... | collective-permute-start | bytes 294920 | tf_op jit(solution)/shard_map/ppermute | solution.py:605
  22.4 10.9 %collective-permute-start.9 = (f32[2,3,32,128]{3,2,1,0:T(8,128)S(1)}, f32[2,3,32,128]{3,2,1,0:T(8,128)S(1)}, u32[]{:S(2)}, u32[]{:S(2)}) collective-permute-start(f32[2,3,32,128]{3,2,1,0:T(8,128)S(1)} %get-tuple-element.90.refs_0_), channel_id=1, source_target_pairs={{0,16},{8,24},{16,0},{24,8},{1,17},{9,25},{17,1},{25,9},{2,18},{10... | collective-permute-start | bytes 294920 | tf_op jit(solution)/shard_map/ppermute | solution.py:605
  25.4 9.6 %collective-permute-start.8 = (f32[2,3,32,128]{3,2,1,0:T(8,128)S(1)}, f32[2,3,32,128]{3,2,1,0:T(8,128)S(1)}, u32[]{:S(2)}, u32[]{:S(2)}) collective-permute-start(f32[2,3,32,128]{3,2,1,0:T(8,128)S(1)} %get-tuple-element.97), channel_id=1, source_target_pairs={{0,24},{8,16},{16,8},{24,0},{1,25},{9,17},{17,9},{25,1},{2,26},{10... | collective-permute-start | bytes 294920 | tf_op jit(solution)/shard_map/ppermute | solution.py:605
  29.5 5.5 %collective-permute-start.10 = (f32[1,3,32,128]{3,2,1,0:T(8,128)S(1)}, f32[1,3,32,128]{3,2,1,0:T(8,128)S(1)}, u32[]{:S(2)}, u32[]{:S(2)}) collective-permute-start(f32[1,3,32,128]{3,2,1,0:T(8,128)S(1)} %get-tuple-element.98), channel_id=1, source_target_pairs={{0,16},{8,24},{16,0},{24,8},{1,17},{9,25},{17,1},{25,9},{2,18},{10... | collective-permute-start | bytes 147464 | tf_op jit(solution)/shard_map/ppermute | solution.py:605
  29.5 5.5 %collective-permute-start.11 = (f32[1,3,32,128]{3,2,1,0:T(8,128)S(1)}, f32[1,3,32,128]{3,2,1,0:T(8,128)S(1)}, u32[]{:S(2)}, u32[]{:S(2)}) collective-permute-start(f32[1,3,32,128]{3,2,1,0:T(8,128)S(1)} %get-tuple-element.99), channel_id=1, source_target_pairs={{0,8},{8,0},{16,24},{24,16},{1,9},{9,1},{17,25},{25,17},{2,10},{10... | collective-permute-start | bytes 147464 | tf_op jit(solution)/shard_map/ppermute | solution.py:605

commit v7 on v6

--- a/solution.py
+++ b/solution.py
@@ -584,8 +584,8 @@
     stage = Stage(tile, state, [], [], name)
     ins, outs = {"w": state["w"], "wh": state["wh"]}, {}
     for t, m in ops:
-        for k in (m - 1, m):
-            ins[("u", t, k)] = state[("u", t, k)]
+        for key in ("now", "uh") if t == 0 else (("u", t, m - 1), ("u", t, m)):
+            ins[key] = state[key]
         rows = tile.ny if t == tile.steps - 1 else tile.rows
         outs[("part", t, m)] = (2, rows, tile.nz)
 
@@ -760,8 +760,9 @@
             for k in range(tile.src - 1, 0, -1):
                 if k not in joined:
                     state[("r", planes, k)] = (xor_swap(tile, state[("s", planes, k)], k), 0)
-        if phase == 1 and not tile.far and tile.steps == 3:
-            run_ahead(tile, state, [(1, tile.nx - 1), (2, tile.nx - 2)], "ahead")
+        ahead = {0: [(0, tile.nx - 1)], 1: [(1, tile.nx - 1), (2, tile.nx - 2)]}.get(phase)
+        if ahead and not tile.far and tile.steps == 3:
+            run_ahead(tile, state, ahead, f"ahead_{phase}")
         for name, k in later:
             group = [planes for planes in pieces if tile.plan[planes][1] == name]
             along = direct[0] if k in joined else None

time: 35.9 us -> 36 us (level)
  starting transfers between devices: 19.5 us -> 18.8 us
  waiting for transfers between devices: 4.96 us -> 5.49 us
    ppermute x6, waiting for transfers between devices: 4.06 us -> 4.49 us  [xor_swap(): return lax.ppermute(block, 'src', [(i, i ^ k) for i in range(tile.src)])]
    pallas_call x16 -> x17, Pallas kernels: 9.85 us -> 10 us  [run_kernel(): pl.pallas_call(kernel, name=name, out_shape=[jax.ShapeDtypeStruct(shape,...]
  transfers between devices with their start and end apart: 12 -> 12, of which waited for: 4 -> 4; matrix products, arithmetic and copies ran while one was open for 0% -> 0% of each run, Pallas kernels for 20% -> 21%
where the time goes in v7:
time: 36 us; the launch traced here: 35.8 us
  starting transfers between devices  18.8 us (52%)
  Pallas kernels  10 us (28%)
  waiting for transfers between devices  5.49 us (15%)
  between operations  1.46 us (4%)
    ppermute x6, starting transfers between devices, xor_swap(): return lax.ppermute(block, 'src', [(i, i ^ k) for i in range(tile.src)])  10.3 us
    pallas_call x17, Pallas kernels, run_kernel(): pl.pallas_call(kernel, name=name, out_shape=[jax.ShapeDtypeStruct(shape,...  10 us
    ppermute x4, starting transfers between devices, swap(): return lax.ppermute(block, axis, pair_swaps(count, first))  5.41 us
    ppermute x6, waiting for transfers between devices, xor_swap(): return lax.ppermute(block, 'src', [(i, i ^ k) for i in range(tile.src)])  4.49 us
    ppermute x2, starting transfers between devices, swap_rows(): return lax.ppermute(block, ('src', 'gy'), joint)  3.12 us
    ppermute x4, waiting for transfers between devices, swap(): return lax.ppermute(block, axis, pair_swaps(count, first))  0.99 us
  transfers between devices with their start and end apart: 12, of which 4 were waited for; matrix products, arithmetic and copies ran while one was open for 0% of the time, Pallas kernels for 21%

profile of v7, /device:TPU:0, one launch (start us, length us, event | category | flops | bytes accessed | tf_op | source)
XLA Modules:
  0.0 35.8 jit_solution(9055029073341535836)
XLA Ops:
  0.6 0.0 copy-start.1
  0.6 0.0 copy-start
  0.7 1.7 %pack_edges.1 = (f32[80,512]{1,0:T(8,128)S(1)}, f32[80,512]{1,0:T(8,128)S(1)}, f32[2,32,512]{2,1,0:T(8,128)S(1)}, f32[1,2,4,32,512]{4,3,2,1,0:T(8,128)S(1)}, f32...) custom-call(f32[1,2,4,32,512]{4,3,2,1,0:T(8,128)} %refs_0_.2, ...), custom_call_target="tpu_custom_call" | custom-call | flops 1000000 | bytes 125000 | tf_op jit(solution)/shard_map/pack_edges/pallas_call | solution.py:35
  2.3 3.1 %collective-permute-start = (f32[80,512]{1,0:T(8,128)S(1)}, f32[80,512]{1,0:T(8,128)S(1)}, u32[]{:S(2)}, u32[]{:S(2)}) collective-permute-start(f32[80,512]{1,0:T(8,128)S(1)} %get-tuple-element.63), channel_id=1, source_target_pairs={{0,8},{1,2},{2,1},{3,11},{8,0},{9,10},{10,9},{11,3},{16,24},{17,18... | collective-permute-start | bytes 491528 | tf_op jit(solution)/shard_map/ppermute | solution.py:75
  5.4 0.0 collective-permute-start.1
  5.5 1.5 %collective-permute-start.2 = (f32[2,32,512]{2,1,0:T(8,128)S(1)}, f32[2,32,512]{2,1,0:T(8,128)S(1)}, u32[]{:S(2)}, u32[]{:S(2)}) collective-permute-start(f32[2,32,512]{2,1,0:T(8,128)S(1)} %get-tuple-element.71), channel_id=1, source_target_pairs={{0,4},{4,0},{1,5},{5,1},{2,6},{6,2},{3,7},{7,3},{8,12},{12,8},{9,1... | collective-permute-start | bytes 393224 | tf_op jit(solution)/shard_map/ppermute | solution.py:64
  7.6 0.0 copy-done.1
  7.7 1.1 %own_state.1 = (f32[9,4,32,512]{3,2,1,0:T(8,128)S(1)}, bf16[3,1,2,4,32,512]{5,4,3,2,1,0:T(8,128)(2,1)S(1)}) custom-call(f32[4,32,512]{2,1,0:T(8,128)S(1)} %get-tuple-element.55.refs_0_, f32[4,32,512]{2,1,0:T(8,128)S(1)} %get-tuple-element.56.refs_1_, f32[4,32,512]{2,1,0:T(8,128)S(1)} %get-tuple-element.57.refs_2_, ...), custom_call_target="tpu_custom_call" | custom-call | flops 3000000 | bytes 375000 | tf_op jit(solution)/shard_map/own_state/pallas_call | solution.py:35
  8.8 0.0 copy-done
  8.8 0.5 %surface_load.1.refs_2_.refs_6_.refs_10_.refs_8_.refs_9_.refs_7_ = f32[3,4,40,128]{3,2,1,0:T(8,128)S(1)} custom-call(s32[1,1536]{1,0:T(1,128)S(1)} %copy-done, s32[1]{0:T(128)S(6)} %copy.16.refs_1_, f32[1,3,1536]{2,1,0:T(4,128)S(1)} %copy.15.refs_2_, f32[9,4,32,512]{3,2,1,0:T(8,128)S(1)} %get-tuple-element.60.refs_3_.refs_0_.refs_1_), custom_call_target="tpu_custom_call" | custom-call | flops 2000000 | bytes 250000 | tf_op jit(solution)/shard_map/surface_load/pallas_call | solution.py:35
  9.3 0.0 collective-permute-done.refs_0_
  9.3 0.0 collective-permute-done.1.refs_1_
  9.4 1.4 %collective-permute-start.3 = (f32[2,8,512]{2,1,0:T(8,128)S(1)}, f32[2,8,512]{2,1,0:T(8,128)S(1)}, u32[]{:S(2)}, u32[]{:S(2)}) collective-permute-start(f32[2,8,512]{2,1,0:T(8,128)S(1)} %halo_edges.1.refs_2_), channel_id=1, source_target_pairs={{0,4},{4,0},{1,5},{5,1},{2,6},{6,2},{3,7},{7,3},{8,12},{12,8},{9,1... | collective-permute-start | bytes 98312 | tf_op jit(solution)/shard_map/ppermute | solution.py:64
  10.8 0.3 halo_state.1
  11.1 0.3 ahead_0.1.refs_3_
  11.4 2.1 %bulk_0.1 = (f32[2,40,512]{2,1,0:T(8,128)S(1)}, f32[4,3,32,128]{3,2,1,0:T(8,128)}, f32[2,40,512]{2,1,0:T(8,128)S(1)}, f32[4,3,32,128]{3,2,1,0:T(8,128)}, f32[2,4...) custom-call(f32[9,4,32,512]{3,2,1,0:T(8,128)S(1)} %get-tuple-element, ...), custom_call_target="tpu_custom_call" | custom-call | flops 10100000 | bytes 1262500 | tf_op jit(solution)/shard_map/bulk_0/pallas_call | solution.py:35
  13.6 0.0 collective-permute-done.2.refs_6_
  13.6 0.0 collective-permute-done.3.refs_7_
  13.6 0.2 front_1.1
  13.8 1.2 %collective-permute-start.4 = (f32[72,512]{1,0:T(8,128)S(1)}, f32[72,512]{1,0:T(8,128)S(1)}, u32[]{:S(2)}, u32[]{:S(2)}) collective-permute-start(f32[72,512]{1,0:T(8,128)S(1)} %get-tuple-element.83), channel_id=1, source_target_pairs={{0,4},{4,0},{1,5},{5,1},{2,6},{6,2},{3,7},{7,3},{8,12},{12,8},{9,1... | collective-permute-start | bytes 442376 | tf_op jit(solution)/shard_map/ppermute | solution.py:64
  15.0 0.9 %bulk_1.1 = (f32[2,40,512]{2,1,0:T(8,128)S(1)}, f32[4,3,32,128]{3,2,1,0:T(8,128)S(1)}, f32[2,32,512]{2,1,0:T(8,128)S(1)}, f32[2,32,512]{2,1,0:T(8,128)S(1)}, f32...) custom-call(f32[9,4,32,512]{3,2,1,0:T(8,128)S(1)} %get-tuple-element.60.refs_3_.refs_0_.refs_1_, ...), custom_call_target="tpu_custom_call" | custom-call | flops 6100000 | bytes 762500 | tf_op jit(solution)/shard_map/bulk_1/pallas_call | solution.py:35
  15.9 1.6 %collective-permute-start.5 = (f32[2,2,3,32,128]{4,3,2,1,0:T(8,128)S(1)}, f32[2,2,3,32,128]{4,3,2,1,0:T(8,128)S(1)}, u32[]{:S(2)}, u32[]{:S(2)}) collective-permute-start(f32[2,2,3,32,128]{4,3,2,1,0:T(8,128)S(1)} %get-tuple-element.89), channel_id=1, source_target_pairs={{0,8},{8,0},{16,24},{24,16},{1,9},{9,1},{17,25},{25,17},{2,10},{10... | collective-permute-start | bytes 589832 | tf_op jit(solution)/shard_map/ppermute | solution.py:605
  17.5 0.5 %ahead_1.1 = (f32[2,40,512]{2,1,0:T(8,128)S(1)}, f32[2,32,512]{2,1,0:T(8,128)S(1)}) custom-call(f32[9,4,32,512]{3,2,1,0:T(8,128)S(1)} %get-tuple-element.60.refs_3_.refs_0_.refs_1_, f32[9,4,8,512]{3,2,1,0:T(8,128)S(1)} %get-tuple-element.67.refs_5_.refs_1_.refs_9_.refs_7_.refs_8_, f32[2,40,512]{2,1,0:T(8,128)S(1)} %get-tuple-element.69.refs_3_.refs_2_.refs_5_, ...), custom_call_target="tpu_custom_call" | custom-call | flops 1000000 | bytes 125000 | tf_op jit(solution)/shard_map/ahead_1/pallas_call | solution.py:35
  18.0 1.0 %collective-permute-done.4.refs_5_ = f32[72,512]{1,0:T(8,128)S(1)} collective-permute-done((f32[72,512]{1,0:T(8,128)S(1)}, f32[72,512]{1,0:T(8,128)S(1)}, u32[]{:S(2)}, u32[]{:S(2)}) %collective-permute-start.4) | collective-permute-done | bytes 147488 | tf_op jit(solution)/shard_map/ppermute | solution.py:64
  19.0 0.2 front_2.1
  19.2 1.3 %collective-permute-start.6 = (f32[72,512]{1,0:T(8,128)S(1)}, f32[72,512]{1,0:T(8,128)S(1)}, u32[]{:S(2)}, u32[]{:S(2)}) collective-permute-start(f32[72,512]{1,0:T(8,128)S(1)} %get-tuple-element.91), channel_id=1, source_target_pairs={{0,4},{4,0},{1,5},{5,1},{2,6},{6,2},{3,7},{7,3},{8,12},{12,8},{9,1... | collective-permute-start | bytes 442376 | tf_op jit(solution)/shard_map/ppermute | solution.py:64
  20.5 0.2 bulk_2.1
  20.7 1.6 %collective-permute-start.7 = (f32[2,1,3,32,128]{4,3,2,1,0:T(8,128)S(1)}, f32[2,1,3,32,128]{4,3,2,1,0:T(8,128)S(1)}, u32[]{:S(2)}, u32[]{:S(2)}) collective-permute-start(f32[2,1,3,32,128]{4,3,2,1,0:T(8,128)S(1)} %get-tuple-element.96), channel_id=1, source_target_pairs={{0,8},{8,0},{16,24},{24,16},{1,9},{9,1},{17,25},{25,17},{2,10},{10... | collective-permute-start | bytes 294920 | tf_op jit(solution)/shard_map/ppermute | solution.py:605
  22.2 0.0 collective-permute-done.5.refs_2_
  22.3 2.7 %collective-permute-start.9 = (f32[2,3,32,128]{3,2,1,0:T(8,128)S(1)}, f32[2,3,32,128]{3,2,1,0:T(8,128)S(1)}, u32[]{:S(2)}, u32[]{:S(2)}) collective-permute-start(f32[2,3,32,128]{3,2,1,0:T(8,128)S(1)} %get-tuple-element.90.refs_0_), channel_id=1, source_target_pairs={{0,16},{8,24},{16,0},{24,8},{1,17},{9,25},{17,1},{25,9},{2,18},{10... | collective-permute-start | bytes 294920 | tf_op jit(solution)/shard_map/ppermute | solution.py:605
  24.9 0.0 collective-permute-done.6.refs_5_
  24.9 0.3 front_3.1
  25.3 0.6 %collective-permute-done.7.refs_3_ = f32[2,1,3,32,128]{4,3,2,1,0:T(8,128)S(1)} collective-permute-done((f32[2,1,3,32,128]{4,3,2,1,0:T(8,128)S(1)}, f32[2,1,3,32,128]{4,3,2,1,0:T(8,128)S(1)}, u32[]{:S(2)}, u32[]{:S(2)}) %collective-permute-start.7) | collective-permute-done | bytes 98336 | tf_op jit(solution)/shard_map/ppermute | solution.py:605
  25.9 3.1 %collective-permute-start.8 = (f32[2,3,32,128]{3,2,1,0:T(8,128)S(1)}, f32[2,3,32,128]{3,2,1,0:T(8,128)S(1)}, u32[]{:S(2)}, u32[]{:S(2)}) collective-permute-start(f32[2,3,32,128]{3,2,1,0:T(8,128)S(1)} %get-tuple-element.97), channel_id=1, source_target_pairs={{0,24},{8,16},{16,8},{24,0},{1,25},{9,17},{17,9},{25,1},{2,26},{10... | collective-permute-start | bytes 294920 | tf_op jit(solution)/shard_map/ppermute | solution.py:605
  29.0 0.1 collective-permute-start.10
  29.1 1.2 %collective-permute-start.11 = (f32[1,3,32,128]{3,2,1,0:T(8,128)S(1)}, f32[1,3,32,128]{3,2,1,0:T(8,128)S(1)}, u32[]{:S(2)}, u32[]{:S(2)}) collective-permute-start(f32[1,3,32,128]{3,2,1,0:T(8,128)S(1)} %get-tuple-element.99), channel_id=1, source_target_pairs={{0,8},{8,0},{16,24},{24,16},{1,9},{9,1},{17,25},{25,17},{2,10},{10... | collective-permute-start | bytes 147464 | tf_op jit(solution)/shard_map/ppermute | solution.py:605
  30.4 0.8 %final_fields.1 = f32[1,2,4,32,512]{4,3,2,1,0:T(8,128)} custom-call(f32[2,32,512]{2,1,0:T(8,128)S(1)} %get-tuple-element.78.refs_0_, f32[2,32,512]{2,1,0:T(8,128)S(1)} %get-tuple-element.79.refs_1_, f32[2,32,512]{2,1,0:T(8,128)S(1)} %get-tuple-element.87.refs_0_.refs_2_, f32[2,32,512]{2,1,0:T(8,128)S(1)} %get-tuple-element.93.refs_3_.refs_0_), custom_call_target="tpu_custom_call" | custom-call | flops 1000000 | bytes 125000 | tf_op jit(solution)/shard_map/final_fields/pallas_call | solution.py:35
  31.2 2.0 %collective-permute-done.9.refs_5_ = f32[2,3,32,128]{3,2,1,0:T(8,128)S(1)} collective-permute-done((f32[2,3,32,128]{3,2,1,0:T(8,128)S(1)}, f32[2,3,32,128]{3,2,1,0:T(8,128)S(1)}, u32[]{:S(2)}, u32[]{:S(2)}) %collective-permute-start.9) | collective-permute-done | bytes 98336 | tf_op jit(solution)/shard_map/ppermute | solution.py:605
  33.2 1.9 %collective-permute-done.10.refs_6_ = f32[1,3,32,128]{3,2,1,0:T(8,128)S(1)} collective-permute-done((f32[1,3,32,128]{3,2,1,0:T(8,128)S(1)}, f32[1,3,32,128]{3,2,1,0:T(8,128)S(1)}, u32[]{:S(2)}, u32[]{:S(2)}) %collective-permute-start.10) | collective-permute-done | bytes 49184 | tf_op jit(solution)/shard_map/ppermute | solution.py:605
  35.1 0.0 collective-permute-done.11.refs_7_
  35.1 0.0 collective-permute-done.8.refs_3_.refs_4_
  35.1 0.7 %combine.1 = (f32[4,32,128]{2,1,0:T(8,128)}, f32[4,32,128]{2,1,0:T(8,128)}, f32[4,32,128]{2,1,0:T(8,128)}) custom-call(f32[4,32,512]{2,1,0:T(8,128)S(1)} %get-tuple-element.55.refs_0_, f32[4,32,512]{2,1,0:T(8,128)S(1)} %get-tuple-element.56.refs_1_, f32[4,32,512]{2,1,0:T(8,128)S(1)} %get-tuple-element.57.refs_2_, ...), custom_call_target="tpu_custom_call" | custom-call | flops 1000000 | bytes 125000 | tf_op jit(solution)/shard_map/combine/pallas_call | solution.py:35
  (4 shorter events, 0.1 us)
Async XLA Ops:
  0.6 7.0 %copy-start.1 = (f32[1,3,1536]{2,0,1:T(1,128)S(1)}, f32[1,3,1536]{2,0,1:T(1,128)}, u32[]{:S(2)}) copy-start(f32[1,3,1536]{2,0,1:T(1,128)} %param.21) | copy-start | bytes 55300
  0.6 8.2 %copy-start = (s32[1,1536]{1,0:T(1,128)S(1)}, s32[1,1536]{1,0:T(1,128)}, u32[]{:S(2)}) copy-start(s32[1,1536]{1,0:T(1,128)} %refs_0_.3) | copy-start | bytes 18436
  2.3 7.0 %collective-permute-start = (f32[80,512]{1,0:T(8,128)S(1)}, f32[80,512]{1,0:T(8,128)S(1)}, u32[]{:S(2)}, u32[]{:S(2)}) collective-permute-start(f32[80,512]{1,0:T(8,128)S(1)} %get-tuple-element.63), channel_id=1, source_target_pairs={{0,8},{1,2},{2,1},{3,11},{8,0},{9,10},{10,9},{11,3},{16,24},{17,18... | collective-permute-start | bytes 491528 | tf_op jit(solution)/shard_map/ppermute | solution.py:75
  5.4 3.9 %collective-permute-start.1 = (f32[80,512]{1,0:T(8,128)S(1)}, f32[80,512]{1,0:T(8,128)S(1)}, u32[]{:S(2)}, u32[]{:S(2)}) collective-permute-start(f32[80,512]{1,0:T(8,128)S(1)} %get-tuple-element.64), channel_id=1, source_target_pairs={{0,1},{1,0},{2,3},{3,2},{8,9},{9,8},{10,11},{11,10},{16,17},{17,16... | collective-permute-start | bytes 491528 | tf_op jit(solution)/shard_map/ppermute | solution.py:75
  5.5 8.1 %collective-permute-start.2 = (f32[2,32,512]{2,1,0:T(8,128)S(1)}, f32[2,32,512]{2,1,0:T(8,128)S(1)}, u32[]{:S(2)}, u32[]{:S(2)}) collective-permute-start(f32[2,32,512]{2,1,0:T(8,128)S(1)} %get-tuple-element.71), channel_id=1, source_target_pairs={{0,4},{4,0},{1,5},{5,1},{2,6},{6,2},{3,7},{7,3},{8,12},{12,8},{9,1... | collective-permute-start | bytes 393224 | tf_op jit(solution)/shard_map/ppermute | solution.py:64
  9.4 4.2 %collective-permute-start.3 = (f32[2,8,512]{2,1,0:T(8,128)S(1)}, f32[2,8,512]{2,1,0:T(8,128)S(1)}, u32[]{:S(2)}, u32[]{:S(2)}) collective-permute-start(f32[2,8,512]{2,1,0:T(8,128)S(1)} %halo_edges.1.refs_2_), channel_id=1, source_target_pairs={{0,4},{4,0},{1,5},{5,1},{2,6},{6,2},{3,7},{7,3},{8,12},{12,8},{9,1... | collective-permute-start | bytes 98312 | tf_op jit(solution)/shard_map/ppermute | solution.py:64
  13.8 5.2 %collective-permute-start.4 = (f32[72,512]{1,0:T(8,128)S(1)}, f32[72,512]{1,0:T(8,128)S(1)}, u32[]{:S(2)}, u32[]{:S(2)}) collective-permute-start(f32[72,512]{1,0:T(8,128)S(1)} %get-tuple-element.83), channel_id=1, source_target_pairs={{0,4},{4,0},{1,5},{5,1},{2,6},{6,2},{3,7},{7,3},{8,12},{12,8},{9,1... | collective-permute-start | bytes 442376 | tf_op jit(solution)/shard_map/ppermute | solution.py:64
  15.9 6.4 %collective-permute-start.5 = (f32[2,2,3,32,128]{4,3,2,1,0:T(8,128)S(1)}, f32[2,2,3,32,128]{4,3,2,1,0:T(8,128)S(1)}, u32[]{:S(2)}, u32[]{:S(2)}) collective-permute-start(f32[2,2,3,32,128]{4,3,2,1,0:T(8,128)S(1)} %get-tuple-element.89), channel_id=1, source_target_pairs={{0,8},{8,0},{16,24},{24,16},{1,9},{9,1},{17,25},{25,17},{2,10},{10... | collective-permute-start | bytes 589832 | tf_op jit(solution)/shard_map/ppermute | solution.py:605
  19.2 5.7 %collective-permute-start.6 = (f32[72,512]{1,0:T(8,128)S(1)}, f32[72,512]{1,0:T(8,128)S(1)}, u32[]{:S(2)}, u32[]{:S(2)}) collective-permute-start(f32[72,512]{1,0:T(8,128)S(1)} %get-tuple-element.91), channel_id=1, source_target_pairs={{0,4},{4,0},{1,5},{5,1},{2,6},{6,2},{3,7},{7,3},{8,12},{12,8},{9,1... | collective-permute-start | bytes 442376 | tf_op jit(solution)/shard_map/ppermute | solution.py:64
  20.7 5.2 %collective-permute-start.7 = (f32[2,1,3,32,128]{4,3,2,1,0:T(8,128)S(1)}, f32[2,1,3,32,128]{4,3,2,1,0:T(8,128)S(1)}, u32[]{:S(2)}, u32[]{:S(2)}) collective-permute-start(f32[2,1,3,32,128]{4,3,2,1,0:T(8,128)S(1)} %get-tuple-element.96), channel_id=1, source_target_pairs={{0,8},{8,0},{16,24},{24,16},{1,9},{9,1},{17,25},{25,17},{2,10},{10... | collective-permute-start | bytes 294920 | tf_op jit(solution)/shard_map/ppermute | solution.py:605
  22.3 10.9 %collective-permute-start.9 = (f32[2,3,32,128]{3,2,1,0:T(8,128)S(1)}, f32[2,3,32,128]{3,2,1,0:T(8,128)S(1)}, u32[]{:S(2)}, u32[]{:S(2)}) collective-permute-start(f32[2,3,32,128]{3,2,1,0:T(8,128)S(1)} %get-tuple-element.90.refs_0_), channel_id=1, source_target_pairs={{0,16},{8,24},{16,0},{24,8},{1,17},{9,25},{17,1},{25,9},{2,18},{10... | collective-permute-start | bytes 294920 | tf_op jit(solution)/shard_map/ppermute | solution.py:605
  25.9 9.2 %collective-permute-start.8 = (f32[2,3,32,128]{3,2,1,0:T(8,128)S(1)}, f32[2,3,32,128]{3,2,1,0:T(8,128)S(1)}, u32[]{:S(2)}, u32[]{:S(2)}) collective-permute-start(f32[2,3,32,128]{3,2,1,0:T(8,128)S(1)} %get-tuple-element.97), channel_id=1, source_target_pairs={{0,24},{8,16},{16,8},{24,0},{1,25},{9,17},{17,9},{25,1},{2,26},{10... | collective-permute-start | bytes 294920 | tf_op jit(solution)/shard_map/ppermute | solution.py:605
  29.0 6.1 %collective-permute-start.10 = (f32[1,3,32,128]{3,2,1,0:T(8,128)S(1)}, f32[1,3,32,128]{3,2,1,0:T(8,128)S(1)}, u32[]{:S(2)}, u32[]{:S(2)}) collective-permute-start(f32[1,3,32,128]{3,2,1,0:T(8,128)S(1)} %get-tuple-element.98), channel_id=1, source_target_pairs={{0,16},{8,24},{16,0},{24,8},{1,17},{9,25},{17,1},{25,9},{2,18},{10... | collective-permute-start | bytes 147464 | tf_op jit(solution)/shard_map/ppermute | solution.py:605
  29.1 5.9 %collective-permute-start.11 = (f32[1,3,32,128]{3,2,1,0:T(8,128)S(1)}, f32[1,3,32,128]{3,2,1,0:T(8,128)S(1)}, u32[]{:S(2)}, u32[]{:S(2)}) collective-permute-start(f32[1,3,32,128]{3,2,1,0:T(8,128)S(1)} %get-tuple-element.99), channel_id=1, source_target_pairs={{0,8},{8,0},{16,24},{24,16},{1,9},{9,1},{17,25},{25,17},{2,10},{10... | collective-permute-start | bytes 147464 | tf_op jit(solution)/shard_map/ppermute | solution.py:605
